TPU v7x, 256 devices: a whole 4x4x8 slice. The times are simulated.
256 devices in a mesh: cell: 64 (over z, x, y_lo), lev: 4 (over y_hi, core).
Axes of the slice: x: 4, y: 4 (y_hi: 2, y_lo: 2; y = y_hi * 2 + y_lo), z: 8, core: 2. Of those that a mesh axis runs over, the one named last changes fastest.
Arguments:
- populations: float32 [4096, 8192], P('cell', 'lev'), may hold values from 0.5 to 1.5
- rate_blocks: bfloat16 [2, 64, 6, 128, 128], P(None, 'lev'), may hold values from -0.21875 to 0.21875
- pattern: int32 [64, 6], P('lev'), may hold values from 0 to 63, as said below
- bracket: int32 [4096], P('cell'), may hold values from 0 to 1
- cross_section: float32 [8192], P('lev'), as said below
- emission: float32 [8192], P('lev'), may hold values from 0.1 to 1
- absorber: float32 [4096], P('cell'), as said below
- stream_speed: float32 [4096], P('cell'), may hold values from 0.25 to 1
- cross_speed: float32 [4096], P('cell'), may hold values from -1 to 1
- inflow: float32 [16, 8192], P(None, 'lev'), may hold values from 0.5 to 1.5
Outputs:
- updated: float32 [4096, 8192], P('cell', 'lev')
- absorption: float32 [4096, 8192], P('cell', 'lev')
Inputs may be any that keep to these rules, and one draw needn't show every extreme that they name: Row r of pattern lists 6 distinct level blocks, the first of them r itself. `cross_section`: each cross section lies between 0.1 / 256 and 0.035. `absorber`: absorber columns lie between 0.5 and 2, except a few whole streamwise rows where they equal 384.
All inputs are finite; a program needn't handle non-finite values.
Results may differ from a plain program's by a relative error of at most 0.00055.
Values may be sent and summed in bfloat16 or wider, within the bound.
No kernel may reach another device: no remote copies, remote signals or barrier semaphores. Data moves between devices by JAX's collectives and lax.ppermute only.
A program may use at most 128 MiB of HBM per device.

v0:
```python
import jax
import jax.numpy as jnp
from jax import lax
from jax.sharding import PartitionSpec as P

NY = 16


time_step = 0.25


def prefix(value, axis, combine, identity, reverse):
    peers, place = (lax.axis_size(axis), lax.axis_index(axis))
    everything = jax.tree.map(lambda part: lax.all_gather(part, axis), value)
    start = jax.tree.map(
        lambda part, zero: jnp.broadcast_to(jnp.asarray(zero, part.dtype), part.shape),
        value,
        identity,
    )

    def turn(k, before):
        at = peers - 1 - k if reverse else k
        reached = at > place if reverse else at < place
        new = combine(before, jax.tree.map(lambda part: part[at], everything))
        return jax.tree.map(lambda a, b: jnp.where(reached, a, b), new, before)

    return lax.fori_loop(0, peers, turn, start)


def shortened(value):

    def short(part):
        return part.astype(jnp.bfloat16) if part.dtype == jnp.float32 else part

    return jax.tree.map(short, value)


def shifted(value, axis, by):
    peers = lax.axis_size(axis)
    pairs = [(i, i + by) for i in range(peers) if 0 <= i + by < peers]
    return lax.ppermute(value, axis, pairs)


def affine(earlier, later):
    return (earlier[0] * later[0], later[0] * earlier[1] + later[1])


def rate_term(populations, rate_blocks, pattern, bracket):
    lowered = populations.astype(jnp.bfloat16)
    gathered = lax.all_gather(lowered, "lev", axis=1, tiled=True)
    cell_count = gathered.shape[0]
    block_size = rate_blocks.shape[3]
    picked = gathered.reshape(cell_count, -1, block_size)[:, pattern, :]
    summed = jnp.zeros((cell_count, rate_blocks.shape[1], block_size), jnp.float32)
    for bracket_id in range(rate_blocks.shape[0]):
        product = jnp.einsum(
            "crkj,rkij->cri", picked, rate_blocks[bracket_id], preferred_element_type=jnp.float32
        )
        summed = jnp.where((bracket == bracket_id)[:, None, None], product, summed)
    return summed.reshape(cell_count, -1)


def radiation(populations, emission, cross_section, absorber):
    cell_count, level_count = populations.shape
    strips = cell_count // NY
    emitted = populations * emission[None, :]
    transmit = jnp.exp(-(absorber[:, None] * cross_section[None, :]))
    layered_pass = transmit.reshape(strips, NY, level_count)
    layered_emit = emitted.reshape(strips, NY, level_count)
    passed_down, local_down = lax.associative_scan(affine, (layered_pass, layered_emit), axis=0)
    passed_up, local_up = lax.associative_scan(
        affine, (layered_pass, layered_emit), reverse=True, axis=0
    )
    zero_field = jnp.zeros((NY, level_count), jnp.float32)
    ones_field = jnp.ones((NY, level_count), jnp.float32)
    enter_down = prefix(
        (passed_down[-1], local_down[-1]), "cell", affine, (ones_field, zero_field), False
    )[1]
    enter_up = prefix((passed_up[0], local_up[0]), "cell", affine, (ones_field, zero_field), True)[
        1
    ]
    downward = local_down + passed_down * enter_down[None]
    upward = local_up + passed_up * enter_up[None]
    absorbed = (1.0 - layered_pass) * (downward + upward - 2.0 * layered_emit)
    return (emitted, absorbed.reshape(cell_count, level_count))


def advection(populations, inflow, stream_speed, cross_speed):
    cell_count, level_count = populations.shape
    layered = populations.reshape(cell_count // NY, NY, level_count)
    arrived = shifted(shortened(layered[-1]), "cell", 1)
    boundary = jnp.where(lax.axis_index("cell") == 0, inflow, arrived)
    upstream = jnp.concatenate([boundary[None], layered[:-1]], axis=0)
    before_y = jnp.roll(layered, 1, axis=1)
    after_y = jnp.roll(layered, -1, axis=1)
    along_x = stream_speed.reshape(-1, NY, 1)
    along_y = cross_speed.reshape(-1, NY, 1)
    flux_sum = (
        -along_x * (layered - upstream)
        - jnp.maximum(along_y, 0.0) * (layered - before_y)
        - jnp.minimum(along_y, 0.0) * (after_y - layered)
    )
    return flux_sum.reshape(cell_count, level_count)


def tendency(
    populations,
    rate_blocks,
    pattern,
    bracket,
    cross_section,
    emission,
    absorber,
    stream_speed,
    cross_speed,
    inflow,
):
    rates_part = rate_term(populations, rate_blocks, pattern, bracket)
    emitted, absorbed = radiation(populations, emission, cross_section, absorber)
    carried = advection(populations, inflow, stream_speed, cross_speed)
    return (rates_part - emitted + absorbed + carried, absorbed)


def local(
    populations,
    rate_blocks,
    pattern,
    bracket,
    cross_section,
    emission,
    absorber,
    stream_speed,
    cross_speed,
    inflow,
):
    first_rate, _ = tendency(
        populations,
        rate_blocks,
        pattern,
        bracket,
        cross_section,
        emission,
        absorber,
        stream_speed,
        cross_speed,
        inflow,
    )
    middle = populations + time_step * first_rate
    second, absorption = tendency(
        middle,
        rate_blocks,
        pattern,
        bracket,
        cross_section,
        emission,
        absorber,
        stream_speed,
        cross_speed,
        inflow,
    )
    updated = 0.5 * (populations + middle + time_step * second)
    return (updated, absorption)


def solution(mesh):
    in_specs = (
        P("cell", "lev"),
        P(None, "lev", None, None, None),
        P("lev", None),
        P("cell"),
        P("lev"),
        P("lev"),
        P("cell"),
        P("cell"),
        P("cell"),
        P(None, "lev"),
    )
    out_specs = (P("cell", "lev"), P("cell", "lev"))
    return jax.shard_map(local, mesh=mesh, in_specs=in_specs, out_specs=out_specs, check_vma=False)
```

profile of v0, /device:TPU:2, one launch (start us, length us, event | category | flops | bytes accessed | tf_op | source)
XLA Modules:
  0.0 2094.0 jit_solution(13246688002968772590)
XLA Ops:
  7.2 2.2 broadcast_multiply_fusion.1
  27.6 3.5 collective-permute-start
  31.1 2.4 pad.101
  33.5 2.4 pad.100
  50.7 1.9 gather_fusion
  52.6 3.7 fusion.16
  56.4 3.9 fusion.43
  60.3 290.7 %all-gather.13.cloned.1.call-done = f32[64,16,2048]{2,1,0:T(8,128)} async-done(((f32[1,16,2048]{2,1,0:T(8,128)}), f32[64,16,2048]{2,1,0:T(8,128)}) %all-gather.13.cloned.1.call-update) | async-done | bytes 8388624 | tf_op jit(solution)/shard_map/all_gather | solution.py:14
  351.0 313.5 %all-gather.11.cloned.1.call-done = f32[64,16,2048]{2,1,0:T(8,128)} async-done(((f32[1,16,2048]{2,1,0:T(8,128)}), f32[64,16,2048]{2,1,0:T(8,128)}) %all-gather.11.cloned.1.call-update) | async-done | bytes 8388624 | tf_op jit(solution)/shard_map/all_gather | solution.py:14
  664.5 69.9 %while.60 = (s32[]{:T(128)}, f32[16,2048]{1,0:T(8,128)S(1)}, s32[]{:T(128)}, f32[64,16,2048]{2,1,0:T(8,128)}, f32[64,16,2048]{2,1,0:T(8,128)}, /*index=5*/s32[]{:T(128)}, s32[]{:T(128)}) while((s32[]{:T(128)}, f32[16,2048]{1,0:T(8,128)S(1)}, s32[]{:T(128)}, f32[64,16,2048]{2,1,0:T(8,128)}, f32[64,16,2048]{2,1,0:T(8,128)}, ...), condition=%wide.region_1.2_spmd.clone, body=%wide.region_0.1_spmd.clone.sunk | while | flops 131076 | bytes 524389 | solution.py:27
  734.4 241.6 %all-gather.17.cloned.1.call-done = f32[64,16,2048]{2,1,0:T(8,128)} async-done(((f32[1,16,2048]{2,1,0:T(8,128)}), f32[64,16,2048]{2,1,0:T(8,128)}) %all-gather.17.cloned.1.call-update) | async-done | bytes 8388624 | tf_op jit(solution)/shard_map/all_gather | solution.py:14
  976.0 311.4 %all-gather.15.cloned.1.call-done = f32[64,16,2048]{2,1,0:T(8,128)} async-done(((f32[1,16,2048]{2,1,0:T(8,128)}), f32[64,16,2048]{2,1,0:T(8,128)}) %all-gather.15.cloned.1.call-update) | async-done | bytes 8388624 | tf_op jit(solution)/shard_map/all_gather | solution.py:14
  1287.4 70.3 %while.61 = (s32[]{:T(128)}, f32[16,2048]{1,0:T(8,128)S(1)}, s32[]{:T(128)}, f32[64,16,2048]{2,1,0:T(8,128)}, f32[64,16,2048]{2,1,0:T(8,128)}, /*index=5*/s32[]{:T(128)}, s32[]{:T(128)}, s32[]{:T(128)}, s32[]{:T(128)}) while((s32[]{:T(128)}, f32[16,2048]{1,0:T(8,128)S(1)}, s32[]{:T(128)}, f32[64,16,2048]{2,1,0:T(8,128)}, ...), condition=%wide.region_3.4_spmd.clone, body=%wide.region_2.3_spmd.clone.sunk | while | flops 131080 | bytes 524451 | solution.py:27
  1357.9 2.5 subtract_multiply_fusion.1
  1376.7 1.9 collective-permute-start.1
  1382.1 1.9 pad_maximum_fusion.5
  1384.0 2.1 add.339
  1389.4 1.9 gather_fusion.1
  1391.3 3.7 fusion.19
  1395.0 3.9 fusion.34
  1398.9 303.2 %all-gather.21.cloned.1.call-done = f32[64,16,2048]{2,1,0:T(8,128)} async-done(((f32[1,16,2048]{2,1,0:T(8,128)}), f32[64,16,2048]{2,1,0:T(8,128)}) %all-gather.21.cloned.1.call-update) | async-done | bytes 8388624 | tf_op jit(solution)/shard_map/all_gather | solution.py:14
  1702.1 70.0 %while.62 = (s32[]{:T(128)}, f32[16,2048]{1,0:T(8,128)S(1)}, s32[]{:T(128)}, f32[64,16,2048]{2,1,0:T(8,128)}, f32[64,16,2048]{2,1,0:T(8,128)}, /*index=5*/s32[]{:T(128)}, s32[]{:T(128)}) while((s32[]{:T(128)}, f32[16,2048]{1,0:T(8,128)S(1)}, s32[]{:T(128)}, f32[64,16,2048]{2,1,0:T(8,128)}, f32[64,16,2048]{2,1,0:T(8,128)}, ...), condition=%wide.region_5.6_spmd.clone, body=%wide.region_4.5_spmd.clone.sunk | while | flops 131076 | bytes 524389 | solution.py:27
  1772.1 241.8 %all-gather.23.cloned.1.call-done = f32[64,16,2048]{2,1,0:T(8,128)} async-done(((f32[1,16,2048]{2,1,0:T(8,128)}), f32[64,16,2048]{2,1,0:T(8,128)}) %all-gather.23.cloned.1.call-update) | async-done | bytes 8388624 | tf_op jit(solution)/shard_map/all_gather | solution.py:14
  2013.8 70.3 %while.63 = (s32[]{:T(128)}, f32[16,2048]{1,0:T(8,128)S(1)}, s32[]{:T(128)}, f32[64,16,2048]{2,1,0:T(8,128)}, f32[64,16,2048]{2,1,0:T(8,128)}, /*index=5*/s32[]{:T(128)}, s32[]{:T(128)}, s32[]{:T(128)}, s32[]{:T(128)}) while((s32[]{:T(128)}, f32[16,2048]{1,0:T(8,128)S(1)}, s32[]{:T(128)}, f32[64,16,2048]{2,1,0:T(8,128)}, ...), condition=%wide.region_7.8_spmd.clone, body=%wide.region_6.7_spmd.clone.sunk | while | flops 131080 | bytes 524451 | solution.py:27
  (470 shorter events, 332.8 us)
Async XLA Ops:
  7.2 42.0 %all-gather.9.cloned.1.call-start = ((), (), s32[]{:S(2)}) async-start(), calls=%async_computation | async-start | bytes 1310720 | tf_op jit(solution)/shard_map/all_gather | solution.py:50
  9.4 341.6 %all-gather.13.cloned.1.call-start = ((), (), s32[]{:S(2)}) async-start(), calls=%async_computation.2 | async-start | bytes 8519680 | tf_op jit(solution)/shard_map/all_gather | solution.py:14
  15.5 649.0 %all-gather.11.cloned.1.call-start = ((), (), s32[]{:S(2)}) async-start(), calls=%async_computation.1 | async-start | bytes 8519680 | tf_op jit(solution)/shard_map/all_gather | solution.py:14
  17.5 18.5 copy-start.9
  18.2 957.8 %all-gather.17.cloned.1.call-start = ((), (), s32[]{:S(2)}) async-start(), calls=%async_computation.4 | async-start | bytes 8519680 | tf_op jit(solution)/shard_map/all_gather | solution.py:14
  24.2 15.6 copy-start
  26.0 1261.4 %all-gather.15.cloned.1.call-start = ((), (), s32[]{:S(2)}) async-start(), calls=%async_computation.3 | async-start | bytes 8519680 | tf_op jit(solution)/shard_map/all_gather | solution.py:14
  26.0 12.9 copy-start.14
  27.6 18.8 collective-permute-start
  37.6 1350.3 %all-gather.19.cloned.1.call-start = ((), (), s32[]{:S(2)}) async-start(), calls=%async_computation.5 | async-start | bytes 1310720 | tf_op jit(solution)/shard_map/all_gather | solution.py:50
  42.1 14.3 copy-start.55
  60.3 1297.5 %copy-start.6 = (f32[4,16,2048]{2,1,0:T(8,128)S(1)}, f32[4,16,2048]{2,1,0:T(8,128)}, u32[]{:S(2)}) copy-start(f32[4,16,2048]{2,1,0:T(8,128)} %copy-done.5) | copy-start | bytes 1572868
  60.3 1297.5 %copy-start.8 = (f32[4,16,2048]{2,1,0:T(8,128)S(1)}, f32[4,16,2048]{2,1,0:T(8,128)}, u32[]{:S(2)}) copy-start(f32[4,16,2048]{2,1,0:T(8,128)} %copy-done.7) | copy-start | bytes 1572868
  60.3 1297.5 %copy-start.40 = (f32[2048]{0:T(1024)S(1)}, f32[2048]{0:T(1024)}, u32[]{:S(2)}) copy-start(f32[2048]{0:T(1024)} %param.22) | copy-start | bytes 24580
  60.3 1297.6 %copy-start.45 = (f32[4,16]{1,0:T(4,128)S(1)}, f32[4,16]{1,0:T(4,128)}, u32[]{:S(2)}) copy-start(f32[4,16]{1,0:T(4,128)} %copy-done.44) | copy-start | bytes 772
  1367.3 334.8 %all-gather.21.cloned.1.call-start = ((), (), s32[]{:S(2)}) async-start(), calls=%async_computation.6 | async-start | bytes 8519680 | tf_op jit(solution)/shard_map/all_gather | solution.py:14
  1371.2 642.6 %all-gather.23.cloned.1.call-start = ((), (), s32[]{:S(2)}) async-start(), calls=%async_computation.7 | async-start | bytes 8519680 | tf_op jit(solution)/shard_map/all_gather | solution.py:14
  1376.7 9.4 collective-permute-start.1
  1398.9 685.3 %copy-start.11 = (f32[4,16,2048]{2,1,0:T(8,128)S(1)}, f32[4,16,2048]{2,1,0:T(8,128)}, u32[]{:S(2)}) copy-start(f32[4,16,2048]{2,1,0:T(8,128)} %copy-done.10) | copy-start | bytes 1572868
  1398.9 685.3 %copy-start.13 = (f32[4,16,2048]{2,1,0:T(8,128)S(1)}, f32[4,16,2048]{2,1,0:T(8,128)}, u32[]{:S(2)}) copy-start(f32[4,16,2048]{2,1,0:T(8,128)} %copy-done.12) | copy-start | bytes 1572868
  1398.9 685.3 %copy-start.46 = (f32[4,16]{1,0:T(4,128)S(1)}, f32[4,16]{1,0:T(4,128)}, u32[]{:S(2)}) copy-start(f32[4,16]{1,0:T(4,128)} %copy-done.44) | copy-start | bytes 772
  2013.8 72.1 %copy-start.49 = (f32[64]{0:T(128)S(1)}, f32[64]{0:T(128)}, u32[]{:S(2)}) copy-start(f32[64]{0:T(128)} %get-tuple-element.621) | copy-start | bytes 772
  2013.8 72.1 %copy-start.51 = (f32[64]{0:T(128)S(1)}, f32[64]{0:T(128)}, u32[]{:S(2)}) copy-start(f32[64]{0:T(128)} %get-tuple-element.622) | copy-start | bytes 772
  2013.8 72.1 %copy-start.53 = (f32[64]{0:T(128)S(1)}, f32[64]{0:T(128)}, u32[]{:S(2)}) copy-start(f32[64]{0:T(128)} %neg.18) | copy-start | bytes 772
  (45 other events, 174.7 us)
Sparse Core Ops, SparseCore 0:
  9.8 26.3 all-gather.8
  38.0 312.9 all-gather.12
  352.8 311.6 all-gather.10
  666.1 309.8 all-gather.16
  977.6 309.7 all-gather.14
  1367.4 20.3 all-gather.18
  1389.6 312.3 all-gather.20
  1703.9 309.9 all-gather.22
where the time goes:
time: 2100 us; the launch traced here: 2090 us
  waiting for transfers between devices  1700 us (81%)
  other arithmetic  319 us (15%)
  local copies, waits for them, and re-layouts  29.6 us (1%)
    all_gather x6, waiting for transfers between devices, prefix(): everything = jax.tree.map(lambda part: lax.all_gather(part, axis), value)  1700 us
    select_n x256, other arithmetic, turn(): return jax.tree.map(lambda a, b: jnp.where(reached, a, b), new, before)  274 us
  transfers between devices with their start and end apart: 10, of which 7 were waited for; matrix products, arithmetic and copies ran while one was open for 10% of the time, Pallas kernels for 0%

commit v1 on v0

v1 whole, which is shorter than its diff:
```python
import functools

import jax
import jax.numpy as jnp
from jax import lax
from jax.experimental import pallas as pl
from jax.experimental.pallas import tpu as pltpu
from jax.sharding import PartitionSpec as P

NY = 16
LANES = 128
ROWS = 8
time_step = 0.25


def column(row):
    n = row.shape[1]
    at_row = lax.broadcasted_iota(jnp.int32, (n, n), 0)
    at_column = lax.broadcasted_iota(jnp.int32, (n, n), 1)
    return jnp.sum(jnp.where(at_row == at_column, row, jnp.zeros_like(row)), axis=1, keepdims=True)


def layers(value):
    return [value[k : k + NY] for k in range(0, value.shape[0], NY)]


def exits(passed, emitted):
    down, up = emitted[0], emitted[-1]
    for t, e in zip(passed[1:], emitted[1:]):
        down = t * down + e
    for t, e in zip(passed[-2::-1], emitted[-2::-1]):
        up = t * up + e
    return down, up


def put_exits(exit_ref, group, groups, down, up):
    for way, value in enumerate((down, up)):
        for half in range(NY // ROWS):
            at = (way * (NY // ROWS) + half) * groups + group
            exit_ref[at] = value[half * ROWS : (half + 1) * ROWS]


def get_enters(enter_ref, group, groups):
    found = []
    for way in range(2):
        halves = [enter_ref[(way * (NY // ROWS) + half) * groups + group] for half in range(NY // ROWS)]
        found.append(jnp.concatenate(halves, axis=0))
    return found


def absorbed_of(passed, emitted, enter_down, enter_up):
    count = len(passed)
    downward, upward = [None] * count, [None] * count
    running = enter_down
    for k in range(count):
        running = passed[k] * running + emitted[k]
        downward[k] = running
    running = enter_up
    for k in reversed(range(count)):
        running = passed[k] * running + emitted[k]
        upward[k] = running
    return [
        (1.0 - t) * (d + u - 2.0 * e) for t, d, u, e in zip(passed, downward, upward, emitted)
    ]


def advection(layered, boundary, along_x, forward_y, backward_y):
    result, upstream = [], boundary
    for k, here in enumerate(layered):
        before = pltpu.roll(here, 1, 0)
        after = pltpu.roll(here, NY - 1, 0)
        result.append(
            -along_x[k] * (here - upstream) - forward_y[k] * (here - before) - backward_y[k] * (after - here)
        )
        upstream = here
    return result


def first_kernel(p_ref, cross_ref, emission_ref, absorber_ref, q_ref, last_ref, exit_ref):
    absorber = column(absorber_ref[...])
    groups = p_ref.shape[1] // LANES
    for g in range(groups):
        at = slice(g * LANES, (g + 1) * LANES)
        p = p_ref[:, at]
        q = p.astype(jnp.bfloat16)
        q_ref[:, at] = q
        last_ref[:, at] = q[-NY:]
        passed = layers(jnp.exp(-(absorber * cross_ref[:, at])))
        emitted = layers(p * emission_ref[:, at])
        put_exits(exit_ref, g, groups, *exits(passed, emitted))


def scan(exit_ref, pass_ref, enter_ref, way):
    count = exit_ref.shape[0]

    def step(i, carry):
        at = jnp.where(way == 0, i, count - 1 - i)
        enter_ref[at] = carry
        return pass_ref[at] * carry + exit_ref[at]

    lax.fori_loop(0, count, step, jnp.zeros(exit_ref.shape[1:], jnp.float32), unroll=8)


def strips_pass(absorbers_ref, cross_ref, pass_ref, half, group):
    strips, cells = absorbers_ref.shape
    y = lax.broadcasted_iota(jnp.int32, (ROWS, cells), 0) + half * ROWS
    mine = lax.rem(lax.broadcasted_iota(jnp.int32, (ROWS, cells), 1), NY) == y
    cross = cross_ref[pl.ds(group, 1), :]
    for s in range(strips):
        depth = jnp.sum(jnp.where(mine, absorbers_ref[s : s + 1, :], 0.0), axis=1, keepdims=True)
        pass_ref[s] = jnp.exp(-(depth * cross))


def scan_kernel(axis, make_pass, exit_ref, *refs):
    groups = 16
    me = lax.axis_index(axis)
    group = lax.rem(me, groups)
    half = lax.rem(me // groups, NY // ROWS)
    way = me // (groups * (NY // ROWS))
    if make_pass:
        absorbers_ref, cross_ref, enter_ref, pass_ref = refs
        strips_pass(absorbers_ref, cross_ref, pass_ref, half, group)
    else:
        pass_ref, enter_ref = refs
    scan(exit_ref, pass_ref, enter_ref, way)


def rate_kernel(pattern_ref, q_ref, table_ref, bracket_ref, out_ref):
    r = pl.program_id(0)
    count = table_ref.shape[2]
    picked = jnp.concatenate(
        [
            q_ref[:, pl.ds(pl.multiple_of(pattern_ref[r, k] * LANES, LANES), LANES)]
            for k in range(count)
        ],
        axis=1,
    )
    both = jnp.concatenate(
        [
            jnp.concatenate([table_ref[b, 0, k] for k in range(count)], axis=1)
            for b in range(table_ref.shape[0])
        ],
        axis=0,
    )
    product = lax.dot_general(
        picked, both, (((1,), (1,)), ((), ())), preferred_element_type=jnp.float32
    )
    bracket = column(bracket_ref[...])
    out_ref[...] = jnp.where(bracket == 0, product[:, :LANES], product[:, LANES:])


def step_kernel(
    final, axis, *refs
):
    (p_ref, rate_ref, enter_ref, arrived_ref, inflow_ref, cross_ref, emission_ref,
     absorber_ref, stream_ref, crossways_ref) = refs[:10]
    absorber = column(absorber_ref[...])
    along_x = layers(column(stream_ref[...]))
    along_y = column(crossways_ref[...])
    forward_y = layers(jnp.maximum(along_y, 0.0))
    backward_y = layers(jnp.minimum(along_y, 0.0))
    inlet = lax.axis_index(axis) == 0
    groups = p_ref.shape[1] // LANES
    for g in range(groups):
        at = slice(g * LANES, (g + 1) * LANES)
        p = layers(p_ref[:, at])
        emission = emission_ref[:, at]
        emitted = [value * emission for value in p]
        passed = layers(jnp.exp(-(absorber * cross_ref[:, at])))
        absorbed = absorbed_of(passed, emitted, *get_enters(enter_ref, g, groups))
        boundary = jnp.where(inlet, inflow_ref[:, at], arrived_ref[:, at].astype(jnp.float32))
        carried = advection(p, boundary, along_x, forward_y, backward_y)
        rates = layers(rate_ref[:, at])
        tendency = [q - e + a + v for q, e, a, v in zip(rates, emitted, absorbed, carried)]
        if final:
            start_ref, updated_ref, absorption_ref = refs[10:]
            start = layers(start_ref[:, at])
            for k, rate in enumerate(tendency):
                here = slice(k * NY, (k + 1) * NY)
                updated_ref[here, at] = 0.5 * (start[k] + p[k] + time_step * rate)
                absorption_ref[here, at] = absorbed[k]
        else:
            middle_ref, q_ref, last_ref, exit_ref = refs[10:]
            middle = [value + time_step * rate for value, rate in zip(p, tendency)]
            for k, value in enumerate(middle):
                here = slice(k * NY, (k + 1) * NY)
                middle_ref[here, at] = value
                q_ref[here, at] = value.astype(jnp.bfloat16)
            last_ref[:, at] = middle[-1].astype(jnp.bfloat16)
            put_exits(exit_ref, g, groups, *exits(passed, [value * emission for value in middle]))


def vmem(count):
    return [pl.BlockSpec(memory_space=pltpu.VMEM)] * count


LIMIT = pltpu.CompilerParams(vmem_limit_bytes=48 * 2**20)


def call(body, args, outs, cost):
    return pl.pallas_call(
        body,
        out_shape=outs,
        in_specs=vmem(len(args)),
        out_specs=vmem(len(outs)),
        compiler_params=LIMIT,
        cost_estimate=pl.CostEstimate(flops=cost, bytes_accessed=cost, transcendentals=0),
    )(*args)


def rate_term(q, rate_blocks, pattern, bracket):
    cells = q.shape[0]
    brackets, rows, count, block, _ = rate_blocks.shape
    return pl.pallas_call(
        rate_kernel,
        grid_spec=pltpu.PrefetchScalarGridSpec(
            num_scalar_prefetch=1,
            grid=(rows,),
            in_specs=[
                pl.BlockSpec(q.shape, lambda r, pattern: (0, 0)),
                pl.BlockSpec((brackets, 1, count, block, block), lambda r, pattern: (0, r, 0, 0, 0)),
                pl.BlockSpec(bracket.shape, lambda r, pattern: (0, 0)),
            ],
            out_specs=pl.BlockSpec((cells, block), lambda r, pattern: (0, r)),
        ),
        out_shape=jax.ShapeDtypeStruct((cells, rows * block), jnp.float32),
        compiler_params=LIMIT,
        cost_estimate=pl.CostEstimate(
            flops=2 * cells * rate_blocks.size, bytes_accessed=2 * rate_blocks.size, transcendentals=0
        ),
    )(pattern, q, rate_blocks, bracket)


def shifted(value, axis):
    peers = lax.axis_size(axis)
    return lax.ppermute(value, axis, [(i, i + 1) for i in range(peers - 1)])


def local(
    populations,
    rate_blocks,
    pattern,
    bracket,
    cross_section,
    emission,
    absorber,
    stream_speed,
    cross_speed,
    inflow,
):
    cells, levels = populations.shape
    strips = lax.axis_size("cell")
    absorbers = lax.all_gather(absorber, "cell")
    bracket = bracket.reshape(1, cells)
    cross = cross_section.reshape(1, levels)
    crosses = cross_section.reshape(levels // LANES, LANES)
    emission = emission.reshape(1, levels)
    absorber = absorber.reshape(1, cells)
    stream = stream_speed.reshape(1, cells)
    crossways = cross_speed.reshape(1, cells)

    field = jax.ShapeDtypeStruct((cells, levels), jnp.float32)
    rounded = jax.ShapeDtypeStruct((cells, levels), jnp.bfloat16)
    layer = jax.ShapeDtypeStruct((NY, levels), jnp.bfloat16)
    tiles = jax.ShapeDtypeStruct((strips, ROWS, LANES), jnp.float32)
    size = cells * levels * 4

    def swap(value):
        return lax.all_to_all(value, "cell", 0, 0, tiled=True)

    q, last, leaving = call(
        first_kernel, (populations, cross, emission, absorber), (rounded, layer, tiles), 3 * size
    )
    gathered = lax.all_gather(q, "lev", axis=1, tiled=True)
    arrived = shifted(last, "cell")
    entering, passes = call(
        functools.partial(scan_kernel, "cell", True), (swap(leaving), absorbers, crosses), (tiles, tiles), size
    )
    entering = swap(entering)
    rates = rate_term(gathered, rate_blocks, pattern, bracket)
    middle, q, last, leaving = call(
        functools.partial(step_kernel, False, "cell"),
        (populations, rates, entering, arrived, inflow, cross, emission, absorber, stream, crossways),
        (field, rounded, layer, tiles),
        5 * size,
    )
    gathered = lax.all_gather(q, "lev", axis=1, tiled=True)
    arrived = shifted(last, "cell")
    (entering,) = call(
        functools.partial(scan_kernel, "cell", False), (swap(leaving), passes), (tiles,), size
    )
    entering = swap(entering)
    rates = rate_term(gathered, rate_blocks, pattern, bracket)
    return call(
        functools.partial(step_kernel, True, "cell"),
        (middle, rates, entering, arrived, inflow, cross, emission, absorber, stream, crossways, populations),
        (field, field),
        5 * size,
    )


def solution(mesh):
    in_specs = (
        P("cell", "lev"),
        P(None, "lev", None, None, None),
        P("lev", None),
        P("cell"),
        P("lev"),
        P("lev"),
        P("cell"),
        P("cell"),
        P("cell"),
        P(None, "lev"),
    )
    out_specs = (P("cell", "lev"), P("cell", "lev"))
    return jax.shard_map(local, mesh=mesh, in_specs=in_specs, out_specs=out_specs, check_vma=False)
```

time: 2100 us -> 416 us (0.20)
  waiting for transfers between devices: 1700 us -> 0.07 us
  blocking collectives: 0 us -> 326 us
  other arithmetic: 319 us -> 0 us
  starting transfers between devices: 5.7 us -> 35.4 us
  Pallas kernels: 0 us -> 28.8 us
    all_gather x8 -> x2, waiting for transfers between devices: 1700 us -> 0.02 us  [local(): gathered = lax.all_gather(q, 'lev', axis=1, tiled=True)]
    unnamed x0 -> x1, blocking collectives: none -> 305 us
    select_n x257 -> x0, other arithmetic: 274 us -> none  [the longest x256 274 us: turn(): return jax.tree.map(lambda a, b: jnp.where(reached, a, b), new, before)]
    pallas_call x0 -> x7, Pallas kernels: none -> 28.8 us  [the longest x2 22.9 us: rate_term(): pl.pallas_call(rate_kernel, grid_spec=pltpu.PrefetchScalarGridSpec(num_sc...]
    all_to_all x0 -> x3, starting transfers between devices: none -> 28.6 us  [swap(): return lax.all_to_all(value, 'cell', 0, 0, tiled=True)]
    all_to_all x0 -> x1, blocking collectives: none -> 21.4 us  [swap(): return lax.all_to_all(value, 'cell', 0, 0, tiled=True)]
  transfers between devices with their start and end apart: 10 -> 7, of which waited for: 7 -> 0; matrix products, arithmetic and copies ran while one was open for 10% -> 1% of each run, Pallas kernels for 0% -> 6%
where the time goes in v1:
time: 416 us; the launch traced here: 415 us
  blocking collectives  326 us (78%)
  starting transfers between devices  35.4 us (9%)
  Pallas kernels  28.8 us (7%)
  between operations  14.8 us (4%)
  local copies, waits for them, and re-layouts  9.88 us (2%)
    unnamed x1, blocking collectives  305 us
    all_to_all x3, starting transfers between devices, swap(): return lax.all_to_all(value, 'cell', 0, 0, tiled=True)  28.6 us
    pallas_call x2, Pallas kernels, rate_term(): pl.pallas_call(rate_kernel, grid_spec=pltpu.PrefetchScalarGridSpec(num_sc...  22.9 us
    all_to_all x1, blocking collectives, swap(): return lax.all_to_all(value, 'cell', 0, 0, tiled=True)  21.4 us
    unnamed x36, local copies, waits for them, and re-layouts  9.81 us
  transfers between devices with their start and end apart: 7, of which 0 were waited for; matrix products, arithmetic and copies ran while one was open for 1% of the time, Pallas kernels for 6%

profile of v1, /device:TPU:2, one launch (start us, length us, event | category | flops | bytes accessed | tf_op | source)
XLA Modules:
  0.0 415.2 jit_solution(6099034000911804241)
XLA Ops:
  7.3 1.0 copy-done
  8.3 0.7 copy-done.5
  9.0 0.7 copy-done.8
  9.7 0.7 copy-done.10
  10.3 1.0 shard_map.113
  11.4 13.0 %all-to-all-start = ((f32[64,8,128]{2,1,0:T(8,128)}), f32[64,8,128]{2,1,0:T(8,128)S(1)}, u32[]{:S(2)}, u32[]{:S(2)}) async-start(f32[64,8,128]{2,1,0:T(8,128)} %get-tuple-element.12), calls=%async_computation | async-start | bytes 524288 | tf_op jit(solution)/shard_map/all_to_all | solution.py:269
  24.4 1.3 dynamic-slice
  26.3 0.9 dynamic-update-slice
  27.2 304.8 %all-reduce = f32[4096]{0:T(1024)S(1)} all-reduce(f32[4096]{0:T(1024)S(1)} %dynamic-update-slice), channel_id=2, replica_groups=mesh['cell'=64,'lev'=4] {'cell'}, use_global_device_ids=true, to_apply=%add | all-reduce | flops 4096 | bytes 32768
  332.0 0.7 copy-done.6
  332.7 1.0 shard_map.115
  333.7 9.7 %all-to-all-start.1 = ((f32[64,8,128]{2,1,0:T(8,128)}), f32[64,8,128]{2,1,0:T(8,128)S(1)}, u32[]{:S(2)}, u32[]{:S(2)}) async-start(f32[64,8,128]{2,1,0:T(8,128)} %get-tuple-element.13), calls=%async_computation.1 | async-start | bytes 524288 | tf_op jit(solution)/shard_map/all_to_all | solution.py:269
  343.4 3.4 collective-permute-start
  346.8 0.8 copy.12.pattern_ref
  347.6 1.2 copy-done.2
  349.5 11.4 %shard_map.114.refs_1_ = f32[64,2048]{1,0:T(8,128)S(1)} custom-call(s32[16,6]{1,0:T(8,128)S(1)} %copy.12.pattern_ref, bf16[64,8192]{1,0:T(8,128)(2,1)S(1)} %copy-done.2, bf16[2,16,6,128,128]{4,3,2,1,0:T(8,128)(2,1)} %table_ref.3, s32[1,64]{1,0:T(1,128)S(1)} %bitcast.18), custom_call_target="tpu_custom_call" | custom-call | flops 402653184 | bytes 6291456 | tf_op jit(solution)/shard_map/pallas_call | solution.py:214
  361.0 1.4 shard_map.116
  362.5 21.4 %all_to_all.20.exit_ref = f32[64,8,128]{2,1,0:T(8,128)S(1)} all-to-all(f32[64,8,128]{2,1,0:T(8,128)S(1)} %get-tuple-element.17), channel_id=1, replica_groups=mesh['cell'=64,'lev'=4] {'cell'}, dimensions={0} | all-to-all | bytes 524288 | tf_op jit(solution)/shard_map/all_to_all | solution.py:269
  383.8 0.9 shard_map.118
  384.7 5.9 %all-to-all-start.3 = ((f32[64,8,128]{2,1,0:T(8,128)}), f32[64,8,128]{2,1,0:T(8,128)S(1)}, u32[]{:S(2)}, u32[]{:S(2)}) async-start(f32[64,8,128]{2,1,0:T(8,128)} %shard_map.118), calls=%async_computation.3 | async-start | bytes 524288 | tf_op jit(solution)/shard_map/all_to_all | solution.py:269
  390.6 3.4 collective-permute-start.1
  394.1 1.2 copy-done.3
  395.3 11.4 %shard_map.117.refs_1_ = f32[64,2048]{1,0:T(8,128)S(1)} custom-call(s32[16,6]{1,0:T(8,128)S(1)} %copy.12.pattern_ref, bf16[64,8192]{1,0:T(8,128)(2,1)S(1)} %copy-done.3, bf16[2,16,6,128,128]{4,3,2,1,0:T(8,128)(2,1)} %table_ref.3, s32[1,64]{1,0:T(1,128)S(1)} %bitcast.19), custom_call_target="tpu_custom_call" | custom-call | flops 402653184 | bytes 6291456 | tf_op jit(solution)/shard_map/pallas_call | solution.py:214
  406.7 1.6 shard_map.119
  (38 shorter events, 0.9 us)
Async XLA Ops:
  7.2 353.8 %copy-start.11 = (f32[64]{0:T(128)S(1)}, f32[64]{0:T(128)}, u32[]{:S(2)}) copy-start(f32[64]{0:T(128)} %param.16) | copy-start | bytes 772
  7.2 353.8 %copy-start.14 = (f32[64]{0:T(128)S(1)}, f32[64]{0:T(128)}, u32[]{:S(2)}) copy-start(f32[64]{0:T(128)} %param.17) | copy-start | bytes 772
  7.2 353.8 %copy-start.15 = (f32[64]{0:T(128)S(1)}, f32[64]{0:T(128)}, u32[]{:S(2)}) copy-start(f32[64]{0:T(128)} %param.18) | copy-start | bytes 772
  7.2 340.4 %all-gather.4.cloned.1.call-start = ((), (), s32[]{:S(2)}) async-start(), calls=%async_computation.4 | async-start | bytes 1310720 | tf_op jit(solution)/shard_map/all_gather | solution.py:274
  7.2 1.0 copy-start
  8.3 0.7 copy-start.5
  9.0 0.7 copy-start.8
  9.7 0.7 copy-start.10
  10.3 350.6 %copy-start.1 = (f32[64,2048]{1,0:T(8,128)S(1)}, f32[64,2048]{1,0:T(8,128)}, u32[]{:S(2)}) copy-start(f32[64,2048]{1,0:T(8,128)} %refs_10_.1) | copy-start | bytes 1572868
  10.3 350.6 %copy-start.4 = (f32[16,2048]{1,0:T(8,128)S(1)}, f32[16,2048]{1,0:T(8,128)}, u32[]{:S(2)}) copy-start(f32[16,2048]{1,0:T(8,128)} %refs_4_.3) | copy-start | bytes 393220
  10.3 350.6 %copy-start.7 = (f32[2048]{0:T(1024)S(1)}, f32[2048]{0:T(1024)}, u32[]{:S(2)}) copy-start(f32[2048]{0:T(1024)} %param.14) | copy-start | bytes 24580
  10.3 350.6 %copy-start.9 = (f32[2048]{0:T(1024)S(1)}, f32[2048]{0:T(1024)}, u32[]{:S(2)}) copy-start(f32[2048]{0:T(1024)} %param.15) | copy-start | bytes 24580
  11.4 320.6 %all-to-all-start = ((f32[64,8,128]{2,1,0:T(8,128)}), f32[64,8,128]{2,1,0:T(8,128)S(1)}, u32[]{:S(2)}, u32[]{:S(2)}) async-start(f32[64,8,128]{2,1,0:T(8,128)} %get-tuple-element.12), calls=%async_computation | async-start | bytes 524288 | tf_op jit(solution)/shard_map/all_to_all | solution.py:269
  24.4 369.6 %copy-start.13 = (s32[64]{0:T(128)S(1)}, s32[64]{0:T(128)}, u32[]{:S(2)}) copy-start(s32[64]{0:T(128)} %param.13) | copy-start | bytes 772
  332.0 0.7 copy-start.6
  333.7 27.2 %all-to-all-start.1 = ((f32[64,8,128]{2,1,0:T(8,128)}), f32[64,8,128]{2,1,0:T(8,128)S(1)}, u32[]{:S(2)}, u32[]{:S(2)}) async-start(f32[64,8,128]{2,1,0:T(8,128)} %get-tuple-element.13), calls=%async_computation.1 | async-start | bytes 524288 | tf_op jit(solution)/shard_map/all_to_all | solution.py:269
  343.4 50.6 %all-gather.6.cloned.1.call-start = ((), (), s32[]{:S(2)}) async-start(), calls=%async_computation.5 | async-start | bytes 1310720 | tf_op jit(solution)/shard_map/all_gather | solution.py:287
  343.4 17.5 %collective-permute-start = (bf16[16,2048]{1,0:T(8,128)(2,1)S(1)}, bf16[16,2048]{1,0:T(8,128)(2,1)S(1)}, u32[]{:S(2)}, u32[]{:S(2)}) collective-permute-start(bf16[16,2048]{1,0:T(8,128)(2,1)S(1)} %get-tuple-element.14), channel_id=1, source_target_pairs={{0,4},{4,8},{8,12},{12,16},{16,20},{20,24},{24,28},{28,32},{32,36}... | collective-permute-start | bytes 196616 | tf_op jit(solution)/shard_map/ppermute | solution.py:236
  347.6 1.2 copy-start.2
  348.8 0.7 copy-start.12
  384.7 22.0 %all-to-all-start.3 = ((f32[64,8,128]{2,1,0:T(8,128)}), f32[64,8,128]{2,1,0:T(8,128)S(1)}, u32[]{:S(2)}, u32[]{:S(2)}) async-start(f32[64,8,128]{2,1,0:T(8,128)} %shard_map.118), calls=%async_computation.3 | async-start | bytes 524288 | tf_op jit(solution)/shard_map/all_to_all | solution.py:269
  390.6 16.1 %collective-permute-start.1 = (bf16[16,2048]{1,0:T(8,128)(2,1)S(1)}, bf16[16,2048]{1,0:T(8,128)(2,1)S(1)}, u32[]{:S(2)}, u32[]{:S(2)}) collective-permute-start(bf16[16,2048]{1,0:T(8,128)(2,1)S(1)} %get-tuple-element.19), channel_id=1, source_target_pairs={{0,4},{4,8},{8,12},{12,16},{16,20},{20,24},{24,28},{28,32},{32,36}... | collective-permute-start | bytes 196616 | tf_op jit(solution)/shard_map/ppermute | solution.py:236
  394.0 1.2 copy-start.3
Sparse Core Ops, SparseCore 0:
  11.5 28.6 all-gather.3
  362.6 25.3 all-gather.5

commit v2 on v1

--- a/solution.py
+++ b/solution.py
@@ -33,19 +33,35 @@
     return down, up
 
 
-def put_exits(exit_ref, group, groups, down, up):
+def put_exits(exit_ref, group, groups, down, up, depths=None):
     for way, value in enumerate((down, up)):
         for half in range(NY // ROWS):
             at = (way * (NY // ROWS) + half) * groups + group
-            exit_ref[at] = value[half * ROWS : (half + 1) * ROWS]
+            part = value[half * ROWS : (half + 1) * ROWS]
+            if depths is not None:
+                part = jnp.concatenate([part, depths[half]], axis=0).astype(exit_ref.dtype)
+            exit_ref[at] = part
 
 
 def get_enters(enter_ref, group, groups):
     found = []
     for way in range(2):
-        halves = [enter_ref[(way * (NY // ROWS) + half) * groups + group] for half in range(NY // ROWS)]
+        halves = [
+            enter_ref[(way * (NY // ROWS) + half) * groups + group]
+            for half in range(NY // ROWS)
+        ]
         found.append(jnp.concatenate(halves, axis=0))
     return found
+
+
+def depth_tiles(absorber):
+    total = sum(layers(absorber))
+    high = total.astype(jnp.bfloat16).astype(jnp.float32)
+    middle = (total - high).astype(jnp.bfloat16).astype(jnp.float32)
+    low = total - high - middle
+    lane = lax.broadcasted_iota(jnp.int32, (NY, LANES), 1)
+    spread = jnp.where(lane == 0, high, jnp.where(lane == 1, middle, jnp.where(lane == 2, low, 0.0)))
+    return [spread[half * ROWS : (half + 1) * ROWS] for half in range(NY // ROWS)]
 
 
 def absorbed_of(passed, emitted, enter_down, enter_up):
@@ -76,8 +92,21 @@
     return result
 
 
-def first_kernel(p_ref, cross_ref, emission_ref, absorber_ref, q_ref, last_ref, exit_ref):
+def first_kernel(p_hbm, cross_hbm, emission_hbm, absorber_hbm, q_ref, last_ref, exit_ref, *scratch):
+    sems = scratch[-1]
+    copies = [
+        pltpu.make_async_copy(source, target, sems.at[i])
+        for i, (source, target) in enumerate(
+            zip((p_hbm, cross_hbm, emission_hbm, absorber_hbm), scratch[:-1])
+        )
+    ]
+    for copy in copies:
+        copy.start()
+    for copy in copies:
+        copy.wait()
+    p_ref, cross_ref, emission_ref, absorber_ref = scratch[:-1]
     absorber = column(absorber_ref[...])
+    depths = depth_tiles(absorber)
     groups = p_ref.shape[1] // LANES
     for g in range(groups):
         at = slice(g * LANES, (g + 1) * LANES)
@@ -87,71 +116,64 @@
         last_ref[:, at] = q[-NY:]
         passed = layers(jnp.exp(-(absorber * cross_ref[:, at])))
         emitted = layers(p * emission_ref[:, at])
-        put_exits(exit_ref, g, groups, *exits(passed, emitted))
-
-
-def scan(exit_ref, pass_ref, enter_ref, way):
-    count = exit_ref.shape[0]
+        put_exits(exit_ref, g, groups, *exits(passed, emitted), depths)
+
+
+def scan(exits_in, pass_ref, enter_ref, way):
+    count = enter_ref.shape[0]
 
     def step(i, carry):
         at = jnp.where(way == 0, i, count - 1 - i)
         enter_ref[at] = carry
-        return pass_ref[at] * carry + exit_ref[at]
-
-    lax.fori_loop(0, count, step, jnp.zeros(exit_ref.shape[1:], jnp.float32), unroll=8)
-
-
-def strips_pass(absorbers_ref, cross_ref, pass_ref, half, group):
-    strips, cells = absorbers_ref.shape
-    y = lax.broadcasted_iota(jnp.int32, (ROWS, cells), 0) + half * ROWS
-    mine = lax.rem(lax.broadcasted_iota(jnp.int32, (ROWS, cells), 1), NY) == y
-    cross = cross_ref[pl.ds(group, 1), :]
-    for s in range(strips):
-        depth = jnp.sum(jnp.where(mine, absorbers_ref[s : s + 1, :], 0.0), axis=1, keepdims=True)
+        return pass_ref[at] * carry + exits_in(at)
+
+    lax.fori_loop(0, count, step, jnp.zeros(enter_ref.shape[1:], jnp.float32), unroll=8)
+
+
+def first_scan_kernel(axis, arrived_ref, cross_ref, enter_ref, pass_ref, exit_ref):
+    groups = cross_ref.shape[0]
+    me = lax.axis_index(axis)
+    cross = cross_ref[pl.ds(lax.rem(me, groups), 1), :]
+    for s in range(arrived_ref.shape[0]):
+        arrived = arrived_ref[s].astype(jnp.float32)
+        exit_ref[s] = arrived[:ROWS]
+        depth = jnp.sum(arrived[ROWS:], axis=1, keepdims=True)
         pass_ref[s] = jnp.exp(-(depth * cross))
-
-
-def scan_kernel(axis, make_pass, exit_ref, *refs):
-    groups = 16
-    me = lax.axis_index(axis)
-    group = lax.rem(me, groups)
-    half = lax.rem(me // groups, NY // ROWS)
-    way = me // (groups * (NY // ROWS))
-    if make_pass:
-        absorbers_ref, cross_ref, enter_ref, pass_ref = refs
-        strips_pass(absorbers_ref, cross_ref, pass_ref, half, group)
-    else:
-        pass_ref, enter_ref = refs
-    scan(exit_ref, pass_ref, enter_ref, way)
+    scan(lambda at: exit_ref[at], pass_ref, enter_ref, me // (groups * (NY // ROWS)))
+
+
+def second_scan_kernel(axis, groups, exit_ref, pass_ref, enter_ref):
+    scan(lambda at: exit_ref[at], pass_ref, enter_ref, lax.axis_index(axis) // (groups * (NY // ROWS)))
 
 
 def rate_kernel(pattern_ref, q_ref, table_ref, bracket_ref, out_ref):
-    r = pl.program_id(0)
-    count = table_ref.shape[2]
-    picked = jnp.concatenate(
-        [
-            q_ref[:, pl.ds(pl.multiple_of(pattern_ref[r, k] * LANES, LANES), LANES)]
-            for k in range(count)
-        ],
-        axis=1,
-    )
-    both = jnp.concatenate(
-        [
-            jnp.concatenate([table_ref[b, 0, k] for k in range(count)], axis=1)
-            for b in range(table_ref.shape[0])
-        ],
-        axis=0,
-    )
-    product = lax.dot_general(
-        picked, both, (((1,), (1,)), ((), ())), preferred_element_type=jnp.float32
-    )
+    brackets, rows, count = table_ref.shape[:3]
     bracket = column(bracket_ref[...])
-    out_ref[...] = jnp.where(bracket == 0, product[:, :LANES], product[:, LANES:])
-
-
-def step_kernel(
-    final, axis, *refs
-):
+    for row in range(rows):
+        r = pl.program_id(0) * rows + row
+        picked = jnp.concatenate(
+            [
+                q_ref[:, pl.ds(pl.multiple_of(pattern_ref[r, k] * LANES, LANES), LANES)]
+                for k in range(count)
+            ],
+            axis=1,
+        )
+        both = jnp.concatenate(
+            [
+                jnp.concatenate([table_ref[b, row, k] for k in range(count)], axis=1)
+                for b in range(brackets)
+            ],
+            axis=0,
+        )
+        product = lax.dot_general(
+            picked, both, (((1,), (1,)), ((), ())), preferred_element_type=jnp.float32
+        )
+        out_ref[:, row * LANES : (row + 1) * LANES] = jnp.where(
+            bracket == 0, product[:, :LANES], product[:, LANES:]
+        )
+
+
+def step_kernel(final, axis, *refs):
     (p_ref, rate_ref, enter_ref, arrived_ref, inflow_ref, cross_ref, emission_ref,
      absorber_ref, stream_ref, crossways_ref) = refs[:10]
     absorber = column(absorber_ref[...])
@@ -197,12 +219,13 @@
 LIMIT = pltpu.CompilerParams(vmem_limit_bytes=48 * 2**20)
 
 
-def call(body, args, outs, cost):
+def call(body, args, outs, cost, scratch=(), in_specs=None):
     return pl.pallas_call(
         body,
         out_shape=outs,
-        in_specs=vmem(len(args)),
+        in_specs=in_specs or vmem(len(args)),
         out_specs=vmem(len(outs)),
+        scratch_shapes=scratch,
         compiler_params=LIMIT,
         cost_estimate=pl.CostEstimate(flops=cost, bytes_accessed=cost, transcendentals=0),
     )(*args)
@@ -211,17 +234,18 @@
 def rate_term(q, rate_blocks, pattern, bracket):
     cells = q.shape[0]
     brackets, rows, count, block, _ = rate_blocks.shape
+    step = rows // 2
     return pl.pallas_call(
         rate_kernel,
         grid_spec=pltpu.PrefetchScalarGridSpec(
             num_scalar_prefetch=1,
-            grid=(rows,),
+            grid=(rows // step,),
             in_specs=[
                 pl.BlockSpec(q.shape, lambda r, pattern: (0, 0)),
-                pl.BlockSpec((brackets, 1, count, block, block), lambda r, pattern: (0, r, 0, 0, 0)),
+                pl.BlockSpec((brackets, step, count, block, block), lambda r, pattern: (0, r, 0, 0, 0)),
                 pl.BlockSpec(bracket.shape, lambda r, pattern: (0, 0)),
             ],
-            out_specs=pl.BlockSpec((cells, block), lambda r, pattern: (0, r)),
+            out_specs=pl.BlockSpec((cells, step * block), lambda r, pattern: (0, r)),
         ),
         out_shape=jax.ShapeDtypeStruct((cells, rows * block), jnp.float32),
         compiler_params=LIMIT,
@@ -250,7 +274,6 @@
 ):
     cells, levels = populations.shape
     strips = lax.axis_size("cell")
-    absorbers = lax.all_gather(absorber, "cell")
     bracket = bracket.reshape(1, cells)
     cross = cross_section.reshape(1, levels)
     crosses = cross_section.reshape(levels // LANES, LANES)
@@ -268,13 +291,24 @@
     def swap(value):
         return lax.all_to_all(value, "cell", 0, 0, tiled=True)
 
+    sources = (populations, cross, emission, absorber)
     q, last, leaving = call(
-        first_kernel, (populations, cross, emission, absorber), (rounded, layer, tiles), 3 * size
+        first_kernel,
+        sources,
+        (rounded, layer, jax.ShapeDtypeStruct((strips, 2 * ROWS, LANES), jnp.bfloat16)),
+        3 * size,
+        [pltpu.VMEM(value.shape, value.dtype) for value in sources]
+        + [pltpu.SemaphoreType.DMA((len(sources),))],
+        [pl.BlockSpec(memory_space=pl.ANY)] * len(sources),
     )
     gathered = lax.all_gather(q, "lev", axis=1, tiled=True)
     arrived = shifted(last, "cell")
     entering, passes = call(
-        functools.partial(scan_kernel, "cell", True), (swap(leaving), absorbers, crosses), (tiles, tiles), size
+        functools.partial(first_scan_kernel, "cell"),
+        (swap(leaving), crosses),
+        (tiles, tiles),
+        size,
+        [pltpu.VMEM(tiles.shape, jnp.float32)],
     )
     entering = swap(entering)
     rates = rate_term(gathered, rate_blocks, pattern, bracket)
@@ -287,7 +321,7 @@
     gathered = lax.all_gather(q, "lev", axis=1, tiled=True)
     arrived = shifted(last, "cell")
     (entering,) = call(
-        functools.partial(scan_kernel, "cell", False), (swap(leaving), passes), (tiles,), size
+        functools.partial(second_scan_kernel, "cell", levels // LANES), (swap(leaving), passes), (tiles,), size
     )
     entering = swap(entering)
     rates = rate_term(gathered, rate_blocks, pattern, bracket)

time: 416 us -> 105 us (0.25)
  blocking collectives: 326 us -> 44.8 us
  starting transfers between devices: 35.4 us -> 18.6 us
  Pallas kernels: 28.8 us -> 15.5 us
    unnamed x1 -> x0, blocking collectives: 305 us -> none
    all_to_all x1 -> x2, blocking collectives: 21.4 us -> 44.8 us  [swap(): return lax.all_to_all(value, 'cell', 0, 0, tiled=True)]
    all_to_all x3 -> x2, starting transfers between devices: 28.6 us -> 11.7 us  [swap(): return lax.all_to_all(value, 'cell', 0, 0, tiled=True)]
    pallas_call x2, Pallas kernels: 22.9 us -> 9.53 us  [rate_term(): pl.pallas_call(rate_kernel, grid_spec=pltpu.PrefetchScalarGridSpec(num_sc...]
    unnamed x36 -> x33, local copies, waits for them, and re-layouts: 9.81 us -> 7.69 us
  transfers between devices with their start and end apart: 7 -> 6, of which waited for: 0 -> 2; matrix products, arithmetic and copies ran while one was open for 1% -> 1% of each run, Pallas kernels for 6% -> 11%
where the time goes in v2:
time: 105 us; the launch traced here: 104 us
  blocking collectives  44.8 us (43%)
  starting transfers between devices  18.6 us (18%)
  Pallas kernels  15.5 us (15%)
  between operations  14.2 us (14%)
  local copies, waits for them, and re-layouts  7.69 us (7%)
  waiting for transfers between devices  2.78 us (3%)
    all_to_all x2, blocking collectives, swap(): return lax.all_to_all(value, 'cell', 0, 0, tiled=True)  44.8 us
    all_to_all x2, starting transfers between devices, swap(): return lax.all_to_all(value, 'cell', 0, 0, tiled=True)  11.7 us
    pallas_call x2, Pallas kernels, rate_term(): pl.pallas_call(rate_kernel, grid_spec=pltpu.PrefetchScalarGridSpec(num_sc...  9.53 us
    unnamed x33, local copies, waits for them, and re-layouts  7.69 us
    ppermute x2, starting transfers between devices, shifted(): return lax.ppermute(value, axis, [(i, i + 1) for i in range(peers - 1)])  6.74 us
    pallas_call x5, Pallas kernels, call(): pl.pallas_call(body, out_shape=outs, in_specs=in_specs or vmem(len(args))...  5.94 us
    all_to_all x2, waiting for transfers between devices, swap(): return lax.all_to_all(value, 'cell', 0, 0, tiled=True)  2.72 us
  transfers between devices with their start and end apart: 6, of which 2 were waited for; matrix products, arithmetic and copies ran while one was open for 1% of the time, Pallas kernels for 11%

profile of v2, /device:TPU:2, one launch (start us, length us, event | category | flops | bytes accessed | tf_op | source)
XLA Modules:
  0.0 103.6 jit_solution(1235891822561029391)
XLA Ops:
  7.3 1.0 copy-done
  8.3 0.7 copy-done.5
  9.0 0.7 copy-done.8
  9.7 0.7 copy-done.10
  10.3 1.0 shard_map.113
  11.4 24.8 %all_to_all.20.arrived_ref = bf16[64,16,128]{2,1,0:T(8,128)(2,1)S(1)} all-to-all(bf16[64,16,128]{2,1,0:T(8,128)(2,1)S(1)} %get-tuple-element.12), channel_id=1, replica_groups=mesh['cell'=64,'lev'=4] {'cell'}, dimensions={0} | all-to-all | bytes 524288 | tf_op jit(solution)/shard_map/all_to_all | solution.py:292
  36.2 0.7 copy-done.6
  36.9 1.0 shard_map.115
  37.9 6.0 %all-to-all-start.1 = ((f32[64,8,128]{2,1,0:T(8,128)}), f32[64,8,128]{2,1,0:T(8,128)S(1)}, u32[]{:S(2)}, u32[]{:S(2)}) async-start(f32[64,8,128]{2,1,0:T(8,128)} %get-tuple-element.13), calls=%async_computation.1 | async-start | bytes 524288 | tf_op jit(solution)/shard_map/all_to_all | solution.py:292
  44.0 3.4 %collective-permute-start = (bf16[16,2048]{1,0:T(8,128)(2,1)S(1)}, bf16[16,2048]{1,0:T(8,128)(2,1)S(1)}, u32[]{:S(2)}, u32[]{:S(2)}) collective-permute-start(bf16[16,2048]{1,0:T(8,128)(2,1)S(1)} %get-tuple-element.14), channel_id=1, source_target_pairs={{0,4},{4,8},{8,12},{12,16},{16,20},{20,24},{24,28},{28,32},{32,36}... | collective-permute-start | bytes 196616 | tf_op jit(solution)/shard_map/ppermute | solution.py:260
  47.4 0.8 copy.12.pattern_ref
  48.2 1.2 %copy-done.2 = bf16[64,8192]{1,0:T(8,128)(2,1)S(1)} copy-done((bf16[64,8192]{1,0:T(8,128)(2,1)S(1)}, bf16[64,8192]{1,0:T(8,128)(2,1)}, u32[]{:S(2)}) %copy-start.2) | copy-done | bytes 1048600
  49.4 0.7 copy-done.12
  50.0 4.8 %shard_map.114.refs_1_ = f32[64,2048]{1,0:T(8,128)S(1)} custom-call(s32[16,6]{1,0:T(8,128)S(1)} %copy.12.pattern_ref, bf16[64,8192]{1,0:T(8,128)(2,1)S(1)} %copy-done.2, bf16[2,16,6,128,128]{4,3,2,1,0:T(8,128)(2,1)} %table_ref.3, s32[1,64]{1,0:T(1,128)S(1)} %bitcast.17), custom_call_target="tpu_custom_call" | custom-call | flops 402653184 | bytes 6291456 | tf_op jit(solution)/shard_map/pallas_call | solution.py:238
  54.8 1.5 %all-to-all-done.1.refs_2_ = f32[64,8,128]{2,1,0:T(8,128)S(1)} async-done(((f32[64,8,128]{2,1,0:T(8,128)}), f32[64,8,128]{2,1,0:T(8,128)S(1)}, u32[]{:S(2)}, u32[]{:S(2)}) %all-to-all-start.1) | async-done | bytes 262176 | tf_op jit(solution)/shard_map/all_to_all | solution.py:292
  56.4 1.4 %shard_map.116 = (f32[64,2048]{1,0:T(8,128)S(1)}, bf16[64,2048]{1,0:T(8,128)(2,1)}, bf16[16,2048]{1,0:T(8,128)(2,1)S(1)}, f32[64,8,128]{2,1,0:T(8,128)S(1)}) custom-call(f32[64,2048]{1,0:T(8,128)S(1)} %copy-done.1, f32[64,2048]{1,0:T(8,128)S(1)} %shard_map.114.refs_1_, f32[64,8,128]{2,1,0:T(8,128)S(1)} %all-to-all-done.1.refs_2_, ...), custom_call_target="tpu_custom_call" | custom-call | flops 2621440 | bytes 2621440 | tf_op jit(solution)/shard_map/pallas_call | solution.py:223
  57.9 20.1 %all_to_all.21.exit_ref = f32[64,8,128]{2,1,0:T(8,128)S(1)} all-to-all(f32[64,8,128]{2,1,0:T(8,128)S(1)} %get-tuple-element.17), channel_id=1, replica_groups=mesh['cell'=64,'lev'=4] {'cell'}, dimensions={0} | all-to-all | bytes 524288 | tf_op jit(solution)/shard_map/all_to_all | solution.py:292
  77.9 0.9 shard_map.118
  78.8 5.7 %all-to-all-start.3 = ((f32[64,8,128]{2,1,0:T(8,128)}), f32[64,8,128]{2,1,0:T(8,128)S(1)}, u32[]{:S(2)}, u32[]{:S(2)}) async-start(f32[64,8,128]{2,1,0:T(8,128)} %shard_map.118), calls=%async_computation.3 | async-start | bytes 524288 | tf_op jit(solution)/shard_map/all_to_all | solution.py:292
  84.5 3.4 %collective-permute-start.1 = (bf16[16,2048]{1,0:T(8,128)(2,1)S(1)}, bf16[16,2048]{1,0:T(8,128)(2,1)S(1)}, u32[]{:S(2)}, u32[]{:S(2)}) collective-permute-start(bf16[16,2048]{1,0:T(8,128)(2,1)S(1)} %get-tuple-element.19), channel_id=1, source_target_pairs={{0,4},{4,8},{8,12},{12,16},{16,20},{20,24},{24,28},{28,32},{32,36}... | collective-permute-start | bytes 196616 | tf_op jit(solution)/shard_map/ppermute | solution.py:260
  87.9 1.2 %copy-done.3 = bf16[64,8192]{1,0:T(8,128)(2,1)S(1)} copy-done((bf16[64,8192]{1,0:T(8,128)(2,1)S(1)}, bf16[64,8192]{1,0:T(8,128)(2,1)}, u32[]{:S(2)}) %copy-start.3) | copy-done | bytes 1048600
  89.2 4.8 %shard_map.117.refs_1_ = f32[64,2048]{1,0:T(8,128)S(1)} custom-call(s32[16,6]{1,0:T(8,128)S(1)} %copy.12.pattern_ref, bf16[64,8192]{1,0:T(8,128)(2,1)S(1)} %copy-done.3, bf16[2,16,6,128,128]{4,3,2,1,0:T(8,128)(2,1)} %table_ref.3, s32[1,64]{1,0:T(1,128)S(1)} %bitcast.18), custom_call_target="tpu_custom_call" | custom-call | flops 402653184 | bytes 6291456 | tf_op jit(solution)/shard_map/pallas_call | solution.py:238
  93.9 1.2 %all-to-all-done.3.refs_2_ = f32[64,8,128]{2,1,0:T(8,128)S(1)} async-done(((f32[64,8,128]{2,1,0:T(8,128)}), f32[64,8,128]{2,1,0:T(8,128)S(1)}, u32[]{:S(2)}, u32[]{:S(2)}) %all-to-all-start.3) | async-done | bytes 262176 | tf_op jit(solution)/shard_map/all_to_all | solution.py:292
  95.1 1.6 %shard_map.119 = (f32[64,2048]{1,0:T(8,128)}, f32[64,2048]{1,0:T(8,128)}) custom-call(f32[64,2048]{1,0:T(8,128)S(1)} %get-tuple-element.15.refs_0_, f32[64,2048]{1,0:T(8,128)S(1)} %shard_map.117.refs_1_, f32[64,8,128]{2,1,0:T(8,128)S(1)} %all-to-all-done.3.refs_2_, bf16[16,2048]{1,0:T(8,128)(2,1)S(1)} %collective-permute-done.1.refs_3_, ...), custom_call_target="tpu_custom_call" | custom-call | flops 2621440 | bytes 2621440 | tf_op jit(solution)/shard_map/pallas_call | solution.py:223
  (32 shorter events, 0.2 us)
Async XLA Ops:
  7.2 49.2 %copy-start.11 = (f32[64]{0:T(128)S(1)}, f32[64]{0:T(128)}, u32[]{:S(2)}) copy-start(f32[64]{0:T(128)} %param.16) | copy-start | bytes 772
  7.2 49.2 %copy-start.14 = (f32[64]{0:T(128)S(1)}, f32[64]{0:T(128)}, u32[]{:S(2)}) copy-start(f32[64]{0:T(128)} %param.17) | copy-start | bytes 772
  7.2 49.2 %copy-start.15 = (f32[64]{0:T(128)S(1)}, f32[64]{0:T(128)}, u32[]{:S(2)}) copy-start(f32[64]{0:T(128)} %param.18) | copy-start | bytes 772
  7.2 41.0 %all-gather.3.cloned.1.call-start = ((), (), s32[]{:S(2)}) async-start(), calls=%async_computation.4 | async-start | bytes 1310720 | tf_op jit(solution)/shard_map/all_gather | solution.py:304
  7.2 1.0 %copy-start = (f32[64,2048]{1,0:T(8,128)S(1)}, f32[64,2048]{1,0:T(8,128)}, u32[]{:S(2)}) copy-start(f32[64,2048]{1,0:T(8,128)} %refs_10_.1) | copy-start | bytes 1572868
  8.3 0.7 copy-start.5
  9.0 0.7 copy-start.8
  9.7 0.7 copy-start.10
  10.3 46.0 %copy-start.1 = (f32[64,2048]{1,0:T(8,128)S(1)}, f32[64,2048]{1,0:T(8,128)}, u32[]{:S(2)}) copy-start(f32[64,2048]{1,0:T(8,128)} %refs_10_.1) | copy-start | bytes 1572868
  10.3 46.1 %copy-start.4 = (f32[16,2048]{1,0:T(8,128)S(1)}, f32[16,2048]{1,0:T(8,128)}, u32[]{:S(2)}) copy-start(f32[16,2048]{1,0:T(8,128)} %refs_4_.3) | copy-start | bytes 393220
  10.3 46.1 %copy-start.7 = (f32[2048]{0:T(1024)S(1)}, f32[2048]{0:T(1024)}, u32[]{:S(2)}) copy-start(f32[2048]{0:T(1024)} %param.14) | copy-start | bytes 24580
  10.3 46.1 %copy-start.9 = (f32[2048]{0:T(1024)S(1)}, f32[2048]{0:T(1024)}, u32[]{:S(2)}) copy-start(f32[2048]{0:T(1024)} %param.15) | copy-start | bytes 24580
  36.2 51.7 %copy-start.13 = (s32[64]{0:T(128)S(1)}, s32[64]{0:T(128)}, u32[]{:S(2)}) copy-start(s32[64]{0:T(128)} %param.13) | copy-start | bytes 772
  36.2 0.7 copy-start.6
  37.9 18.4 %all-to-all-start.1 = ((f32[64,8,128]{2,1,0:T(8,128)}), f32[64,8,128]{2,1,0:T(8,128)S(1)}, u32[]{:S(2)}, u32[]{:S(2)}) async-start(f32[64,8,128]{2,1,0:T(8,128)} %get-tuple-element.13), calls=%async_computation.1 | async-start | bytes 524288 | tf_op jit(solution)/shard_map/all_to_all | solution.py:292
  44.0 44.0 %all-gather.5.cloned.1.call-start = ((), (), s32[]{:S(2)}) async-start(), calls=%async_computation.5 | async-start | bytes 1310720 | tf_op jit(solution)/shard_map/all_gather | solution.py:321
  44.0 10.8 %collective-permute-start = (bf16[16,2048]{1,0:T(8,128)(2,1)S(1)}, bf16[16,2048]{1,0:T(8,128)(2,1)S(1)}, u32[]{:S(2)}, u32[]{:S(2)}) collective-permute-start(bf16[16,2048]{1,0:T(8,128)(2,1)S(1)} %get-tuple-element.14), channel_id=1, source_target_pairs={{0,4},{4,8},{8,12},{12,16},{16,20},{20,24},{24,28},{28,32},{32,36}... | collective-permute-start | bytes 196616 | tf_op jit(solution)/shard_map/ppermute | solution.py:260
  48.2 1.2 %copy-start.2 = (bf16[64,8192]{1,0:T(8,128)(2,1)S(1)}, bf16[64,8192]{1,0:T(8,128)(2,1)}, u32[]{:S(2)}) copy-start(bf16[64,8192]{1,0:T(8,128)(2,1)} %all-gather.3.cloned.1.call-done.q_ref) | copy-start | bytes 3145732
  49.4 0.7 copy-start.12
  78.8 16.3 %all-to-all-start.3 = ((f32[64,8,128]{2,1,0:T(8,128)}), f32[64,8,128]{2,1,0:T(8,128)S(1)}, u32[]{:S(2)}, u32[]{:S(2)}) async-start(f32[64,8,128]{2,1,0:T(8,128)} %shard_map.118), calls=%async_computation.3 | async-start | bytes 524288 | tf_op jit(solution)/shard_map/all_to_all | solution.py:292
  84.5 9.4 %collective-permute-start.1 = (bf16[16,2048]{1,0:T(8,128)(2,1)S(1)}, bf16[16,2048]{1,0:T(8,128)(2,1)S(1)}, u32[]{:S(2)}, u32[]{:S(2)}) collective-permute-start(bf16[16,2048]{1,0:T(8,128)(2,1)S(1)} %get-tuple-element.19), channel_id=1, source_target_pairs={{0,4},{4,8},{8,12},{12,16},{16,20},{20,24},{24,28},{28,32},{32,36}... | collective-permute-start | bytes 196616 | tf_op jit(solution)/shard_map/ppermute | solution.py:260
  87.9 1.2 %copy-start.3 = (bf16[64,8192]{1,0:T(8,128)(2,1)S(1)}, bf16[64,8192]{1,0:T(8,128)(2,1)}, u32[]{:S(2)}) copy-start(bf16[64,8192]{1,0:T(8,128)(2,1)} %all-gather.5.cloned.1.call-done.q_ref) | copy-start | bytes 3145732
Sparse Core Ops, SparseCore 0:
  11.5 28.2 all-gather.2
  58.0 24.0 all-gather.4

commit v3 on v2

--- a/solution.py
+++ b/solution.py
@@ -146,21 +146,25 @@
     scan(lambda at: exit_ref[at], pass_ref, enter_ref, lax.axis_index(axis) // (groups * (NY // ROWS)))
 
 
-def rate_kernel(pattern_ref, q_ref, table_ref, bracket_ref, out_ref):
+def rate_kernel(axis, pattern_ref, *refs):
+    pieces, (table_ref, bracket_ref, out_ref, q_ref) = refs[:-4], refs[-4:]
     brackets, rows, count = table_ref.shape[:3]
+    width = pieces[0].shape[1]
+    for place, piece in enumerate(pieces):
+        q_ref[:, place * width : (place + 1) * width] = piece[...]
+    me = lax.axis_index(axis)
     bracket = column(bracket_ref[...])
-    for row in range(rows):
-        r = pl.program_id(0) * rows + row
-        picked = jnp.concatenate(
-            [
-                q_ref[:, pl.ds(pl.multiple_of(pattern_ref[r, k] * LANES, LANES), LANES)]
-                for k in range(count)
-            ],
-            axis=1,
-        )
+
+    def block(r, k):
+        source = pattern_ref[r, k]
+        place = lax.rem(source, rows) + rows * ((source // rows) ^ me)
+        return q_ref[:, pl.ds(pl.multiple_of(place * LANES, LANES), LANES)]
+
+    for r in range(rows):
+        picked = jnp.concatenate([block(r, k) for k in range(count)], axis=1)
         both = jnp.concatenate(
             [
-                jnp.concatenate([table_ref[b, row, k] for k in range(count)], axis=1)
+                jnp.concatenate([table_ref[b, r, k] for k in range(count)], axis=1)
                 for b in range(brackets)
             ],
             axis=0,
@@ -168,7 +172,7 @@
         product = lax.dot_general(
             picked, both, (((1,), (1,)), ((), ())), preferred_element_type=jnp.float32
         )
-        out_ref[:, row * LANES : (row + 1) * LANES] = jnp.where(
+        out_ref[:, r * LANES : (r + 1) * LANES] = jnp.where(
             bracket == 0, product[:, :LANES], product[:, LANES:]
         )
 
@@ -216,7 +220,7 @@
     return [pl.BlockSpec(memory_space=pltpu.VMEM)] * count
 
 
-LIMIT = pltpu.CompilerParams(vmem_limit_bytes=48 * 2**20)
+LIMIT = pltpu.CompilerParams(vmem_limit_bytes=24 * 2**20)
 
 
 def call(body, args, outs, cost, scratch=(), in_specs=None):
@@ -231,28 +235,27 @@
     )(*args)
 
 
-def rate_term(q, rate_blocks, pattern, bracket):
-    cells = q.shape[0]
-    brackets, rows, count, block, _ = rate_blocks.shape
-    step = rows // 2
+def gathered(q, axis):
+    def swap(value, apart):
+        return lax.ppermute(value, axis, [(i, i ^ apart) for i in range(lax.axis_size(axis))])
+
+    far = swap(q, 2)
+    return q, swap(q, 1), far, swap(far, 1)
+
+
+def rate_term(pieces, rate_blocks, pattern, bracket):
+    cells, levels = pieces[0].shape
     return pl.pallas_call(
-        rate_kernel,
-        grid_spec=pltpu.PrefetchScalarGridSpec(
-            num_scalar_prefetch=1,
-            grid=(rows // step,),
-            in_specs=[
-                pl.BlockSpec(q.shape, lambda r, pattern: (0, 0)),
-                pl.BlockSpec((brackets, step, count, block, block), lambda r, pattern: (0, r, 0, 0, 0)),
-                pl.BlockSpec(bracket.shape, lambda r, pattern: (0, 0)),
-            ],
-            out_specs=pl.BlockSpec((cells, step * block), lambda r, pattern: (0, r)),
-        ),
-        out_shape=jax.ShapeDtypeStruct((cells, rows * block), jnp.float32),
+        functools.partial(rate_kernel, "lev"),
+        in_specs=[pl.BlockSpec(memory_space=pltpu.SMEM)] + vmem(len(pieces) + 2),
+        out_specs=pl.BlockSpec(memory_space=pltpu.VMEM),
+        out_shape=jax.ShapeDtypeStruct((cells, levels), jnp.float32),
+        scratch_shapes=[pltpu.VMEM((cells, len(pieces) * levels), jnp.bfloat16)],
         compiler_params=LIMIT,
         cost_estimate=pl.CostEstimate(
             flops=2 * cells * rate_blocks.size, bytes_accessed=2 * rate_blocks.size, transcendentals=0
         ),
-    )(pattern, q, rate_blocks, bracket)
+    )(pattern, *pieces, rate_blocks, bracket)
 
 
 def shifted(value, axis):
@@ -299,9 +302,9 @@
         3 * size,
         [pltpu.VMEM(value.shape, value.dtype) for value in sources]
         + [pltpu.SemaphoreType.DMA((len(sources),))],
-        [pl.BlockSpec(memory_space=pl.ANY)] * len(sources),
-    )
-    gathered = lax.all_gather(q, "lev", axis=1, tiled=True)
+        [pl.BlockSpec(memory_space=pltpu.HBM)] * len(sources),
+    )
+    pieces = gathered(q, "lev")
     arrived = shifted(last, "cell")
     entering, passes = call(
         functools.partial(first_scan_kernel, "cell"),
@@ -311,20 +314,20 @@
         [pltpu.VMEM(tiles.shape, jnp.float32)],
     )
     entering = swap(entering)
-    rates = rate_term(gathered, rate_blocks, pattern, bracket)
+    rates = rate_term(pieces, rate_blocks, pattern, bracket)
     middle, q, last, leaving = call(
         functools.partial(step_kernel, False, "cell"),
         (populations, rates, entering, arrived, inflow, cross, emission, absorber, stream, crossways),
         (field, rounded, layer, tiles),
         5 * size,
     )
-    gathered = lax.all_gather(q, "lev", axis=1, tiled=True)
+    pieces = gathered(q, "lev")
     arrived = shifted(last, "cell")
     (entering,) = call(
         functools.partial(second_scan_kernel, "cell", levels // LANES), (swap(leaving), passes), (tiles,), size
     )
     entering = swap(entering)
-    rates = rate_term(gathered, rate_blocks, pattern, bracket)
+    rates = rate_term(pieces, rate_blocks, pattern, bracket)
     return call(
         functools.partial(step_kernel, True, "cell"),
         (middle, rates, entering, arrived, inflow, cross, emission, absorber, stream, crossways, populations),

time: 105 us -> 94.2 us (0.90)
  blocking collectives: 44.8 us -> 0 us
  starting transfers between devices: 18.6 us -> 49.3 us
  waiting for transfers between devices: 2.78 us -> 20.4 us
  between operations: 14.2 us -> 0.87 us
  Pallas kernels: 15.5 us -> 11.4 us
  local copies, waits for them, and re-layouts: 7.69 us -> 10.8 us
    all_to_all x2 -> x0, blocking collectives: 44.8 us -> none  [swap(): return lax.all_to_all(value, 'cell', 0, 0, tiled=True)]
    all_to_all x2 -> x4, starting transfers between devices: 11.7 us -> 35.5 us  [swap(): return lax.all_to_all(value, 'cell', 0, 0, tiled=True)]
    all_to_all x2 -> x4, waiting for transfers between devices: 2.72 us -> 20.3 us  [swap(): return lax.all_to_all(value, 'cell', 0, 0, tiled=True)]
    ppermute x0 -> x6, starting transfers between devices: none -> 7.15 us  [swap(): lax.ppermute(value, axis, [(i, i ^ apart) for i in range(lax.axis_size(ax...]
    pallas_call x2, Pallas kernels: 9.53 us -> 5.46 us  [rate_term(): pl.pallas_call(functools.partial(rate_kernel, 'lev'), in_specs=[pl.BlockS...]
    unnamed x33, local copies, waits for them, and re-layouts: 7.69 us -> 10.8 us
  transfers between devices with their start and end apart: 6 -> 12, of which waited for: 2 -> 4; matrix products, arithmetic and copies ran while one was open for 1% -> 1% of each run, Pallas kernels for 11% -> 8%
where the time goes in v3:
time: 94.2 us; the launch traced here: 92.8 us
  starting transfers between devices  49.3 us (52%)
  waiting for transfers between devices  20.4 us (22%)
  Pallas kernels  11.4 us (12%)
  local copies, waits for them, and re-layouts  10.8 us (11%)
    all_to_all x4, starting transfers between devices, swap(): return lax.all_to_all(value, 'cell', 0, 0, tiled=True)  35.5 us
    all_to_all x4, waiting for transfers between devices, swap(): return lax.all_to_all(value, 'cell', 0, 0, tiled=True)  20.3 us
    unnamed x33, local copies, waits for them, and re-layouts  10.8 us
    ppermute x6, starting transfers between devices, swap(): lax.ppermute(value, axis, [(i, i ^ apart) for i in range(lax.axis_size(ax...  7.15 us
    ppermute x2, starting transfers between devices, shifted(): return lax.ppermute(value, axis, [(i, i + 1) for i in range(peers - 1)])  6.72 us
    pallas_call x5, Pallas kernels, call(): pl.pallas_call(body, out_shape=outs, in_specs=in_specs or vmem(len(args))...  5.97 us
    pallas_call x2, Pallas kernels, rate_term(): pl.pallas_call(functools.partial(rate_kernel, 'lev'), in_specs=[pl.BlockS...  5.46 us
  transfers between devices with their start and end apart: 12, of which 4 were waited for; matrix products, arithmetic and copies ran while one was open for 1% of the time, Pallas kernels for 8%

profile of v3, /device:TPU:2, one launch (start us, length us, event | category | flops | bytes accessed | tf_op | source)
XLA Modules:
  0.0 92.8 jit_solution(17827773334424095432)
XLA Ops:
  0.7 1.1 %copy-done.2 = f32[64,2048]{1,0:T(8,128)S(1)} copy-done((f32[64,2048]{1,0:T(8,128)S(1)}, f32[64,2048]{1,0:T(8,128)}, u32[]{:S(2)}) %copy-start.2) | copy-done | bytes 524312
  1.7 0.7 copy-done.5
  3.8 1.0 %shard_map.113 = (bf16[64,2048]{1,0:T(8,128)(2,1)S(1)}, bf16[16,2048]{1,0:T(8,128)(2,1)S(1)}, bf16[64,16,128]{2,1,0:T(8,128)(2,1)}) custom-call(f32[64,2048]{1,0:T(8,128)S(1)} %copy-done.2, f32[1,2048]{1,0:T(1,128)S(1)} %bitcast.7, f32[1,2048]{1,0:T(1,128)S(1)} %bitcast.11, f32[1,64]{1,0:T(1,128)S(1)} %bitcast.14), custom_call_target="tpu_custom_call" | custom-call | flops 1572864 | bytes 1572864 | tf_op jit(solution)/shard_map/pallas_call | solution.py:227
  4.8 13.0 %all-to-all-start = ((bf16[64,16,128]{2,1,0:T(8,128)(2,1)}), bf16[64,16,128]{2,1,0:T(8,128)(2,1)S(1)}, u32[]{:S(2)}, u32[]{:S(2)}) async-start(bf16[64,16,128]{2,1,0:T(8,128)(2,1)} %get-tuple-element.12), calls=%async_computation | async-start | bytes 524288 | tf_op jit(solution)/shard_map/all_to_all | solution.py:295
  17.9 3.0 %collective-permute-start.1 = (bf16[64,2048]{1,0:T(8,128)(2,1)S(1)}, bf16[64,2048]{1,0:T(8,128)(2,1)S(1)}, u32[]{:S(2)}, u32[]{:S(2)}) collective-permute-start(bf16[64,2048]{1,0:T(8,128)(2,1)S(1)} %get-tuple-element.11.refs_0_), channel_id=1, source_target_pairs={{0,2},{1,3},{2,0},{3,1},{4,6},{5,7},{6,4},{7,5},{8,10},{9,11},{10,... | collective-permute-start | bytes 786440 | tf_op jit(solution)/shard_map/ppermute | solution.py:240
  20.9 9.0 %all-to-all-done.arrived_ref = bf16[64,16,128]{2,1,0:T(8,128)(2,1)S(1)} async-done(((bf16[64,16,128]{2,1,0:T(8,128)(2,1)}), bf16[64,16,128]{2,1,0:T(8,128)(2,1)S(1)}, u32[]{:S(2)}, u32[]{:S(2)}) %all-to-all-start) | async-done | bytes 262176 | tf_op jit(solution)/shard_map/all_to_all | solution.py:295
  29.8 0.7 copy-done.6
  30.5 1.0 %shard_map.115 = (f32[64,8,128]{2,1,0:T(8,128)}, f32[64,8,128]{2,1,0:T(8,128)S(1)}) custom-call(bf16[64,16,128]{2,1,0:T(8,128)(2,1)S(1)} %all-to-all-done.arrived_ref, f32[16,128]{1,0:T(8,128)S(1)} %bitcast.8), custom_call_target="tpu_custom_call" | custom-call | flops 524288 | bytes 524288 | tf_op jit(solution)/shard_map/pallas_call | solution.py:227
  31.6 6.0 %all-to-all-start.1 = ((f32[64,8,128]{2,1,0:T(8,128)}), f32[64,8,128]{2,1,0:T(8,128)S(1)}, u32[]{:S(2)}, u32[]{:S(2)}) async-start(f32[64,8,128]{2,1,0:T(8,128)} %get-tuple-element.13), calls=%async_computation.1 | async-start | bytes 524288 | tf_op jit(solution)/shard_map/all_to_all | solution.py:295
  38.2 3.4 %collective-permute-start.3 = (bf16[16,2048]{1,0:T(8,128)(2,1)S(1)}, bf16[16,2048]{1,0:T(8,128)(2,1)S(1)}, u32[]{:S(2)}, u32[]{:S(2)}) collective-permute-start(bf16[16,2048]{1,0:T(8,128)(2,1)S(1)} %get-tuple-element.14), channel_id=1, source_target_pairs={{0,4},{4,8},{8,12},{12,16},{16,20},{20,24},{24,28},{28,32},{32,36}... | collective-permute-start | bytes 196616 | tf_op jit(solution)/shard_map/ppermute | solution.py:263
  41.6 0.8 copy.12.pattern_ref
  42.3 2.8 %copy-done = bf16[2,16,6,128,128]{4,3,2,1,0:T(8,128)(2,1)S(1)} copy-done((bf16[2,16,6,128,128]{4,3,2,1,0:T(8,128)(2,1)S(1)}, bf16[2,16,6,128,128]{4,3,2,1,0:T(8,128)(2,1)}, u32[]{:S(2)}) %copy-start) | copy-done | bytes 6291480
  45.8 2.7 %shard_map.114.refs_1_ = f32[64,2048]{1,0:T(8,128)S(1)} custom-call(s32[16,6]{1,0:T(8,128)S(1)} %copy.12.pattern_ref, bf16[64,2048]{1,0:T(8,128)(2,1)S(1)} %get-tuple-element.11.refs_0_, bf16[64,2048]{1,0:T(8,128)(2,1)S(1)} %collective-permute-done.refs_1_, bf16[64,2048]{1,0:T(8,128)(2,1)S(1)} %collective-permute-done.1.refs_2_, ...), custom_call_target="tpu_custom_call" | custom-call | flops 402653184 | bytes 6291456 | tf_op jit(solution)/shard_map/pallas_call | solution.py:248
  49.1 1.4 %shard_map.116 = (f32[64,2048]{1,0:T(8,128)S(1)}, bf16[64,2048]{1,0:T(8,128)(2,1)S(1)}, bf16[16,2048]{1,0:T(8,128)(2,1)S(1)}, f32[64,8,128]{2,1,0:T(8,128)}) custom-call(f32[64,2048]{1,0:T(8,128)S(1)} %copy-done.3, f32[64,2048]{1,0:T(8,128)S(1)} %shard_map.114.refs_1_, f32[64,8,128]{2,1,0:T(8,128)S(1)} %all-to-all-done.1.refs_2_, ...), custom_call_target="tpu_custom_call" | custom-call | flops 2621440 | bytes 2621440 | tf_op jit(solution)/shard_map/pallas_call | solution.py:227
  50.6 10.4 %all-to-all-start.2 = ((f32[64,8,128]{2,1,0:T(8,128)}), f32[64,8,128]{2,1,0:T(8,128)S(1)}, u32[]{:S(2)}, u32[]{:S(2)}) async-start(f32[64,8,128]{2,1,0:T(8,128)} %get-tuple-element.17), calls=%async_computation.2 | async-start | bytes 524288 | tf_op jit(solution)/shard_map/all_to_all | solution.py:295
  61.0 3.0 %collective-permute-start.5 = (bf16[64,2048]{1,0:T(8,128)(2,1)S(1)}, bf16[64,2048]{1,0:T(8,128)(2,1)S(1)}, u32[]{:S(2)}, u32[]{:S(2)}) collective-permute-start(bf16[64,2048]{1,0:T(8,128)(2,1)S(1)} %get-tuple-element.16.refs_0_), channel_id=1, source_target_pairs={{0,2},{1,3},{2,0},{3,1},{4,6},{5,7},{6,4},{7,5},{8,10},{9,11},{10,... | collective-permute-start | bytes 786440 | tf_op jit(solution)/shard_map/ppermute | solution.py:240
  64.0 8.9 %all-to-all-done.2.exit_ref = f32[64,8,128]{2,1,0:T(8,128)S(1)} async-done(((f32[64,8,128]{2,1,0:T(8,128)}), f32[64,8,128]{2,1,0:T(8,128)S(1)}, u32[]{:S(2)}, u32[]{:S(2)}) %all-to-all-start.2) | async-done | bytes 262176 | tf_op jit(solution)/shard_map/all_to_all | solution.py:295
  72.9 0.9 shard_map.118
  73.8 6.0 %all-to-all-start.3 = ((f32[64,8,128]{2,1,0:T(8,128)}), f32[64,8,128]{2,1,0:T(8,128)S(1)}, u32[]{:S(2)}, u32[]{:S(2)}) async-start(f32[64,8,128]{2,1,0:T(8,128)} %shard_map.118), calls=%async_computation.3 | async-start | bytes 524288 | tf_op jit(solution)/shard_map/all_to_all | solution.py:295
  80.4 3.4 %collective-permute-start.7 = (bf16[16,2048]{1,0:T(8,128)(2,1)S(1)}, bf16[16,2048]{1,0:T(8,128)(2,1)S(1)}, u32[]{:S(2)}, u32[]{:S(2)}) collective-permute-start(bf16[16,2048]{1,0:T(8,128)(2,1)S(1)} %get-tuple-element.19), channel_id=1, source_target_pairs={{0,4},{4,8},{8,12},{12,16},{16,20},{20,24},{24,28},{28,32},{32,36}... | collective-permute-start | bytes 196616 | tf_op jit(solution)/shard_map/ppermute | solution.py:263
  83.8 2.8 %copy-done.1 = bf16[2,16,6,128,128]{4,3,2,1,0:T(8,128)(2,1)S(1)} copy-done((bf16[2,16,6,128,128]{4,3,2,1,0:T(8,128)(2,1)S(1)}, bf16[2,16,6,128,128]{4,3,2,1,0:T(8,128)(2,1)}, u32[]{:S(2)}) %copy-start.1) | copy-done | bytes 6291480
  86.6 2.7 %shard_map.117.refs_1_ = f32[64,2048]{1,0:T(8,128)S(1)} custom-call(s32[16,6]{1,0:T(8,128)S(1)} %copy.12.pattern_ref, bf16[64,2048]{1,0:T(8,128)(2,1)S(1)} %get-tuple-element.16.refs_0_, bf16[64,2048]{1,0:T(8,128)(2,1)S(1)} %collective-permute-done.4.refs_1_, bf16[64,2048]{1,0:T(8,128)(2,1)S(1)} %collective-permute-done.5.refs_2_, ...), custom_call_target="tpu_custom_call" | custom-call | flops 402653184 | bytes 6291456 | tf_op jit(solution)/shard_map/pallas_call | solution.py:248
  89.3 1.9 %all-to-all-done.3.refs_2_ = f32[64,8,128]{2,1,0:T(8,128)S(1)} async-done(((f32[64,8,128]{2,1,0:T(8,128)}), f32[64,8,128]{2,1,0:T(8,128)S(1)}, u32[]{:S(2)}, u32[]{:S(2)}) %all-to-all-start.3) | async-done | bytes 262176 | tf_op jit(solution)/shard_map/all_to_all | solution.py:295
  91.2 1.6 %shard_map.119 = (f32[64,2048]{1,0:T(8,128)}, f32[64,2048]{1,0:T(8,128)}) custom-call(f32[64,2048]{1,0:T(8,128)S(1)} %get-tuple-element.15.refs_0_, f32[64,2048]{1,0:T(8,128)S(1)} %shard_map.117.refs_1_, f32[64,8,128]{2,1,0:T(8,128)S(1)} %all-to-all-done.3.refs_2_, bf16[16,2048]{1,0:T(8,128)(2,1)S(1)} %collective-permute-done.7.refs_3_, ...), custom_call_target="tpu_custom_call" | custom-call | flops 2621440 | bytes 2621440 | tf_op jit(solution)/shard_map/pallas_call | solution.py:227
  (40 shorter events, 3.8 us)
Async XLA Ops:
  0.6 48.5 %copy-start.11 = (f32[64]{0:T(128)S(1)}, f32[64]{0:T(128)}, u32[]{:S(2)}) copy-start(f32[64]{0:T(128)} %param.16) | copy-start | bytes 772
  0.6 48.5 %copy-start.15 = (f32[64]{0:T(128)S(1)}, f32[64]{0:T(128)}, u32[]{:S(2)}) copy-start(f32[64]{0:T(128)} %param.18) | copy-start | bytes 772
  0.7 48.4 %copy-start.14 = (f32[64]{0:T(128)S(1)}, f32[64]{0:T(128)}, u32[]{:S(2)}) copy-start(f32[64]{0:T(128)} %param.17) | copy-start | bytes 772
  0.7 1.1 %copy-start.2 = (f32[64,2048]{1,0:T(8,128)S(1)}, f32[64,2048]{1,0:T(8,128)}, u32[]{:S(2)}) copy-start(f32[64,2048]{1,0:T(8,128)} %refs_10_.1) | copy-start | bytes 1572868
  3.8 45.3 %copy-start.3 = (f32[64,2048]{1,0:T(8,128)S(1)}, f32[64,2048]{1,0:T(8,128)}, u32[]{:S(2)}) copy-start(f32[64,2048]{1,0:T(8,128)} %refs_10_.1) | copy-start | bytes 1572868
  3.8 45.3 %copy-start.4 = (f32[16,2048]{1,0:T(8,128)S(1)}, f32[16,2048]{1,0:T(8,128)}, u32[]{:S(2)}) copy-start(f32[16,2048]{1,0:T(8,128)} %refs_4_.7) | copy-start | bytes 393220
  3.8 45.3 %copy-start.7 = (f32[2048]{0:T(1024)S(1)}, f32[2048]{0:T(1024)}, u32[]{:S(2)}) copy-start(f32[2048]{0:T(1024)} %param.14) | copy-start | bytes 24580
  3.8 45.4 %copy-start.9 = (f32[2048]{0:T(1024)S(1)}, f32[2048]{0:T(1024)}, u32[]{:S(2)}) copy-start(f32[2048]{0:T(1024)} %param.15) | copy-start | bytes 24580
  4.8 79.0 %copy-start.13 = (s32[64]{0:T(128)S(1)}, s32[64]{0:T(128)}, u32[]{:S(2)}) copy-start(s32[64]{0:T(128)} %param.13) | copy-start | bytes 772
  4.8 25.0 %all-to-all-start = ((bf16[64,16,128]{2,1,0:T(8,128)(2,1)}), bf16[64,16,128]{2,1,0:T(8,128)(2,1)S(1)}, u32[]{:S(2)}, u32[]{:S(2)}) async-start(bf16[64,16,128]{2,1,0:T(8,128)(2,1)} %get-tuple-element.12), calls=%async_computation | async-start | bytes 524288 | tf_op jit(solution)/shard_map/all_to_all | solution.py:295
  17.9 19.8 %collective-permute-start.1 = (bf16[64,2048]{1,0:T(8,128)(2,1)S(1)}, bf16[64,2048]{1,0:T(8,128)(2,1)S(1)}, u32[]{:S(2)}, u32[]{:S(2)}) collective-permute-start(bf16[64,2048]{1,0:T(8,128)(2,1)S(1)} %get-tuple-element.11.refs_0_), channel_id=1, source_target_pairs={{0,2},{1,3},{2,0},{3,1},{4,6},{5,7},{6,4},{7,5},{8,10},{9,11},{10,... | collective-permute-start | bytes 786440 | tf_op jit(solution)/shard_map/ppermute | solution.py:240
  29.8 0.7 copy-start.6
  31.6 17.5 %all-to-all-start.1 = ((f32[64,8,128]{2,1,0:T(8,128)}), f32[64,8,128]{2,1,0:T(8,128)S(1)}, u32[]{:S(2)}, u32[]{:S(2)}) async-start(f32[64,8,128]{2,1,0:T(8,128)} %get-tuple-element.13), calls=%async_computation.1 | async-start | bytes 524288 | tf_op jit(solution)/shard_map/all_to_all | solution.py:295
  37.6 4.7 %collective-permute-start = (bf16[64,2048]{1,0:T(8,128)(2,1)S(1)}, bf16[64,2048]{1,0:T(8,128)(2,1)S(1)}, u32[]{:S(2)}, u32[]{:S(2)}) collective-permute-start(bf16[64,2048]{1,0:T(8,128)(2,1)S(1)} %get-tuple-element.11.refs_0_), channel_id=1, source_target_pairs={{0,1},{1,0},{2,3},{3,2},{4,5},{5,4},{6,7},{7,6},{8,9},{9,8},{10,11... | collective-permute-start | bytes 786440 | tf_op jit(solution)/shard_map/ppermute | solution.py:240
  37.7 4.6 %collective-permute-start.2 = (bf16[64,2048]{1,0:T(8,128)(2,1)S(1)}, bf16[64,2048]{1,0:T(8,128)(2,1)S(1)}, u32[]{:S(2)}, u32[]{:S(2)}) collective-permute-start(bf16[64,2048]{1,0:T(8,128)(2,1)S(1)} %collective-permute-done.1.refs_2_), channel_id=1, source_target_pairs={{0,1},{1,0},{2,3},{3,2},{4,5},{5,4},{6,7},{7,6},{8,9},{9,8},{10,11... | collective-permute-start | bytes 786440 | tf_op jit(solution)/shard_map/ppermute | solution.py:240
  38.2 10.3 %collective-permute-start.3 = (bf16[16,2048]{1,0:T(8,128)(2,1)S(1)}, bf16[16,2048]{1,0:T(8,128)(2,1)S(1)}, u32[]{:S(2)}, u32[]{:S(2)}) collective-permute-start(bf16[16,2048]{1,0:T(8,128)(2,1)S(1)} %get-tuple-element.14), channel_id=1, source_target_pairs={{0,4},{4,8},{8,12},{12,16},{16,20},{20,24},{24,28},{28,32},{32,36}... | collective-permute-start | bytes 196616 | tf_op jit(solution)/shard_map/ppermute | solution.py:263
  42.3 2.8 %copy-start = (bf16[2,16,6,128,128]{4,3,2,1,0:T(8,128)(2,1)S(1)}, bf16[2,16,6,128,128]{4,3,2,1,0:T(8,128)(2,1)}, u32[]{:S(2)}) copy-start(bf16[2,16,6,128,128]{4,3,2,1,0:T(8,128)(2,1)} %refs_4_.6) | copy-start | bytes 18874372
  50.6 22.3 %all-to-all-start.2 = ((f32[64,8,128]{2,1,0:T(8,128)}), f32[64,8,128]{2,1,0:T(8,128)S(1)}, u32[]{:S(2)}, u32[]{:S(2)}) async-start(f32[64,8,128]{2,1,0:T(8,128)} %get-tuple-element.17), calls=%async_computation.2 | async-start | bytes 524288 | tf_op jit(solution)/shard_map/all_to_all | solution.py:295
  61.0 18.9 %collective-permute-start.5 = (bf16[64,2048]{1,0:T(8,128)(2,1)S(1)}, bf16[64,2048]{1,0:T(8,128)(2,1)S(1)}, u32[]{:S(2)}, u32[]{:S(2)}) collective-permute-start(bf16[64,2048]{1,0:T(8,128)(2,1)S(1)} %get-tuple-element.16.refs_0_), channel_id=1, source_target_pairs={{0,2},{1,3},{2,0},{3,1},{4,6},{5,7},{6,4},{7,5},{8,10},{9,11},{10,... | collective-permute-start | bytes 786440 | tf_op jit(solution)/shard_map/ppermute | solution.py:240
  73.8 17.4 %all-to-all-start.3 = ((f32[64,8,128]{2,1,0:T(8,128)}), f32[64,8,128]{2,1,0:T(8,128)S(1)}, u32[]{:S(2)}, u32[]{:S(2)}) async-start(f32[64,8,128]{2,1,0:T(8,128)} %shard_map.118), calls=%async_computation.3 | async-start | bytes 524288 | tf_op jit(solution)/shard_map/all_to_all | solution.py:295
  79.8 4.0 %collective-permute-start.4 = (bf16[64,2048]{1,0:T(8,128)(2,1)S(1)}, bf16[64,2048]{1,0:T(8,128)(2,1)S(1)}, u32[]{:S(2)}, u32[]{:S(2)}) collective-permute-start(bf16[64,2048]{1,0:T(8,128)(2,1)S(1)} %get-tuple-element.16.refs_0_), channel_id=1, source_target_pairs={{0,1},{1,0},{2,3},{3,2},{4,5},{5,4},{6,7},{7,6},{8,9},{9,8},{10,11... | collective-permute-start | bytes 786440 | tf_op jit(solution)/shard_map/ppermute | solution.py:240
  79.9 3.9 %collective-permute-start.6 = (bf16[64,2048]{1,0:T(8,128)(2,1)S(1)}, bf16[64,2048]{1,0:T(8,128)(2,1)S(1)}, u32[]{:S(2)}, u32[]{:S(2)}) collective-permute-start(bf16[64,2048]{1,0:T(8,128)(2,1)S(1)} %collective-permute-done.5.refs_2_), channel_id=1, source_target_pairs={{0,1},{1,0},{2,3},{3,2},{4,5},{5,4},{6,7},{7,6},{8,9},{9,8},{10,11... | collective-permute-start | bytes 786440 | tf_op jit(solution)/shard_map/ppermute | solution.py:240
  80.4 8.9 %collective-permute-start.7 = (bf16[16,2048]{1,0:T(8,128)(2,1)S(1)}, bf16[16,2048]{1,0:T(8,128)(2,1)S(1)}, u32[]{:S(2)}, u32[]{:S(2)}) collective-permute-start(bf16[16,2048]{1,0:T(8,128)(2,1)S(1)} %get-tuple-element.19), channel_id=1, source_target_pairs={{0,4},{4,8},{8,12},{12,16},{16,20},{20,24},{24,28},{28,32},{32,36}... | collective-permute-start | bytes 196616 | tf_op jit(solution)/shard_map/ppermute | solution.py:263
  83.8 2.8 %copy-start.1 = (bf16[2,16,6,128,128]{4,3,2,1,0:T(8,128)(2,1)S(1)}, bf16[2,16,6,128,128]{4,3,2,1,0:T(8,128)(2,1)}, u32[]{:S(2)}) copy-start(bf16[2,16,6,128,128]{4,3,2,1,0:T(8,128)(2,1)} %refs_4_.6) | copy-start | bytes 18874372
  (4 other events, 2.7 us)

commit v4 on v3

--- a/solution.py
+++ b/solution.py
@@ -10,6 +10,8 @@
 NY = 16
 LANES = 128
 ROWS = 8
+HALF = 4
+PARTS = 3
 time_step = 0.25
 
 
@@ -33,35 +35,43 @@
     return down, up
 
 
-def put_exits(exit_ref, group, groups, down, up, depths=None):
-    for way, value in enumerate((down, up)):
-        for half in range(NY // ROWS):
-            at = (way * (NY // ROWS) + half) * groups + group
-            part = value[half * ROWS : (half + 1) * ROWS]
-            if depths is not None:
-                part = jnp.concatenate([part, depths[half]], axis=0).astype(exit_ref.dtype)
-            exit_ref[at] = part
+def top(value):
+    return lax.broadcasted_iota(jnp.int32, value.shape, 0) < HALF
+
+
+def to_tiles(down, up):
+    tiles = []
+    for k in range(0, NY, ROWS):
+        d, u = down[k : k + ROWS], up[k : k + ROWS]
+        tiles.append(jnp.where(top(d), d, pltpu.roll(u, HALF, 0)))
+        tiles.append(jnp.where(top(d), pltpu.roll(d, HALF, 0), u))
+    return tiles
+
+
+def from_tiles(tiles):
+    down, up = [], []
+    for first, second in zip(tiles[::2], tiles[1::2]):
+        down.append(jnp.where(top(first), first, pltpu.roll(second, HALF, 0)))
+        up.append(jnp.where(top(first), pltpu.roll(first, HALF, 0), second))
+    return jnp.concatenate(down, axis=0), jnp.concatenate(up, axis=0)
 
 
 def get_enters(enter_ref, group, groups):
-    found = []
-    for way in range(2):
-        halves = [
-            enter_ref[(way * (NY // ROWS) + half) * groups + group]
-            for half in range(NY // ROWS)
-        ]
-        found.append(jnp.concatenate(halves, axis=0))
-    return found
+    return from_tiles([enter_ref[k * groups + group, :ROWS] for k in range(NY // HALF)])
 
 
 def depth_tiles(absorber):
-    total = sum(layers(absorber))
-    high = total.astype(jnp.bfloat16).astype(jnp.float32)
-    middle = (total - high).astype(jnp.bfloat16).astype(jnp.float32)
-    low = total - high - middle
     lane = lax.broadcasted_iota(jnp.int32, (NY, LANES), 1)
-    spread = jnp.where(lane == 0, high, jnp.where(lane == 1, middle, jnp.where(lane == 2, low, 0.0)))
-    return [spread[half * ROWS : (half + 1) * ROWS] for half in range(NY // ROWS)]
+    by_layer = layers(absorber)
+    count = len(by_layer)
+    forward = reverse = jnp.zeros((NY, LANES), jnp.float32)
+    for k, value in enumerate(by_layer):
+        high = value.astype(jnp.bfloat16).astype(jnp.float32)
+        middle = (value - high).astype(jnp.bfloat16).astype(jnp.float32)
+        for j, part in enumerate((high, middle, value - high - middle)):
+            forward = jnp.where(lane == PARTS * k + j, part, forward)
+            reverse = jnp.where(lane == PARTS * (count - 1 - k) + j, part, reverse)
+    return to_tiles(forward, reverse)
 
 
 def absorbed_of(passed, emitted, enter_down, enter_up):
@@ -69,11 +79,11 @@
     downward, upward = [None] * count, [None] * count
     running = enter_down
     for k in range(count):
-        running = passed[k] * running + emitted[k]
+        running = emitted[k] if running is None else passed[k] * running + emitted[k]
         downward[k] = running
     running = enter_up
     for k in reversed(range(count)):
-        running = passed[k] * running + emitted[k]
+        running = emitted[k] if running is None else passed[k] * running + emitted[k]
         upward[k] = running
     return [
         (1.0 - t) * (d + u - 2.0 * e) for t, d, u, e in zip(passed, downward, upward, emitted)
@@ -116,34 +126,63 @@
         last_ref[:, at] = q[-NY:]
         passed = layers(jnp.exp(-(absorber * cross_ref[:, at])))
         emitted = layers(p * emission_ref[:, at])
-        put_exits(exit_ref, g, groups, *exits(passed, emitted), depths)
-
-
-def scan(exits_in, pass_ref, enter_ref, way):
+        for k, (tile, depth) in enumerate(zip(to_tiles(*exits(passed, emitted)), depths)):
+            exit_ref[k * groups + g] = jnp.concatenate([tile, depth], axis=0).astype(jnp.bfloat16)
+
+
+def scan(exit_of, pass_ref, enter_ref):
     count = enter_ref.shape[0]
-
-    def step(i, carry):
-        at = jnp.where(way == 0, i, count - 1 - i)
-        enter_ref[at] = carry
-        return pass_ref[at] * carry + exits_in(at)
-
-    lax.fori_loop(0, count, step, jnp.zeros(enter_ref.shape[1:], jnp.float32), unroll=8)
+    carry = jnp.zeros(enter_ref.shape[1:], jnp.float32)
+    upper = top(carry)
+    for i in range(count):
+        j = count - 1 - i
+        enter_ref[i, :HALF] = carry[:HALF]
+        enter_ref[j, HALF:] = carry[HALF:]
+        carry = jnp.where(upper, pass_ref[i], pass_ref[j]) * carry + jnp.where(
+            upper, exit_of(i), exit_of(j)
+        )
 
 
 def first_scan_kernel(axis, arrived_ref, cross_ref, enter_ref, pass_ref, exit_ref):
-    groups = cross_ref.shape[0]
-    me = lax.axis_index(axis)
-    cross = cross_ref[pl.ds(lax.rem(me, groups), 1), :]
+    group = lax.rem(lax.axis_index(axis), cross_ref.shape[0])
+    cross = cross_ref[pl.ds(group, 1), :]
     for s in range(arrived_ref.shape[0]):
         arrived = arrived_ref[s].astype(jnp.float32)
         exit_ref[s] = arrived[:ROWS]
         depth = jnp.sum(arrived[ROWS:], axis=1, keepdims=True)
         pass_ref[s] = jnp.exp(-(depth * cross))
-    scan(lambda at: exit_ref[at], pass_ref, enter_ref, me // (groups * (NY // ROWS)))
-
-
-def second_scan_kernel(axis, groups, exit_ref, pass_ref, enter_ref):
-    scan(lambda at: exit_ref[at], pass_ref, enter_ref, lax.axis_index(axis) // (groups * (NY // ROWS)))
+    scan(lambda at: exit_ref[at], pass_ref, enter_ref)
+
+
+def response_kernel(axis, count, arrived_ref, cross_ref, emission_ref, same_ref, other_ref):
+    group = lax.rem(lax.axis_index(axis), cross_ref.shape[0])
+    cross = cross_ref[pl.ds(group, 1), :]
+    emission = time_step * emission_ref[pl.ds(group, 1), :]
+    lane = lax.broadcasted_iota(jnp.int32, (ROWS, LANES), 1)
+    mine = [(lane >= PARTS * k) & (lane < PARTS * (k + 1)) for k in range(count)]
+    for s in range(arrived_ref.shape[0]):
+        depths = arrived_ref[s].astype(jnp.float32)[ROWS:]
+        after = jnp.ones((ROWS, LANES), jnp.float32)
+        taken = other = jnp.zeros((ROWS, LANES), jnp.float32)
+        for k in reversed(range(count)):
+            depth = jnp.sum(jnp.where(mine[k], depths, 0.0), axis=1, keepdims=True)
+            t = jnp.exp(-(depth * cross))
+            taken = taken + (1.0 - t)
+            other = other + (after * after) * (t * (1.0 - t))
+            after = after * t
+        same_ref[s] = emission * (after * taken)
+        other_ref[s] = emission * other
+
+
+def second_scan_kernel(arrived_ref, entered_ref, pass_ref, same_ref, other_ref, enter_ref, exit_ref):
+    for s in range(arrived_ref.shape[0]):
+        entered = entered_ref[s]
+        exit_ref[s] = (
+            arrived_ref[s, ROWS:]
+            + same_ref[s] * entered
+            + other_ref[s] * pltpu.roll(entered, HALF, 0)
+        )
+    scan(lambda at: exit_ref[at], pass_ref, enter_ref)
 
 
 def rate_kernel(axis, pattern_ref, *refs):
@@ -193,7 +232,8 @@
         emission = emission_ref[:, at]
         emitted = [value * emission for value in p]
         passed = layers(jnp.exp(-(absorber * cross_ref[:, at])))
-        absorbed = absorbed_of(passed, emitted, *get_enters(enter_ref, g, groups))
+        entering = get_enters(enter_ref, g, groups) if final else (None, None)
+        absorbed = absorbed_of(passed, emitted, *entering)
         boundary = jnp.where(inlet, inflow_ref[:, at], arrived_ref[:, at].astype(jnp.float32))
         carried = advection(p, boundary, along_x, forward_y, backward_y)
         rates = layers(rate_ref[:, at])
@@ -206,14 +246,39 @@
                 updated_ref[here, at] = 0.5 * (start[k] + p[k] + time_step * rate)
                 absorption_ref[here, at] = absorbed[k]
         else:
-            middle_ref, q_ref, last_ref, exit_ref = refs[10:]
+            middle_ref, swap_ref = refs[10:]
             middle = [value + time_step * rate for value, rate in zip(p, tendency)]
             for k, value in enumerate(middle):
-                here = slice(k * NY, (k + 1) * NY)
-                middle_ref[here, at] = value
-                q_ref[here, at] = value.astype(jnp.bfloat16)
-            last_ref[:, at] = middle[-1].astype(jnp.bfloat16)
-            put_exits(exit_ref, g, groups, *exits(passed, [value * emission for value in middle]))
+                middle_ref[k * NY : (k + 1) * NY, at] = value
+            leaving = to_tiles(*exits(passed, [value * emission for value in middle]))
+            for k, tile in enumerate(leaving):
+                swap_ref[k * groups + g, :ROWS] = enter_ref[k * groups + g]
+                swap_ref[k * groups + g, ROWS:] = tile
+
+
+def middle_kernel(part_ref, swap_ref, cross_ref, absorber_ref, middle_ref, q_ref, last_ref):
+    absorber = column(absorber_ref[...])
+    groups = part_ref.shape[1] // LANES
+    for g in range(groups):
+        at = slice(g * LANES, (g + 1) * LANES)
+        part = layers(part_ref[:, at])
+        passed = layers(jnp.exp(-(absorber * cross_ref[:, at])))
+        downward, upward = get_enters(swap_ref, g, groups)
+        count = len(passed)
+        down, up = [None] * count, [None] * count
+        for k in range(count):
+            downward = passed[k] * downward
+            down[k] = downward
+        for k in reversed(range(count)):
+            upward = passed[k] * upward
+            up[k] = upward
+        for k in range(count):
+            here = slice(k * NY, (k + 1) * NY)
+            value = part[k] + time_step * ((1.0 - passed[k]) * (down[k] + up[k]))
+            middle_ref[here, at] = value
+            q_ref[here, at] = value.astype(jnp.bfloat16)
+            if k == count - 1:
+                last_ref[:, at] = value.astype(jnp.bfloat16)
 
 
 def vmem(count):
@@ -306,25 +371,39 @@
     )
     pieces = gathered(q, "lev")
     arrived = shifted(last, "cell")
-    entering, passes = call(
+    sent = swap(leaving)
+    entered, passes = call(
         functools.partial(first_scan_kernel, "cell"),
-        (swap(leaving), crosses),
+        (sent, crosses),
         (tiles, tiles),
         size,
         [pltpu.VMEM(tiles.shape, jnp.float32)],
     )
-    entering = swap(entering)
     rates = rate_term(pieces, rate_blocks, pattern, bracket)
-    middle, q, last, leaving = call(
+    same, other = call(
+        functools.partial(response_kernel, "cell", cells // NY),
+        (sent, crosses, emission.reshape(crosses.shape)),
+        (tiles, tiles),
+        size,
+    )
+    part, leaving = call(
         functools.partial(step_kernel, False, "cell"),
-        (populations, rates, entering, arrived, inflow, cross, emission, absorber, stream, crossways),
-        (field, rounded, layer, tiles),
+        (populations, rates, entered, arrived, inflow, cross, emission, absorber, stream, crossways),
+        (field, jax.ShapeDtypeStruct((strips, 2 * ROWS, LANES), jnp.float32)),
         5 * size,
+    )
+    swapped = swap(leaving)
+    middle, q, last = call(
+        middle_kernel, (part, swapped, cross, absorber), (field, rounded, layer), 3 * size
     )
     pieces = gathered(q, "lev")
     arrived = shifted(last, "cell")
     (entering,) = call(
-        functools.partial(second_scan_kernel, "cell", levels // LANES), (swap(leaving), passes), (tiles,), size
+        second_scan_kernel,
+        (swapped, entered, passes, same, other),
+        (tiles,),
+        size,
+        [pltpu.VMEM(tiles.shape, jnp.float32)],
     )
     entering = swap(entering)
     rates = rate_term(pieces, rate_blocks, pattern, bracket)

time: 94.2 us -> 85.2 us (0.904)
  blocking collectives: 0 us -> 22 us
  starting transfers between devices: 49.3 us -> 31.7 us
  waiting for transfers between devices: 20.4 us -> 8.11 us
    all_to_all x0 -> x1, blocking collectives: none -> 22 us  [swap(): return lax.all_to_all(value, 'cell', 0, 0, tiled=True)]
    all_to_all x4 -> x2, starting transfers between devices: 35.5 us -> 18.6 us  [swap(): return lax.all_to_all(value, 'cell', 0, 0, tiled=True)]
    all_to_all x4 -> x2, waiting for transfers between devices: 20.3 us -> 8.09 us  [swap(): return lax.all_to_all(value, 'cell', 0, 0, tiled=True)]
    pallas_call x5 -> x7, Pallas kernels: 5.97 us -> 5.28 us  [call(): pl.pallas_call(body, out_shape=outs, in_specs=in_specs or vmem(len(args))...]
  transfers between devices with their start and end apart: 12 -> 10, of which waited for: 4 -> 2; matrix products, arithmetic and copies ran while one was open for 1% -> 1% of each run, Pallas kernels for 8% -> 8%
where the time goes in v4:
time: 85.2 us; the launch traced here: 84.2 us
  starting transfers between devices  31.7 us (37%)
  blocking collectives  22 us (26%)
  local copies, waits for them, and re-layouts  10.8 us (13%)
  Pallas kernels  10.7 us (13%)
  waiting for transfers between devices  8.11 us (10%)
  between operations  0.9 us (1%)
    all_to_all x1, blocking collectives, swap(): return lax.all_to_all(value, 'cell', 0, 0, tiled=True)  22 us
    all_to_all x2, starting transfers between devices, swap(): return lax.all_to_all(value, 'cell', 0, 0, tiled=True)  18.6 us
    unnamed x33, local copies, waits for them, and re-layouts  10.8 us
    all_to_all x2, waiting for transfers between devices, swap(): return lax.all_to_all(value, 'cell', 0, 0, tiled=True)  8.09 us
    ppermute x2, starting transfers between devices, shifted(): return lax.ppermute(value, axis, [(i, i + 1) for i in range(peers - 1)])  6.72 us
    ppermute x6, starting transfers between devices, swap(): lax.ppermute(value, axis, [(i, i ^ apart) for i in range(lax.axis_size(ax...  6.37 us
    pallas_call x2, Pallas kernels, rate_term(): pl.pallas_call(functools.partial(rate_kernel, 'lev'), in_specs=[pl.BlockS...  5.45 us
    pallas_call x7, Pallas kernels, call(): pl.pallas_call(body, out_shape=outs, in_specs=in_specs or vmem(len(args))...  5.28 us
  transfers between devices with their start and end apart: 10, of which 2 were waited for; matrix products, arithmetic and copies ran while one was open for 1% of the time, Pallas kernels for 8%

profile of v4, /device:TPU:2, one launch (start us, length us, event | category | flops | bytes accessed | tf_op | source)
XLA Modules:
  0.0 84.2 jit_solution(326103394015304568)
XLA Ops:
  0.7 1.1 %copy-done.2 = f32[64,2048]{1,0:T(8,128)S(1)} copy-done((f32[64,2048]{1,0:T(8,128)S(1)}, f32[64,2048]{1,0:T(8,128)}, u32[]{:S(2)}) %copy-start.2) | copy-done | bytes 524312
  1.7 0.7 copy-done.5
  2.4 0.7 copy-done.8
  3.1 0.7 copy-done.10
  3.8 1.1 %shard_map.113 = (bf16[64,2048]{1,0:T(8,128)(2,1)S(1)}, bf16[16,2048]{1,0:T(8,128)(2,1)S(1)}, bf16[64,16,128]{2,1,0:T(8,128)(2,1)}) custom-call(f32[64,2048]{1,0:T(8,128)S(1)} %copy-done.2, f32[1,2048]{1,0:T(1,128)S(1)} %bitcast.8, f32[1,2048]{1,0:T(1,128)S(1)} %bitcast.14, f32[1,64]{1,0:T(1,128)S(1)} %bitcast.18), custom_call_target="tpu_custom_call" | custom-call | flops 1572864 | bytes 1572864 | tf_op jit(solution)/shard_map/pallas_call | solution.py:292
  4.9 3.3 %collective-permute-start.1 = (bf16[64,2048]{1,0:T(8,128)(2,1)S(1)}, bf16[64,2048]{1,0:T(8,128)(2,1)S(1)}, u32[]{:S(2)}, u32[]{:S(2)}) collective-permute-start(bf16[64,2048]{1,0:T(8,128)(2,1)S(1)} %get-tuple-element.14.refs_0_), channel_id=1, source_target_pairs={{0,2},{1,3},{2,0},{3,1},{4,6},{5,7},{6,4},{7,5},{8,10},{9,11},{10,... | collective-permute-start | bytes 786440 | tf_op jit(solution)/shard_map/ppermute | solution.py:305
  8.2 12.1 %all-to-all-start = ((bf16[64,16,128]{2,1,0:T(8,128)(2,1)}), bf16[64,16,128]{2,1,0:T(8,128)(2,1)S(1)}, u32[]{:S(2)}, u32[]{:S(2)}) async-start(bf16[64,16,128]{2,1,0:T(8,128)(2,1)} %get-tuple-element.15), calls=%async_computation | async-start | bytes 524288 | tf_op jit(solution)/shard_map/all_to_all | solution.py:360
  20.9 3.4 %collective-permute-start.3 = (bf16[16,2048]{1,0:T(8,128)(2,1)S(1)}, bf16[16,2048]{1,0:T(8,128)(2,1)S(1)}, u32[]{:S(2)}, u32[]{:S(2)}) collective-permute-start(bf16[16,2048]{1,0:T(8,128)(2,1)S(1)} %get-tuple-element.17), channel_id=1, source_target_pairs={{0,4},{4,8},{8,12},{12,16},{16,20},{20,24},{24,28},{28,32},{32,36}... | collective-permute-start | bytes 196616 | tf_op jit(solution)/shard_map/ppermute | solution.py:328
  24.3 0.8 copy.12.pattern_ref
  25.0 6.9 %all-to-all-done.arrived_ref = bf16[64,16,128]{2,1,0:T(8,128)(2,1)S(1)} async-done(((bf16[64,16,128]{2,1,0:T(8,128)(2,1)}), bf16[64,16,128]{2,1,0:T(8,128)(2,1)S(1)}, u32[]{:S(2)}, u32[]{:S(2)}) %all-to-all-start) | async-done | bytes 262176 | tf_op jit(solution)/shard_map/all_to_all | solution.py:360
  32.0 0.7 copy-done.6
  32.9 2.8 %copy-done = bf16[2,16,6,128,128]{4,3,2,1,0:T(8,128)(2,1)S(1)} copy-done((bf16[2,16,6,128,128]{4,3,2,1,0:T(8,128)(2,1)S(1)}, bf16[2,16,6,128,128]{4,3,2,1,0:T(8,128)(2,1)}, u32[]{:S(2)}) %copy-start) | copy-done | bytes 6291480
  35.7 0.7 copy-done.12
  36.3 2.7 %shard_map.114.refs_1_ = f32[64,2048]{1,0:T(8,128)S(1)} custom-call(s32[16,6]{1,0:T(8,128)S(1)} %copy.12.pattern_ref, bf16[64,2048]{1,0:T(8,128)(2,1)S(1)} %get-tuple-element.14.refs_0_, bf16[64,2048]{1,0:T(8,128)(2,1)S(1)} %collective-permute-done.refs_1_, bf16[64,2048]{1,0:T(8,128)(2,1)S(1)} %collective-permute-done.1.refs_2_, ...), custom_call_target="tpu_custom_call" | custom-call | flops 402653184 | bytes 6291456 | tf_op jit(solution)/shard_map/pallas_call | solution.py:313
  39.2 0.7 shard_map.116
  39.9 22.0 %all_to_all.15.swap_ref.arrived_ref = f32[64,16,128]{2,1,0:T(8,128)S(1)} all-to-all(f32[64,16,128]{2,1,0:T(8,128)S(1)} %get-tuple-element.19), channel_id=1, replica_groups=mesh['cell'=64,'lev'=4] {'cell'}, dimensions={0} | all-to-all | bytes 1048576 | tf_op jit(solution)/shard_map/all_to_all | solution.py:360
  62.2 1.9 %collective-permute-start.5 = (bf16[64,2048]{1,0:T(8,128)(2,1)S(1)}, bf16[64,2048]{1,0:T(8,128)(2,1)S(1)}, u32[]{:S(2)}, u32[]{:S(2)}) collective-permute-start(bf16[64,2048]{1,0:T(8,128)(2,1)S(1)} %get-tuple-element.21.refs_0_), channel_id=1, source_target_pairs={{0,2},{1,3},{2,0},{3,1},{4,6},{5,7},{6,4},{7,5},{8,10},{9,11},{10,... | collective-permute-start | bytes 786440 | tf_op jit(solution)/shard_map/ppermute | solution.py:305
  64.6 0.9 %shard_map.120 = f32[64,8,128]{2,1,0:T(8,128)} custom-call(f32[64,16,128]{2,1,0:T(8,128)S(1)} %all_to_all.15.swap_ref.arrived_ref, f32[64,8,128]{2,1,0:T(8,128)S(1)} %get-tuple-element.16.refs_2_.entered_ref, f32[64,8,128]{2,1,0:T(8,128)S(1)} %get-tuple-element.22.pass_ref, f32[64,8,128]{2,1,0:T(8,128)S(1)} %get-tuple-element.23.same_ref, ...), custom_call_target="tpu_custom_call" | custom-call | flops 524288 | bytes 524288 | tf_op jit(solution)/shard_map/pallas_call | solution.py:292
  65.4 6.5 %all-to-all-start.2 = ((f32[64,8,128]{2,1,0:T(8,128)}), f32[64,8,128]{2,1,0:T(8,128)S(1)}, u32[]{:S(2)}, u32[]{:S(2)}) async-start(f32[64,8,128]{2,1,0:T(8,128)} %shard_map.120), calls=%async_computation.2 | async-start | bytes 524288 | tf_op jit(solution)/shard_map/all_to_all | solution.py:360
  72.5 3.4 %collective-permute-start.7 = (bf16[16,2048]{1,0:T(8,128)(2,1)S(1)}, bf16[16,2048]{1,0:T(8,128)(2,1)S(1)}, u32[]{:S(2)}, u32[]{:S(2)}) collective-permute-start(bf16[16,2048]{1,0:T(8,128)(2,1)S(1)} %get-tuple-element.25), channel_id=1, source_target_pairs={{0,4},{4,8},{8,12},{12,16},{16,20},{20,24},{24,28},{28,32},{32,36}... | collective-permute-start | bytes 196616 | tf_op jit(solution)/shard_map/ppermute | solution.py:328
  75.9 2.8 %copy-done.1 = bf16[2,16,6,128,128]{4,3,2,1,0:T(8,128)(2,1)S(1)} copy-done((bf16[2,16,6,128,128]{4,3,2,1,0:T(8,128)(2,1)S(1)}, bf16[2,16,6,128,128]{4,3,2,1,0:T(8,128)(2,1)}, u32[]{:S(2)}) %copy-start.1) | copy-done | bytes 6291480
  78.7 2.7 %shard_map.118.refs_1_ = f32[64,2048]{1,0:T(8,128)S(1)} custom-call(s32[16,6]{1,0:T(8,128)S(1)} %copy.12.pattern_ref, bf16[64,2048]{1,0:T(8,128)(2,1)S(1)} %get-tuple-element.21.refs_0_, bf16[64,2048]{1,0:T(8,128)(2,1)S(1)} %collective-permute-done.4.refs_1_, bf16[64,2048]{1,0:T(8,128)(2,1)S(1)} %collective-permute-done.5.refs_2_, ...), custom_call_target="tpu_custom_call" | custom-call | flops 402653184 | bytes 6291456 | tf_op jit(solution)/shard_map/pallas_call | solution.py:313
  81.5 1.2 %all-to-all-done.2.refs_2_ = f32[64,8,128]{2,1,0:T(8,128)S(1)} async-done(((f32[64,8,128]{2,1,0:T(8,128)}), f32[64,8,128]{2,1,0:T(8,128)S(1)}, u32[]{:S(2)}, u32[]{:S(2)}) %all-to-all-start.2) | async-done | bytes 262176 | tf_op jit(solution)/shard_map/all_to_all | solution.py:360
  82.6 1.6 %shard_map.121 = (f32[64,2048]{1,0:T(8,128)}, f32[64,2048]{1,0:T(8,128)}) custom-call(f32[64,2048]{1,0:T(8,128)S(1)} %get-tuple-element.20.refs_0_, f32[64,2048]{1,0:T(8,128)S(1)} %shard_map.118.refs_1_, f32[64,8,128]{2,1,0:T(8,128)S(1)} %all-to-all-done.2.refs_2_, bf16[16,2048]{1,0:T(8,128)(2,1)S(1)} %collective-permute-done.7.refs_3_, ...), custom_call_target="tpu_custom_call" | custom-call | flops 2621440 | bytes 2621440 | tf_op jit(solution)/shard_map/pallas_call | solution.py:292
  (39 shorter events, 2.2 us)
Async XLA Ops:
  0.6 38.5 %copy-start.11 = (f32[64]{0:T(128)S(1)}, f32[64]{0:T(128)}, u32[]{:S(2)}) copy-start(f32[64]{0:T(128)} %param.16) | copy-start | bytes 772
  0.6 38.5 %copy-start.14 = (f32[64]{0:T(128)S(1)}, f32[64]{0:T(128)}, u32[]{:S(2)}) copy-start(f32[64]{0:T(128)} %param.17) | copy-start | bytes 772
  0.7 38.5 %copy-start.15 = (f32[64]{0:T(128)S(1)}, f32[64]{0:T(128)}, u32[]{:S(2)}) copy-start(f32[64]{0:T(128)} %param.18) | copy-start | bytes 772
  0.7 1.1 %copy-start.2 = (f32[64,2048]{1,0:T(8,128)S(1)}, f32[64,2048]{1,0:T(8,128)}, u32[]{:S(2)}) copy-start(f32[64,2048]{1,0:T(8,128)} %refs_10_.1) | copy-start | bytes 1572868
  1.7 0.7 copy-start.5
  2.4 0.7 copy-start.8
  3.8 35.3 %copy-start.3 = (f32[64,2048]{1,0:T(8,128)S(1)}, f32[64,2048]{1,0:T(8,128)}, u32[]{:S(2)}) copy-start(f32[64,2048]{1,0:T(8,128)} %refs_10_.1) | copy-start | bytes 1572868
  3.8 35.4 %copy-start.4 = (f32[16,2048]{1,0:T(8,128)S(1)}, f32[16,2048]{1,0:T(8,128)}, u32[]{:S(2)}) copy-start(f32[16,2048]{1,0:T(8,128)} %refs_4_.7) | copy-start | bytes 393220
  3.8 35.4 %copy-start.7 = (f32[2048]{0:T(1024)S(1)}, f32[2048]{0:T(1024)}, u32[]{:S(2)}) copy-start(f32[2048]{0:T(1024)} %param.14) | copy-start | bytes 24580
  3.8 35.4 %copy-start.9 = (f32[2048]{0:T(1024)S(1)}, f32[2048]{0:T(1024)}, u32[]{:S(2)}) copy-start(f32[2048]{0:T(1024)} %param.15) | copy-start | bytes 24580
  4.9 15.5 %collective-permute-start.1 = (bf16[64,2048]{1,0:T(8,128)(2,1)S(1)}, bf16[64,2048]{1,0:T(8,128)(2,1)S(1)}, u32[]{:S(2)}, u32[]{:S(2)}) collective-permute-start(bf16[64,2048]{1,0:T(8,128)(2,1)S(1)} %get-tuple-element.14.refs_0_), channel_id=1, source_target_pairs={{0,2},{1,3},{2,0},{3,1},{4,6},{5,7},{6,4},{7,5},{8,10},{9,11},{10,... | collective-permute-start | bytes 786440 | tf_op jit(solution)/shard_map/ppermute | solution.py:305
  8.2 23.8 %all-to-all-start = ((bf16[64,16,128]{2,1,0:T(8,128)(2,1)}), bf16[64,16,128]{2,1,0:T(8,128)(2,1)S(1)}, u32[]{:S(2)}, u32[]{:S(2)}) async-start(bf16[64,16,128]{2,1,0:T(8,128)(2,1)} %get-tuple-element.15), calls=%async_computation | async-start | bytes 524288 | tf_op jit(solution)/shard_map/all_to_all | solution.py:360
  20.3 12.6 %collective-permute-start = (bf16[64,2048]{1,0:T(8,128)(2,1)S(1)}, bf16[64,2048]{1,0:T(8,128)(2,1)S(1)}, u32[]{:S(2)}, u32[]{:S(2)}) collective-permute-start(bf16[64,2048]{1,0:T(8,128)(2,1)S(1)} %get-tuple-element.14.refs_0_), channel_id=1, source_target_pairs={{0,1},{1,0},{2,3},{3,2},{4,5},{5,4},{6,7},{7,6},{8,9},{9,8},{10,11... | collective-permute-start | bytes 786440 | tf_op jit(solution)/shard_map/ppermute | solution.py:305
  20.4 12.5 %collective-permute-start.2 = (bf16[64,2048]{1,0:T(8,128)(2,1)S(1)}, bf16[64,2048]{1,0:T(8,128)(2,1)S(1)}, u32[]{:S(2)}, u32[]{:S(2)}) collective-permute-start(bf16[64,2048]{1,0:T(8,128)(2,1)S(1)} %collective-permute-done.1.refs_2_), channel_id=1, source_target_pairs={{0,1},{1,0},{2,3},{3,2},{4,5},{5,4},{6,7},{7,6},{8,9},{9,8},{10,11... | collective-permute-start | bytes 786440 | tf_op jit(solution)/shard_map/ppermute | solution.py:305
  20.9 18.2 %collective-permute-start.3 = (bf16[16,2048]{1,0:T(8,128)(2,1)S(1)}, bf16[16,2048]{1,0:T(8,128)(2,1)S(1)}, u32[]{:S(2)}, u32[]{:S(2)}) collective-permute-start(bf16[16,2048]{1,0:T(8,128)(2,1)S(1)} %get-tuple-element.17), channel_id=1, source_target_pairs={{0,4},{4,8},{8,12},{12,16},{16,20},{20,24},{24,28},{28,32},{32,36}... | collective-permute-start | bytes 196616 | tf_op jit(solution)/shard_map/ppermute | solution.py:328
  32.0 0.7 copy-start.6
  32.9 2.8 %copy-start = (bf16[2,16,6,128,128]{4,3,2,1,0:T(8,128)(2,1)S(1)}, bf16[2,16,6,128,128]{4,3,2,1,0:T(8,128)(2,1)}, u32[]{:S(2)}) copy-start(bf16[2,16,6,128,128]{4,3,2,1,0:T(8,128)(2,1)} %refs_4_.6) | copy-start | bytes 18874372
  36.3 39.6 %copy-start.13 = (s32[64]{0:T(128)S(1)}, s32[64]{0:T(128)}, u32[]{:S(2)}) copy-start(s32[64]{0:T(128)} %param.13) | copy-start | bytes 772
  62.2 9.9 %collective-permute-start.5 = (bf16[64,2048]{1,0:T(8,128)(2,1)S(1)}, bf16[64,2048]{1,0:T(8,128)(2,1)S(1)}, u32[]{:S(2)}, u32[]{:S(2)}) collective-permute-start(bf16[64,2048]{1,0:T(8,128)(2,1)S(1)} %get-tuple-element.21.refs_0_), channel_id=1, source_target_pairs={{0,2},{1,3},{2,0},{3,1},{4,6},{5,7},{6,4},{7,5},{8,10},{9,11},{10,... | collective-permute-start | bytes 786440 | tf_op jit(solution)/shard_map/ppermute | solution.py:305
  65.4 17.2 %all-to-all-start.2 = ((f32[64,8,128]{2,1,0:T(8,128)}), f32[64,8,128]{2,1,0:T(8,128)S(1)}, u32[]{:S(2)}, u32[]{:S(2)}) async-start(f32[64,8,128]{2,1,0:T(8,128)} %shard_map.120), calls=%async_computation.2 | async-start | bytes 524288 | tf_op jit(solution)/shard_map/all_to_all | solution.py:360
  71.9 4.0 %collective-permute-start.4 = (bf16[64,2048]{1,0:T(8,128)(2,1)S(1)}, bf16[64,2048]{1,0:T(8,128)(2,1)S(1)}, u32[]{:S(2)}, u32[]{:S(2)}) collective-permute-start(bf16[64,2048]{1,0:T(8,128)(2,1)S(1)} %get-tuple-element.21.refs_0_), channel_id=1, source_target_pairs={{0,1},{1,0},{2,3},{3,2},{4,5},{5,4},{6,7},{7,6},{8,9},{9,8},{10,11... | collective-permute-start | bytes 786440 | tf_op jit(solution)/shard_map/ppermute | solution.py:305
  72.0 3.9 %collective-permute-start.6 = (bf16[64,2048]{1,0:T(8,128)(2,1)S(1)}, bf16[64,2048]{1,0:T(8,128)(2,1)S(1)}, u32[]{:S(2)}, u32[]{:S(2)}) collective-permute-start(bf16[64,2048]{1,0:T(8,128)(2,1)S(1)} %collective-permute-done.5.refs_2_), channel_id=1, source_target_pairs={{0,1},{1,0},{2,3},{3,2},{4,5},{5,4},{6,7},{7,6},{8,9},{9,8},{10,11... | collective-permute-start | bytes 786440 | tf_op jit(solution)/shard_map/ppermute | solution.py:305
  72.5 8.9 %collective-permute-start.7 = (bf16[16,2048]{1,0:T(8,128)(2,1)S(1)}, bf16[16,2048]{1,0:T(8,128)(2,1)S(1)}, u32[]{:S(2)}, u32[]{:S(2)}) collective-permute-start(bf16[16,2048]{1,0:T(8,128)(2,1)S(1)} %get-tuple-element.25), channel_id=1, source_target_pairs={{0,4},{4,8},{8,12},{12,16},{16,20},{20,24},{24,28},{28,32},{32,36}... | collective-permute-start | bytes 196616 | tf_op jit(solution)/shard_map/ppermute | solution.py:328
  75.9 2.8 %copy-start.1 = (bf16[2,16,6,128,128]{4,3,2,1,0:T(8,128)(2,1)S(1)}, bf16[2,16,6,128,128]{4,3,2,1,0:T(8,128)(2,1)}, u32[]{:S(2)}) copy-start(bf16[2,16,6,128,128]{4,3,2,1,0:T(8,128)(2,1)} %refs_4_.6) | copy-start | bytes 18874372
  (2 other events, 1.3 us)

commit v5 on v4

--- a/solution.py
+++ b/solution.py
@@ -11,7 +11,8 @@
 LANES = 128
 ROWS = 8
 HALF = 4
-PARTS = 3
+PARTS = 2
+FIRST = 63
 time_step = 0.25
 
 
@@ -67,8 +68,7 @@
     forward = reverse = jnp.zeros((NY, LANES), jnp.float32)
     for k, value in enumerate(by_layer):
         high = value.astype(jnp.bfloat16).astype(jnp.float32)
-        middle = (value - high).astype(jnp.bfloat16).astype(jnp.float32)
-        for j, part in enumerate((high, middle, value - high - middle)):
+        for j, part in enumerate((high, value - high)):
             forward = jnp.where(lane == PARTS * k + j, part, forward)
             reverse = jnp.where(lane == PARTS * (count - 1 - k) + j, part, reverse)
     return to_tiles(forward, reverse)
@@ -100,6 +100,10 @@
         )
         upstream = here
     return result
+
+
+def depth_lanes(count):
+    return lax.broadcasted_iota(jnp.int32, (ROWS, LANES), 1) < PARTS * count
 
 
 def first_kernel(p_hbm, cross_hbm, emission_hbm, absorber_hbm, q_ref, last_ref, exit_ref, *scratch):
@@ -127,7 +131,9 @@
         passed = layers(jnp.exp(-(absorber * cross_ref[:, at])))
         emitted = layers(p * emission_ref[:, at])
         for k, (tile, depth) in enumerate(zip(to_tiles(*exits(passed, emitted)), depths)):
-            exit_ref[k * groups + g] = jnp.concatenate([tile, depth], axis=0).astype(jnp.bfloat16)
+            rest = tile - tile.astype(jnp.bfloat16).astype(jnp.float32)
+            below = jnp.where(depth_lanes(len(passed)), depth, rest)
+            exit_ref[k * groups + g] = jnp.concatenate([tile, below], axis=0).astype(jnp.bfloat16)
 
 
 def scan(exit_of, pass_ref, enter_ref):
@@ -143,13 +149,14 @@
         )
 
 
-def first_scan_kernel(axis, arrived_ref, cross_ref, enter_ref, pass_ref, exit_ref):
+def first_scan_kernel(axis, count, arrived_ref, cross_ref, enter_ref, pass_ref, exit_ref):
     group = lax.rem(lax.axis_index(axis), cross_ref.shape[0])
     cross = cross_ref[pl.ds(group, 1), :]
     for s in range(arrived_ref.shape[0]):
         arrived = arrived_ref[s].astype(jnp.float32)
-        exit_ref[s] = arrived[:ROWS]
-        depth = jnp.sum(arrived[ROWS:], axis=1, keepdims=True)
+        depths = depth_lanes(count)
+        exit_ref[s] = arrived[:ROWS] + jnp.where(depths, 0.0, arrived[ROWS:])
+        depth = jnp.sum(jnp.where(depths, arrived[ROWS:], 0.0), axis=1, keepdims=True)
         pass_ref[s] = jnp.exp(-(depth * cross))
     scan(lambda at: exit_ref[at], pass_ref, enter_ref)
 
@@ -288,14 +295,14 @@
 LIMIT = pltpu.CompilerParams(vmem_limit_bytes=24 * 2**20)
 
 
-def call(body, args, outs, cost, scratch=(), in_specs=None):
+def call(body, args, outs, cost, scratch=(), in_specs=None, params=LIMIT):
     return pl.pallas_call(
         body,
         out_shape=outs,
         in_specs=in_specs or vmem(len(args)),
         out_specs=vmem(len(outs)),
         scratch_shapes=scratch,
-        compiler_params=LIMIT,
+        compiler_params=params,
         cost_estimate=pl.CostEstimate(flops=cost, bytes_accessed=cost, transcendentals=0),
     )(*args)
 
@@ -367,19 +374,21 @@
         3 * size,
         [pltpu.VMEM(value.shape, value.dtype) for value in sources]
         + [pltpu.SemaphoreType.DMA((len(sources),))],
-        [pl.BlockSpec(memory_space=pltpu.HBM)] * len(sources),
+        [pl.BlockSpec(memory_space=pl.ANY)] * len(sources),
+        pltpu.CompilerParams(vmem_limit_bytes=FIRST * 2**20),
     )
     pieces = gathered(q, "lev")
     arrived = shifted(last, "cell")
-    sent = swap(leaving)
+    sent, rates = lax.optimization_barrier(
+        (swap(leaving), rate_term(pieces, rate_blocks, pattern, bracket))
+    )
     entered, passes = call(
-        functools.partial(first_scan_kernel, "cell"),
+        functools.partial(first_scan_kernel, "cell", cells // NY),
         (sent, crosses),
         (tiles, tiles),
         size,
         [pltpu.VMEM(tiles.shape, jnp.float32)],
     )
-    rates = rate_term(pieces, rate_blocks, pattern, bracket)
     same, other = call(
         functools.partial(response_kernel, "cell", cells // NY),
         (sent, crosses, emission.reshape(crosses.shape)),

time: 85.2 us -> 83 us (0.974)
  blocking collectives: 22 us -> 27.8 us
  waiting for transfers between devices: 8.11 us -> 2.35 us
  local copies, waits for them, and re-layouts: 10.8 us -> 7.96 us
  Pallas kernels: 10.7 us -> 11.9 us
    all_to_all x1, blocking collectives: 22 us -> 27.8 us  [swap(): return lax.all_to_all(value, 'cell', 0, 0, tiled=True)]
    all_to_all x2, waiting for transfers between devices: 8.09 us -> 2.33 us  [swap(): return lax.all_to_all(value, 'cell', 0, 0, tiled=True)]
    unnamed x33 -> x23, local copies, waits for them, and re-layouts: 10.8 us -> 7.96 us
    pallas_call x7, Pallas kernels: 5.28 us -> 6.42 us  [call(): pl.pallas_call(body, out_shape=outs, in_specs=in_specs or vmem(len(args))...]
  transfers between devices with their start and end apart: 10 -> 10, of which waited for: 2 -> 1; matrix products, arithmetic and copies ran while one was open for 1% -> 1% of each run, Pallas kernels for 8% -> 8%
where the time goes in v5:
time: 83 us; the launch traced here: 82.5 us
  starting transfers between devices  31.7 us (38%)
  blocking collectives  27.8 us (33%)
  Pallas kernels  11.9 us (14%)
  local copies, waits for them, and re-layouts  7.96 us (10%)
  waiting for transfers between devices  2.35 us (3%)
  between operations  0.9 us (1%)
    all_to_all x1, blocking collectives, swap(): return lax.all_to_all(value, 'cell', 0, 0, tiled=True)  27.8 us
    all_to_all x2, starting transfers between devices, swap(): return lax.all_to_all(value, 'cell', 0, 0, tiled=True)  18.6 us
    unnamed x23, local copies, waits for them, and re-layouts  7.96 us
    ppermute x2, starting transfers between devices, shifted(): return lax.ppermute(value, axis, [(i, i + 1) for i in range(peers - 1)])  6.72 us
    pallas_call x7, Pallas kernels, call(): pl.pallas_call(body, out_shape=outs, in_specs=in_specs or vmem(len(args))...  6.42 us
    ppermute x6, starting transfers between devices, swap(): lax.ppermute(value, axis, [(i, i ^ apart) for i in range(lax.axis_size(ax...  6.38 us
    pallas_call x2, Pallas kernels, rate_term(): pl.pallas_call(functools.partial(rate_kernel, 'lev'), in_specs=[pl.BlockS...  5.46 us
    all_to_all x2, waiting for transfers between devices, swap(): return lax.all_to_all(value, 'cell', 0, 0, tiled=True)  2.33 us
  transfers between devices with their start and end apart: 10, of which 1 were waited for; matrix products, arithmetic and copies ran while one was open for 1% of the time, Pallas kernels for 8%

profile of v5, /device:TPU:2, one launch (start us, length us, event | category | flops | bytes accessed | tf_op | source)
XLA Modules:
  0.0 82.5 jit_solution(9938037756365073282)
XLA Ops:
  0.7 2.2 %shard_map.113 = (bf16[64,2048]{1,0:T(8,128)(2,1)}, bf16[16,2048]{1,0:T(8,128)(2,1)}, bf16[64,16,128]{2,1,0:T(8,128)(2,1)}) custom-call(f32[64,2048]{1,0:T(8,128)} %refs_10_.1, f32[1,2048]{1,0:T(1,128)} %bitcast.8, f32[1,2048]{1,0:T(1,128)} %bitcast.14, f32[1,64]{1,0:T(1,128)} %bitcast.18), custom_call_target="tpu_custom_call" | custom-call | flops 1572864 | bytes 1572864 | tf_op jit(solution)/shard_map/pallas_call | solution.py:299
  2.9 3.3 %collective-permute-start.1 = (bf16[64,2048]{1,0:T(8,128)(2,1)}, bf16[64,2048]{1,0:T(8,128)(2,1)S(1)}, u32[]{:S(2)}, u32[]{:S(2)}) collective-permute-start(bf16[64,2048]{1,0:T(8,128)(2,1)} %get-tuple-element.17.refs_0_), channel_id=1, source_target_pairs={{0,2},{1,3},{2,0},{3,1},{4,6},{5,7},{6,4},{7,5},{8,10},{9,11},{10,... | collective-permute-start | bytes 786440 | tf_op jit(solution)/shard_map/ppermute | solution.py:312
  6.2 12.1 %all-to-all-start = ((bf16[64,16,128]{2,1,0:T(8,128)(2,1)}), bf16[64,16,128]{2,1,0:T(8,128)(2,1)S(1)}, u32[]{:S(2)}, u32[]{:S(2)}) async-start(bf16[64,16,128]{2,1,0:T(8,128)(2,1)} %get-tuple-element.16), calls=%async_computation | async-start | bytes 524288 | tf_op jit(solution)/shard_map/all_to_all | solution.py:367
  18.4 0.5 collective-permute-start.2
  18.9 3.4 %collective-permute-start.3 = (bf16[16,2048]{1,0:T(8,128)(2,1)}, bf16[16,2048]{1,0:T(8,128)(2,1)S(1)}, u32[]{:S(2)}, u32[]{:S(2)}) collective-permute-start(bf16[16,2048]{1,0:T(8,128)(2,1)} %get-tuple-element.21), channel_id=1, source_target_pairs={{0,4},{4,8},{8,12},{12,16},{16,20},{20,24},{24,28},{28,32},{32,36}... | collective-permute-start | bytes 196616 | tf_op jit(solution)/shard_map/ppermute | solution.py:335
  22.3 0.8 copy.12.pattern_ref
  23.1 2.8 %copy-done = bf16[2,16,6,128,128]{4,3,2,1,0:T(8,128)(2,1)S(1)} copy-done((bf16[2,16,6,128,128]{4,3,2,1,0:T(8,128)(2,1)S(1)}, bf16[2,16,6,128,128]{4,3,2,1,0:T(8,128)(2,1)}, u32[]{:S(2)}) %copy-start) | copy-done | bytes 6291480
  25.9 0.9 %copy-done.5 = bf16[64,2048]{1,0:T(8,128)(2,1)S(1)} copy-done((bf16[64,2048]{1,0:T(8,128)(2,1)S(1)}, bf16[64,2048]{1,0:T(8,128)(2,1)}, u32[]{:S(2)}) %copy-start.5) | copy-done | bytes 262168
  26.8 0.7 copy-done.8
  27.5 2.7 %shard_map.114.refs_1_ = f32[64,2048]{1,0:T(8,128)S(1)} custom-call(s32[16,6]{1,0:T(8,128)S(1)} %copy.12.pattern_ref, bf16[64,2048]{1,0:T(8,128)(2,1)S(1)} %copy-done.5, bf16[64,2048]{1,0:T(8,128)(2,1)S(1)} %collective-permute-done.refs_1_, bf16[64,2048]{1,0:T(8,128)(2,1)S(1)} %collective-permute-done.1.refs_2_, ...), custom_call_target="tpu_custom_call" | custom-call | flops 402653184 | bytes 6291456 | tf_op jit(solution)/shard_map/pallas_call | solution.py:320
  30.2 0.2 shard_map.115
  30.5 0.7 shard_map.116
  31.2 27.8 %all_to_all.15.swap_ref.arrived_ref = f32[64,16,128]{2,1,0:T(8,128)S(1)} all-to-all(f32[64,16,128]{2,1,0:T(8,128)S(1)} %get-tuple-element.23), channel_id=1, replica_groups=mesh['cell'=64,'lev'=4] {'cell'}, dimensions={0} | all-to-all | bytes 1048576 | tf_op jit(solution)/shard_map/all_to_all | solution.py:367
  59.0 0.3 shard_map.117
  59.3 1.9 %collective-permute-start.5 = (bf16[64,2048]{1,0:T(8,128)(2,1)S(1)}, bf16[64,2048]{1,0:T(8,128)(2,1)S(1)}, u32[]{:S(2)}, u32[]{:S(2)}) collective-permute-start(bf16[64,2048]{1,0:T(8,128)(2,1)S(1)} %get-tuple-element.25.refs_0_), channel_id=1, source_target_pairs={{0,2},{1,3},{2,0},{3,1},{4,6},{5,7},{6,4},{7,5},{8,10},{9,11},{10,... | collective-permute-start | bytes 786440 | tf_op jit(solution)/shard_map/ppermute | solution.py:312
  61.2 0.5 shard_map.119
  61.7 0.8 %shard_map.120 = f32[64,8,128]{2,1,0:T(8,128)} custom-call(f32[64,16,128]{2,1,0:T(8,128)S(1)} %all_to_all.15.swap_ref.arrived_ref, f32[64,8,128]{2,1,0:T(8,128)S(1)} %get-tuple-element.20.refs_2_.entered_ref, f32[64,8,128]{2,1,0:T(8,128)S(1)} %get-tuple-element.26.pass_ref, f32[64,8,128]{2,1,0:T(8,128)S(1)} %get-tuple-element.27.same_ref, ...), custom_call_target="tpu_custom_call" | custom-call | flops 524288 | bytes 524288 | tf_op jit(solution)/shard_map/pallas_call | solution.py:299
  62.6 6.4 %all-to-all-start.2 = ((f32[64,8,128]{2,1,0:T(8,128)}), f32[64,8,128]{2,1,0:T(8,128)S(1)}, u32[]{:S(2)}, u32[]{:S(2)}) async-start(f32[64,8,128]{2,1,0:T(8,128)} %shard_map.120), calls=%async_computation.2 | async-start | bytes 524288 | tf_op jit(solution)/shard_map/all_to_all | solution.py:367
  69.1 0.5 collective-permute-start.6
  69.6 3.4 %collective-permute-start.7 = (bf16[16,2048]{1,0:T(8,128)(2,1)S(1)}, bf16[16,2048]{1,0:T(8,128)(2,1)S(1)}, u32[]{:S(2)}, u32[]{:S(2)}) collective-permute-start(bf16[16,2048]{1,0:T(8,128)(2,1)S(1)} %get-tuple-element.29), channel_id=1, source_target_pairs={{0,4},{4,8},{8,12},{12,16},{16,20},{20,24},{24,28},{28,32},{32,36}... | collective-permute-start | bytes 196616 | tf_op jit(solution)/shard_map/ppermute | solution.py:335
  73.0 2.8 %copy-done.1 = bf16[2,16,6,128,128]{4,3,2,1,0:T(8,128)(2,1)S(1)} copy-done((bf16[2,16,6,128,128]{4,3,2,1,0:T(8,128)(2,1)S(1)}, bf16[2,16,6,128,128]{4,3,2,1,0:T(8,128)(2,1)}, u32[]{:S(2)}) %copy-start.1) | copy-done | bytes 6291480
  75.8 2.7 %shard_map.118.refs_1_ = f32[64,2048]{1,0:T(8,128)S(1)} custom-call(s32[16,6]{1,0:T(8,128)S(1)} %copy.12.pattern_ref, bf16[64,2048]{1,0:T(8,128)(2,1)S(1)} %get-tuple-element.25.refs_0_, bf16[64,2048]{1,0:T(8,128)(2,1)S(1)} %collective-permute-done.4.refs_1_, bf16[64,2048]{1,0:T(8,128)(2,1)S(1)} %collective-permute-done.5.refs_2_, ...), custom_call_target="tpu_custom_call" | custom-call | flops 402653184 | bytes 6291456 | tf_op jit(solution)/shard_map/pallas_call | solution.py:320
  78.5 2.3 %all-to-all-done.2.refs_2_ = f32[64,8,128]{2,1,0:T(8,128)S(1)} async-done(((f32[64,8,128]{2,1,0:T(8,128)}), f32[64,8,128]{2,1,0:T(8,128)S(1)}, u32[]{:S(2)}, u32[]{:S(2)}) %all-to-all-start.2) | async-done | bytes 262176 | tf_op jit(solution)/shard_map/all_to_all | solution.py:367
  80.9 1.7 %shard_map.121 = (f32[64,2048]{1,0:T(8,128)}, f32[64,2048]{1,0:T(8,128)}) custom-call(f32[64,2048]{1,0:T(8,128)S(1)} %get-tuple-element.24.refs_0_, f32[64,2048]{1,0:T(8,128)S(1)} %shard_map.118.refs_1_, f32[64,8,128]{2,1,0:T(8,128)S(1)} %all-to-all-done.2.refs_2_, bf16[16,2048]{1,0:T(8,128)(2,1)S(1)} %collective-permute-done.7.refs_3_, ...), custom_call_target="tpu_custom_call" | custom-call | flops 2621440 | bytes 2621440 | tf_op jit(solution)/shard_map/pallas_call | solution.py:299
  (29 shorter events, 0.2 us)
Async XLA Ops:
  0.6 29.6 %copy-start.4 = (f32[2048]{0:T(1024)S(1)}, f32[2048]{0:T(1024)}, u32[]{:S(2)}) copy-start(f32[2048]{0:T(1024)} %param.14) | copy-start | bytes 24580
  0.6 29.8 %copy-start.7 = (f32[64]{0:T(128)S(1)}, f32[64]{0:T(128)}, u32[]{:S(2)}) copy-start(f32[64]{0:T(128)} %param.16) | copy-start | bytes 772
  0.7 29.8 %copy-start.6 = (f32[2048]{0:T(1024)S(1)}, f32[2048]{0:T(1024)}, u32[]{:S(2)}) copy-start(f32[2048]{0:T(1024)} %param.15) | copy-start | bytes 24580
  0.7 29.8 %copy-start.2 = (f32[64,2048]{1,0:T(8,128)S(1)}, f32[64,2048]{1,0:T(8,128)}, u32[]{:S(2)}) copy-start(f32[64,2048]{1,0:T(8,128)} %refs_10_.1) | copy-start | bytes 1572868
  0.7 29.8 %copy-start.9 = (f32[64]{0:T(128)S(1)}, f32[64]{0:T(128)}, u32[]{:S(2)}) copy-start(f32[64]{0:T(128)} %param.17) | copy-start | bytes 772
  0.7 29.8 %copy-start.10 = (f32[64]{0:T(128)S(1)}, f32[64]{0:T(128)}, u32[]{:S(2)}) copy-start(f32[64]{0:T(128)} %param.18) | copy-start | bytes 772
  0.7 29.8 %copy-start.3 = (f32[16,2048]{1,0:T(8,128)S(1)}, f32[16,2048]{1,0:T(8,128)}, u32[]{:S(2)}) copy-start(f32[16,2048]{1,0:T(8,128)} %refs_4_.7) | copy-start | bytes 393220
  2.9 15.5 %collective-permute-start.1 = (bf16[64,2048]{1,0:T(8,128)(2,1)}, bf16[64,2048]{1,0:T(8,128)(2,1)S(1)}, u32[]{:S(2)}, u32[]{:S(2)}) collective-permute-start(bf16[64,2048]{1,0:T(8,128)(2,1)} %get-tuple-element.17.refs_0_), channel_id=1, source_target_pairs={{0,2},{1,3},{2,0},{3,1},{4,6},{5,7},{6,4},{7,5},{8,10},{9,11},{10,... | collective-permute-start | bytes 786440 | tf_op jit(solution)/shard_map/ppermute | solution.py:312
  6.2 24.0 %all-to-all-start = ((bf16[64,16,128]{2,1,0:T(8,128)(2,1)}), bf16[64,16,128]{2,1,0:T(8,128)(2,1)S(1)}, u32[]{:S(2)}, u32[]{:S(2)}) async-start(bf16[64,16,128]{2,1,0:T(8,128)(2,1)} %get-tuple-element.16), calls=%async_computation | async-start | bytes 524288 | tf_op jit(solution)/shard_map/all_to_all | solution.py:367
  18.3 4.7 %collective-permute-start = (bf16[64,2048]{1,0:T(8,128)(2,1)}, bf16[64,2048]{1,0:T(8,128)(2,1)S(1)}, u32[]{:S(2)}, u32[]{:S(2)}) collective-permute-start(bf16[64,2048]{1,0:T(8,128)(2,1)} %get-tuple-element.17.refs_0_), channel_id=1, source_target_pairs={{0,1},{1,0},{2,3},{3,2},{4,5},{5,4},{6,7},{7,6},{8,9},{9,8},{10,11... | collective-permute-start | bytes 786440 | tf_op jit(solution)/shard_map/ppermute | solution.py:312
  18.4 4.6 %collective-permute-start.2 = (bf16[64,2048]{1,0:T(8,128)(2,1)S(1)}, bf16[64,2048]{1,0:T(8,128)(2,1)S(1)}, u32[]{:S(2)}, u32[]{:S(2)}) collective-permute-start(bf16[64,2048]{1,0:T(8,128)(2,1)S(1)} %collective-permute-done.1.refs_2_), channel_id=1, source_target_pairs={{0,1},{1,0},{2,3},{3,2},{4,5},{5,4},{6,7},{7,6},{8,9},{9,8},{10,11... | collective-permute-start | bytes 786440 | tf_op jit(solution)/shard_map/ppermute | solution.py:312
  18.9 11.5 %collective-permute-start.3 = (bf16[16,2048]{1,0:T(8,128)(2,1)}, bf16[16,2048]{1,0:T(8,128)(2,1)S(1)}, u32[]{:S(2)}, u32[]{:S(2)}) collective-permute-start(bf16[16,2048]{1,0:T(8,128)(2,1)} %get-tuple-element.21), channel_id=1, source_target_pairs={{0,4},{4,8},{8,12},{12,16},{16,20},{20,24},{24,28},{28,32},{32,36}... | collective-permute-start | bytes 196616 | tf_op jit(solution)/shard_map/ppermute | solution.py:335
  23.1 2.8 %copy-start = (bf16[2,16,6,128,128]{4,3,2,1,0:T(8,128)(2,1)S(1)}, bf16[2,16,6,128,128]{4,3,2,1,0:T(8,128)(2,1)}, u32[]{:S(2)}) copy-start(bf16[2,16,6,128,128]{4,3,2,1,0:T(8,128)(2,1)} %refs_4_.6) | copy-start | bytes 18874372
  25.9 0.9 %copy-start.5 = (bf16[64,2048]{1,0:T(8,128)(2,1)S(1)}, bf16[64,2048]{1,0:T(8,128)(2,1)}, u32[]{:S(2)}) copy-start(bf16[64,2048]{1,0:T(8,128)(2,1)} %get-tuple-element.17.refs_0_) | copy-start | bytes 786436
  26.8 0.7 copy-start.8
  59.3 9.8 %collective-permute-start.5 = (bf16[64,2048]{1,0:T(8,128)(2,1)S(1)}, bf16[64,2048]{1,0:T(8,128)(2,1)S(1)}, u32[]{:S(2)}, u32[]{:S(2)}) collective-permute-start(bf16[64,2048]{1,0:T(8,128)(2,1)S(1)} %get-tuple-element.25.refs_0_), channel_id=1, source_target_pairs={{0,2},{1,3},{2,0},{3,1},{4,6},{5,7},{6,4},{7,5},{8,10},{9,11},{10,... | collective-permute-start | bytes 786440 | tf_op jit(solution)/shard_map/ppermute | solution.py:312
  62.6 18.3 %all-to-all-start.2 = ((f32[64,8,128]{2,1,0:T(8,128)}), f32[64,8,128]{2,1,0:T(8,128)S(1)}, u32[]{:S(2)}, u32[]{:S(2)}) async-start(f32[64,8,128]{2,1,0:T(8,128)} %shard_map.120), calls=%async_computation.2 | async-start | bytes 524288 | tf_op jit(solution)/shard_map/all_to_all | solution.py:367
  69.0 4.0 %collective-permute-start.4 = (bf16[64,2048]{1,0:T(8,128)(2,1)S(1)}, bf16[64,2048]{1,0:T(8,128)(2,1)S(1)}, u32[]{:S(2)}, u32[]{:S(2)}) collective-permute-start(bf16[64,2048]{1,0:T(8,128)(2,1)S(1)} %get-tuple-element.25.refs_0_), channel_id=1, source_target_pairs={{0,1},{1,0},{2,3},{3,2},{4,5},{5,4},{6,7},{7,6},{8,9},{9,8},{10,11... | collective-permute-start | bytes 786440 | tf_op jit(solution)/shard_map/ppermute | solution.py:312
  69.1 3.9 %collective-permute-start.6 = (bf16[64,2048]{1,0:T(8,128)(2,1)S(1)}, bf16[64,2048]{1,0:T(8,128)(2,1)S(1)}, u32[]{:S(2)}, u32[]{:S(2)}) collective-permute-start(bf16[64,2048]{1,0:T(8,128)(2,1)S(1)} %collective-permute-done.5.refs_2_), channel_id=1, source_target_pairs={{0,1},{1,0},{2,3},{3,2},{4,5},{5,4},{6,7},{7,6},{8,9},{9,8},{10,11... | collective-permute-start | bytes 786440 | tf_op jit(solution)/shard_map/ppermute | solution.py:312
  69.6 8.9 %collective-permute-start.7 = (bf16[16,2048]{1,0:T(8,128)(2,1)S(1)}, bf16[16,2048]{1,0:T(8,128)(2,1)S(1)}, u32[]{:S(2)}, u32[]{:S(2)}) collective-permute-start(bf16[16,2048]{1,0:T(8,128)(2,1)S(1)} %get-tuple-element.29), channel_id=1, source_target_pairs={{0,4},{4,8},{8,12},{12,16},{16,20},{20,24},{24,28},{28,32},{32,36}... | collective-permute-start | bytes 196616 | tf_op jit(solution)/shard_map/ppermute | solution.py:335
  73.0 2.8 %copy-start.1 = (bf16[2,16,6,128,128]{4,3,2,1,0:T(8,128)(2,1)S(1)}, bf16[2,16,6,128,128]{4,3,2,1,0:T(8,128)(2,1)}, u32[]{:S(2)}) copy-start(bf16[2,16,6,128,128]{4,3,2,1,0:T(8,128)(2,1)} %refs_4_.6) | copy-start | bytes 18874372

commit v6 on v5

--- a/solution.py
+++ b/solution.py
@@ -12,7 +12,8 @@
 ROWS = 8
 HALF = 4
 PARTS = 2
-FIRST = 63
+FIRST = 53
+LONG = 40000
 time_step = 0.25
 
 
@@ -202,7 +203,7 @@
     bracket = column(bracket_ref[...])
 
     def block(r, k):
-        source = pattern_ref[r, k]
+        source = pattern_ref[k, r]
         place = lax.rem(source, rows) + rows * ((source // rows) ^ me)
         return q_ref[:, pl.ds(pl.multiple_of(place * LANES, LANES), LANES)]
 
@@ -350,6 +351,7 @@
     cells, levels = populations.shape
     strips = lax.axis_size("cell")
     bracket = bracket.reshape(1, cells)
+    pattern = pattern.T
     cross = cross_section.reshape(1, levels)
     crosses = cross_section.reshape(levels // LANES, LANES)
     emission = emission.reshape(1, levels)
@@ -371,7 +373,7 @@
         first_kernel,
         sources,
         (rounded, layer, jax.ShapeDtypeStruct((strips, 2 * ROWS, LANES), jnp.bfloat16)),
-        3 * size,
+        LONG * size,
         [pltpu.VMEM(value.shape, value.dtype) for value in sources]
         + [pltpu.SemaphoreType.DMA((len(sources),))],
         [pl.BlockSpec(memory_space=pl.ANY)] * len(sources),

time: 83 us -> 82.5 us (level)
  waiting for transfers between devices: 2.35 us -> 4.63 us
  blocking collectives: 27.8 us -> 25.6 us
    all_to_all x2, waiting for transfers between devices: 2.33 us -> 4.61 us  [swap(): return lax.all_to_all(value, 'cell', 0, 0, tiled=True)]
    all_to_all x1, blocking collectives: 27.8 us -> 25.6 us  [swap(): return lax.all_to_all(value, 'cell', 0, 0, tiled=True)]
    unnamed x23 -> x28, local copies, waits for them, and re-layouts: 7.96 us -> 7.65 us
  transfers between devices with their start and end apart: 10 -> 10, of which waited for: 1 -> 2; matrix products, arithmetic and copies ran while one was open for 1% -> 0% of each run, Pallas kernels for 8% -> 8%
where the time goes in v6:
time: 82.5 us; the launch traced here: 82.1 us
  starting transfers between devices  31.7 us (38%)
  blocking collectives  25.6 us (31%)
  Pallas kernels  11.6 us (14%)
  local copies, waits for them, and re-layouts  7.65 us (9%)
  waiting for transfers between devices  4.63 us (6%)
  between operations  0.9 us (1%)
    all_to_all x1, blocking collectives, swap(): return lax.all_to_all(value, 'cell', 0, 0, tiled=True)  25.6 us
    all_to_all x2, starting transfers between devices, swap(): return lax.all_to_all(value, 'cell', 0, 0, tiled=True)  18.6 us
    unnamed x28, local copies, waits for them, and re-layouts  7.65 us
    ppermute x2, starting transfers between devices, shifted(): return lax.ppermute(value, axis, [(i, i + 1) for i in range(peers - 1)])  6.72 us
    ppermute x6, starting transfers between devices, swap(): lax.ppermute(value, axis, [(i, i ^ apart) for i in range(lax.axis_size(ax...  6.37 us
    pallas_call x7, Pallas kernels, call(): pl.pallas_call(body, out_shape=outs, in_specs=in_specs or vmem(len(args))...  6.33 us
    pallas_call x2, Pallas kernels, rate_term(): pl.pallas_call(functools.partial(rate_kernel, 'lev'), in_specs=[pl.BlockS...  5.31 us
    all_to_all x2, waiting for transfers between devices, swap(): return lax.all_to_all(value, 'cell', 0, 0, tiled=True)  4.61 us
  transfers between devices with their start and end apart: 10, of which 2 were waited for; matrix products, arithmetic and copies ran while one was open for 0% of the time, Pallas kernels for 8%

profile of v6, /device:TPU:2, one launch (start us, length us, event | category | flops | bytes accessed | tf_op | source)
XLA Modules:
  0.0 82.1 jit_solution(13800209863951166075)
XLA Ops:
  0.6 0.7 copy-done.4
  1.3 0.7 copy-done.6
  2.0 0.7 copy-done.9
  2.7 2.1 %shard_map.113 = (bf16[64,2048]{1,0:T(8,128)(2,1)S(1)}, bf16[16,2048]{1,0:T(8,128)(2,1)S(1)}, bf16[64,16,128]{2,1,0:T(8,128)(2,1)}) custom-call(f32[64,2048]{1,0:T(8,128)} %refs_10_.1, f32[1,2048]{1,0:T(1,128)S(1)} %bitcast.9, f32[1,2048]{1,0:T(1,128)S(1)} %bitcast.15, f32[1,64]{1,0:T(1,128)S(1)} %bitcast.21), custom_call_target="tpu_custom_call" | custom-call | flops 20971520000 | bytes 20971520000 | tf_op jit(solution)/shard_map/pallas_call | solution.py:300
  4.9 3.3 %collective-permute-start.1 = (bf16[64,2048]{1,0:T(8,128)(2,1)S(1)}, bf16[64,2048]{1,0:T(8,128)(2,1)S(1)}, u32[]{:S(2)}, u32[]{:S(2)}) collective-permute-start(bf16[64,2048]{1,0:T(8,128)(2,1)S(1)} %get-tuple-element.17.refs_0_), channel_id=1, source_target_pairs={{0,2},{1,3},{2,0},{3,1},{4,6},{5,7},{6,4},{7,5},{8,10},{9,11},{10,... | collective-permute-start | bytes 786440 | tf_op jit(solution)/shard_map/ppermute | solution.py:313
  8.2 12.1 %all-to-all-start = ((bf16[64,16,128]{2,1,0:T(8,128)(2,1)}), bf16[64,16,128]{2,1,0:T(8,128)(2,1)S(1)}, u32[]{:S(2)}, u32[]{:S(2)}) async-start(bf16[64,16,128]{2,1,0:T(8,128)(2,1)} %get-tuple-element.16), calls=%async_computation | async-start | bytes 524288 | tf_op jit(solution)/shard_map/all_to_all | solution.py:369
  20.4 0.5 collective-permute-start.2
  20.9 3.4 %collective-permute-start.3 = (bf16[16,2048]{1,0:T(8,128)(2,1)S(1)}, bf16[16,2048]{1,0:T(8,128)(2,1)S(1)}, u32[]{:S(2)}, u32[]{:S(2)}) collective-permute-start(bf16[16,2048]{1,0:T(8,128)(2,1)S(1)} %get-tuple-element.21), channel_id=1, source_target_pairs={{0,4},{4,8},{8,12},{12,16},{16,20},{20,24},{24,28},{28,32},{32,36}... | collective-permute-start | bytes 196616 | tf_op jit(solution)/shard_map/ppermute | solution.py:336
  24.3 2.8 %copy-done = bf16[2,16,6,128,128]{4,3,2,1,0:T(8,128)(2,1)S(1)} copy-done((bf16[2,16,6,128,128]{4,3,2,1,0:T(8,128)(2,1)S(1)}, bf16[2,16,6,128,128]{4,3,2,1,0:T(8,128)(2,1)}, u32[]{:S(2)}) %copy-start) | copy-done | bytes 6291480
  27.1 2.6 %shard_map.114.refs_1_ = f32[64,2048]{1,0:T(8,128)S(1)} custom-call(s32[6,16]{1,0:T(8,128)S(1)} %bitcast.19, bf16[64,2048]{1,0:T(8,128)(2,1)S(1)} %get-tuple-element.17.refs_0_, bf16[64,2048]{1,0:T(8,128)(2,1)S(1)} %collective-permute-done.refs_1_, bf16[64,2048]{1,0:T(8,128)(2,1)S(1)} %collective-permute-done.1.refs_2_, ...), custom_call_target="tpu_custom_call" | custom-call | flops 402653184 | bytes 6291456 | tf_op jit(solution)/shard_map/pallas_call | solution.py:321
  29.8 2.2 %all-to-all-done.arrived_ref = bf16[64,16,128]{2,1,0:T(8,128)(2,1)S(1)} async-done(((bf16[64,16,128]{2,1,0:T(8,128)(2,1)}), bf16[64,16,128]{2,1,0:T(8,128)(2,1)S(1)}, u32[]{:S(2)}, u32[]{:S(2)}) %all-to-all-start) | async-done | bytes 262176 | tf_op jit(solution)/shard_map/all_to_all | solution.py:369
  32.3 0.7 shard_map.116
  33.0 25.6 %all_to_all.15.swap_ref.arrived_ref = f32[64,16,128]{2,1,0:T(8,128)S(1)} all-to-all(f32[64,16,128]{2,1,0:T(8,128)S(1)} %get-tuple-element.23), channel_id=1, replica_groups=mesh['cell'=64,'lev'=4] {'cell'}, dimensions={0} | all-to-all | bytes 1048576 | tf_op jit(solution)/shard_map/all_to_all | solution.py:369
  58.5 0.3 shard_map.117
  58.9 1.9 %collective-permute-start.5 = (bf16[64,2048]{1,0:T(8,128)(2,1)S(1)}, bf16[64,2048]{1,0:T(8,128)(2,1)S(1)}, u32[]{:S(2)}, u32[]{:S(2)}) collective-permute-start(bf16[64,2048]{1,0:T(8,128)(2,1)S(1)} %get-tuple-element.25.refs_0_), channel_id=1, source_target_pairs={{0,2},{1,3},{2,0},{3,1},{4,6},{5,7},{6,4},{7,5},{8,10},{9,11},{10,... | collective-permute-start | bytes 786440 | tf_op jit(solution)/shard_map/ppermute | solution.py:313
  60.8 0.5 shard_map.119
  61.3 0.9 %shard_map.120 = f32[64,8,128]{2,1,0:T(8,128)} custom-call(f32[64,16,128]{2,1,0:T(8,128)S(1)} %all_to_all.15.swap_ref.arrived_ref, f32[64,8,128]{2,1,0:T(8,128)S(1)} %get-tuple-element.20.refs_2_.entered_ref, f32[64,8,128]{2,1,0:T(8,128)S(1)} %get-tuple-element.26.pass_ref, f32[64,8,128]{2,1,0:T(8,128)S(1)} %get-tuple-element.27.same_ref, ...), custom_call_target="tpu_custom_call" | custom-call | flops 524288 | bytes 524288 | tf_op jit(solution)/shard_map/pallas_call | solution.py:300
  62.1 6.4 %all-to-all-start.2 = ((f32[64,8,128]{2,1,0:T(8,128)}), f32[64,8,128]{2,1,0:T(8,128)S(1)}, u32[]{:S(2)}, u32[]{:S(2)}) async-start(f32[64,8,128]{2,1,0:T(8,128)} %shard_map.120), calls=%async_computation.2 | async-start | bytes 524288 | tf_op jit(solution)/shard_map/all_to_all | solution.py:369
  68.7 0.5 collective-permute-start.6
  69.2 3.4 %collective-permute-start.7 = (bf16[16,2048]{1,0:T(8,128)(2,1)S(1)}, bf16[16,2048]{1,0:T(8,128)(2,1)S(1)}, u32[]{:S(2)}, u32[]{:S(2)}) collective-permute-start(bf16[16,2048]{1,0:T(8,128)(2,1)S(1)} %get-tuple-element.29), channel_id=1, source_target_pairs={{0,4},{4,8},{8,12},{12,16},{16,20},{20,24},{24,28},{28,32},{32,36}... | collective-permute-start | bytes 196616 | tf_op jit(solution)/shard_map/ppermute | solution.py:336
  72.6 2.8 %copy-done.1 = bf16[2,16,6,128,128]{4,3,2,1,0:T(8,128)(2,1)S(1)} copy-done((bf16[2,16,6,128,128]{4,3,2,1,0:T(8,128)(2,1)S(1)}, bf16[2,16,6,128,128]{4,3,2,1,0:T(8,128)(2,1)}, u32[]{:S(2)}) %copy-start.1) | copy-done | bytes 6291480
  75.4 2.7 %shard_map.118.refs_1_ = f32[64,2048]{1,0:T(8,128)S(1)} custom-call(s32[6,16]{1,0:T(8,128)S(1)} %bitcast.20, bf16[64,2048]{1,0:T(8,128)(2,1)S(1)} %get-tuple-element.25.refs_0_, bf16[64,2048]{1,0:T(8,128)(2,1)S(1)} %collective-permute-done.4.refs_1_, bf16[64,2048]{1,0:T(8,128)(2,1)S(1)} %collective-permute-done.5.refs_2_, ...), custom_call_target="tpu_custom_call" | custom-call | flops 402653184 | bytes 6291456 | tf_op jit(solution)/shard_map/pallas_call | solution.py:321
  78.0 2.4 %all-to-all-done.2.refs_2_ = f32[64,8,128]{2,1,0:T(8,128)S(1)} async-done(((f32[64,8,128]{2,1,0:T(8,128)}), f32[64,8,128]{2,1,0:T(8,128)S(1)}, u32[]{:S(2)}, u32[]{:S(2)}) %all-to-all-start.2) | async-done | bytes 262176 | tf_op jit(solution)/shard_map/all_to_all | solution.py:369
  80.4 1.6 %shard_map.121 = (f32[64,2048]{1,0:T(8,128)}, f32[64,2048]{1,0:T(8,128)}) custom-call(f32[64,2048]{1,0:T(8,128)S(1)} %get-tuple-element.24.refs_0_, f32[64,2048]{1,0:T(8,128)S(1)} %shard_map.118.refs_1_, f32[64,8,128]{2,1,0:T(8,128)S(1)} %all-to-all-done.2.refs_2_, bf16[16,2048]{1,0:T(8,128)(2,1)S(1)} %collective-permute-done.7.refs_3_, ...), custom_call_target="tpu_custom_call" | custom-call | flops 2621440 | bytes 2621440 | tf_op jit(solution)/shard_map/pallas_call | solution.py:300
  (34 shorter events, 0.5 us)
Async XLA Ops:
  0.6 0.7 copy-start.4
  1.3 0.7 copy-start.6
  2.0 0.7 copy-start.9
  2.7 21.6 %copy-start.8 = (s32[16,6]{0,1:T(8,128)S(1)}, s32[16,6]{0,1:T(8,128)}, u32[]{:S(2)}) copy-start(s32[16,6]{0,1:T(8,128)} %param.12) | copy-start | bytes 1156
  2.7 21.6 %copy-start.11 = (s32[64]{0:T(128)S(1)}, s32[64]{0:T(128)}, u32[]{:S(2)}) copy-start(s32[64]{0:T(128)} %param.13) | copy-start | bytes 772
  2.7 29.5 %copy-start.3 = (f32[16,2048]{1,0:T(8,128)S(1)}, f32[16,2048]{1,0:T(8,128)}, u32[]{:S(2)}) copy-start(f32[16,2048]{1,0:T(8,128)} %refs_4_.7) | copy-start | bytes 393220
  2.7 29.5 %copy-start.7 = (f32[2048]{0:T(1024)S(1)}, f32[2048]{0:T(1024)}, u32[]{:S(2)}) copy-start(f32[2048]{0:T(1024)} %param.15) | copy-start | bytes 24580
  4.8 27.1 %copy-start.5 = (f32[2048]{0:T(1024)S(1)}, f32[2048]{0:T(1024)}, u32[]{:S(2)}) copy-start(f32[2048]{0:T(1024)} %param.14) | copy-start | bytes 24580
  4.9 27.4 %copy-start.2 = (f32[64,2048]{1,0:T(8,128)S(1)}, f32[64,2048]{1,0:T(8,128)}, u32[]{:S(2)}) copy-start(f32[64,2048]{1,0:T(8,128)} %refs_10_.1) | copy-start | bytes 1572868
  4.9 27.4 %copy-start.12 = (f32[64]{0:T(128)S(1)}, f32[64]{0:T(128)}, u32[]{:S(2)}) copy-start(f32[64]{0:T(128)} %param.17) | copy-start | bytes 772
  4.9 27.4 %copy-start.13 = (f32[64]{0:T(128)S(1)}, f32[64]{0:T(128)}, u32[]{:S(2)}) copy-start(f32[64]{0:T(128)} %param.18) | copy-start | bytes 772
  4.9 15.5 %collective-permute-start.1 = (bf16[64,2048]{1,0:T(8,128)(2,1)S(1)}, bf16[64,2048]{1,0:T(8,128)(2,1)S(1)}, u32[]{:S(2)}, u32[]{:S(2)}) collective-permute-start(bf16[64,2048]{1,0:T(8,128)(2,1)S(1)} %get-tuple-element.17.refs_0_), channel_id=1, source_target_pairs={{0,2},{1,3},{2,0},{3,1},{4,6},{5,7},{6,4},{7,5},{8,10},{9,11},{10,... | collective-permute-start | bytes 786440 | tf_op jit(solution)/shard_map/ppermute | solution.py:313
  8.2 23.8 %all-to-all-start = ((bf16[64,16,128]{2,1,0:T(8,128)(2,1)}), bf16[64,16,128]{2,1,0:T(8,128)(2,1)S(1)}, u32[]{:S(2)}, u32[]{:S(2)}) async-start(bf16[64,16,128]{2,1,0:T(8,128)(2,1)} %get-tuple-element.16), calls=%async_computation | async-start | bytes 524288 | tf_op jit(solution)/shard_map/all_to_all | solution.py:369
  20.3 4.0 %collective-permute-start = (bf16[64,2048]{1,0:T(8,128)(2,1)S(1)}, bf16[64,2048]{1,0:T(8,128)(2,1)S(1)}, u32[]{:S(2)}, u32[]{:S(2)}) collective-permute-start(bf16[64,2048]{1,0:T(8,128)(2,1)S(1)} %get-tuple-element.17.refs_0_), channel_id=1, source_target_pairs={{0,1},{1,0},{2,3},{3,2},{4,5},{5,4},{6,7},{7,6},{8,9},{9,8},{10,11... | collective-permute-start | bytes 786440 | tf_op jit(solution)/shard_map/ppermute | solution.py:313
  20.4 3.9 %collective-permute-start.2 = (bf16[64,2048]{1,0:T(8,128)(2,1)S(1)}, bf16[64,2048]{1,0:T(8,128)(2,1)S(1)}, u32[]{:S(2)}, u32[]{:S(2)}) collective-permute-start(bf16[64,2048]{1,0:T(8,128)(2,1)S(1)} %collective-permute-done.1.refs_2_), channel_id=1, source_target_pairs={{0,1},{1,0},{2,3},{3,2},{4,5},{5,4},{6,7},{7,6},{8,9},{9,8},{10,11... | collective-permute-start | bytes 786440 | tf_op jit(solution)/shard_map/ppermute | solution.py:313
  20.9 11.3 %collective-permute-start.3 = (bf16[16,2048]{1,0:T(8,128)(2,1)S(1)}, bf16[16,2048]{1,0:T(8,128)(2,1)S(1)}, u32[]{:S(2)}, u32[]{:S(2)}) collective-permute-start(bf16[16,2048]{1,0:T(8,128)(2,1)S(1)} %get-tuple-element.21), channel_id=1, source_target_pairs={{0,4},{4,8},{8,12},{12,16},{16,20},{20,24},{24,28},{28,32},{32,36}... | collective-permute-start | bytes 196616 | tf_op jit(solution)/shard_map/ppermute | solution.py:336
  24.3 2.8 %copy-start = (bf16[2,16,6,128,128]{4,3,2,1,0:T(8,128)(2,1)S(1)}, bf16[2,16,6,128,128]{4,3,2,1,0:T(8,128)(2,1)}, u32[]{:S(2)}) copy-start(bf16[2,16,6,128,128]{4,3,2,1,0:T(8,128)(2,1)} %refs_4_.6) | copy-start | bytes 18874372
  33.0 47.5 %copy-start.10 = (f32[64]{0:T(128)S(1)}, f32[64]{0:T(128)}, u32[]{:S(2)}) copy-start(f32[64]{0:T(128)} %param.16) | copy-start | bytes 772
  58.9 9.8 %collective-permute-start.5 = (bf16[64,2048]{1,0:T(8,128)(2,1)S(1)}, bf16[64,2048]{1,0:T(8,128)(2,1)S(1)}, u32[]{:S(2)}, u32[]{:S(2)}) collective-permute-start(bf16[64,2048]{1,0:T(8,128)(2,1)S(1)} %get-tuple-element.25.refs_0_), channel_id=1, source_target_pairs={{0,2},{1,3},{2,0},{3,1},{4,6},{5,7},{6,4},{7,5},{8,10},{9,11},{10,... | collective-permute-start | bytes 786440 | tf_op jit(solution)/shard_map/ppermute | solution.py:313
  62.1 18.3 %all-to-all-start.2 = ((f32[64,8,128]{2,1,0:T(8,128)}), f32[64,8,128]{2,1,0:T(8,128)S(1)}, u32[]{:S(2)}, u32[]{:S(2)}) async-start(f32[64,8,128]{2,1,0:T(8,128)} %shard_map.120), calls=%async_computation.2 | async-start | bytes 524288 | tf_op jit(solution)/shard_map/all_to_all | solution.py:369
  68.6 4.0 %collective-permute-start.4 = (bf16[64,2048]{1,0:T(8,128)(2,1)S(1)}, bf16[64,2048]{1,0:T(8,128)(2,1)S(1)}, u32[]{:S(2)}, u32[]{:S(2)}) collective-permute-start(bf16[64,2048]{1,0:T(8,128)(2,1)S(1)} %get-tuple-element.25.refs_0_), channel_id=1, source_target_pairs={{0,1},{1,0},{2,3},{3,2},{4,5},{5,4},{6,7},{7,6},{8,9},{9,8},{10,11... | collective-permute-start | bytes 786440 | tf_op jit(solution)/shard_map/ppermute | solution.py:313
  68.7 3.9 %collective-permute-start.6 = (bf16[64,2048]{1,0:T(8,128)(2,1)S(1)}, bf16[64,2048]{1,0:T(8,128)(2,1)S(1)}, u32[]{:S(2)}, u32[]{:S(2)}) collective-permute-start(bf16[64,2048]{1,0:T(8,128)(2,1)S(1)} %collective-permute-done.5.refs_2_), channel_id=1, source_target_pairs={{0,1},{1,0},{2,3},{3,2},{4,5},{5,4},{6,7},{7,6},{8,9},{9,8},{10,11... | collective-permute-start | bytes 786440 | tf_op jit(solution)/shard_map/ppermute | solution.py:313
  69.2 8.8 %collective-permute-start.7 = (bf16[16,2048]{1,0:T(8,128)(2,1)S(1)}, bf16[16,2048]{1,0:T(8,128)(2,1)S(1)}, u32[]{:S(2)}, u32[]{:S(2)}) collective-permute-start(bf16[16,2048]{1,0:T(8,128)(2,1)S(1)} %get-tuple-element.29), channel_id=1, source_target_pairs={{0,4},{4,8},{8,12},{12,16},{16,20},{20,24},{24,28},{28,32},{32,36}... | collective-permute-start | bytes 196616 | tf_op jit(solution)/shard_map/ppermute | solution.py:336
  72.6 2.8 %copy-start.1 = (bf16[2,16,6,128,128]{4,3,2,1,0:T(8,128)(2,1)S(1)}, bf16[2,16,6,128,128]{4,3,2,1,0:T(8,128)(2,1)}, u32[]{:S(2)}) copy-start(bf16[2,16,6,128,128]{4,3,2,1,0:T(8,128)(2,1)} %refs_4_.6) | copy-start | bytes 18874372

commit v7 on v6

--- a/solution.py
+++ b/solution.py
@@ -12,7 +12,7 @@
 ROWS = 8
 HALF = 4
 PARTS = 2
-FIRST = 53
+FIRST = 57
 LONG = 40000
 time_step = 0.25
 

time: 82.5 us -> 81.5 us (0.988)
  local copies, waits for them, and re-layouts: 7.65 us -> 6.56 us
  waiting for transfers between devices: 4.63 us -> 3.69 us
  blocking collectives: 25.6 us -> 26.5 us
    unnamed x28 -> x24, local copies, waits for them, and re-layouts: 7.65 us -> 6.56 us
    all_to_all x1, blocking collectives: 25.6 us -> 26.5 us  [swap(): return lax.all_to_all(value, 'cell', 0, 0, tiled=True)]
    all_to_all x2, waiting for transfers between devices: 4.61 us -> 3.67 us  [swap(): return lax.all_to_all(value, 'cell', 0, 0, tiled=True)]
where the time goes in v7:
time: 81.5 us; the launch traced here: 81.1 us
  starting transfers between devices  31.7 us (39%)
  blocking collectives  26.5 us (33%)
  Pallas kernels  11.7 us (14%)
  local copies, waits for them, and re-layouts  6.56 us (8%)
  waiting for transfers between devices  3.69 us (5%)
  between operations  0.93 us (1%)
    all_to_all x1, blocking collectives, swap(): return lax.all_to_all(value, 'cell', 0, 0, tiled=True)  26.5 us
    all_to_all x2, starting transfers between devices, swap(): return lax.all_to_all(value, 'cell', 0, 0, tiled=True)  18.6 us
    ppermute x2, starting transfers between devices, shifted(): return lax.ppermute(value, axis, [(i, i + 1) for i in range(peers - 1)])  6.72 us
    unnamed x24, local copies, waits for them, and re-layouts  6.56 us
    pallas_call x7, Pallas kernels, call(): pl.pallas_call(body, out_shape=outs, in_specs=in_specs or vmem(len(args))...  6.42 us
    ppermute x6, starting transfers between devices, swap(): lax.ppermute(value, axis, [(i, i ^ apart) for i in range(lax.axis_size(ax...  6.37 us
    pallas_call x2, Pallas kernels, rate_term(): pl.pallas_call(functools.partial(rate_kernel, 'lev'), in_specs=[pl.BlockS...  5.32 us
    all_to_all x2, waiting for transfers between devices, swap(): return lax.all_to_all(value, 'cell', 0, 0, tiled=True)  3.67 us
  transfers between devices with their start and end apart: 10, of which 2 were waited for; matrix products, arithmetic and copies ran while one was open for 0% of the time, Pallas kernels for 8%

profile of v7, /device:TPU:2, one launch (start us, length us, event | category | flops | bytes accessed | tf_op | source)
XLA Modules:
  0.0 81.1 jit_solution(12847891668907225752)
XLA Ops:
  0.7 2.2 %shard_map.113 = (bf16[64,2048]{1,0:T(8,128)(2,1)}, bf16[16,2048]{1,0:T(8,128)(2,1)}, bf16[64,16,128]{2,1,0:T(8,128)(2,1)}) custom-call(f32[64,2048]{1,0:T(8,128)} %refs_10_.1, f32[1,2048]{1,0:T(1,128)} %bitcast.9, f32[1,2048]{1,0:T(1,128)} %bitcast.15, f32[1,64]{1,0:T(1,128)} %bitcast.21), custom_call_target="tpu_custom_call" | custom-call | flops 20971520000 | bytes 20971520000 | tf_op jit(solution)/shard_map/pallas_call | solution.py:300
  3.0 3.3 %collective-permute-start.1 = (bf16[64,2048]{1,0:T(8,128)(2,1)}, bf16[64,2048]{1,0:T(8,128)(2,1)S(1)}, u32[]{:S(2)}, u32[]{:S(2)}) collective-permute-start(bf16[64,2048]{1,0:T(8,128)(2,1)} %get-tuple-element.17.refs_0_), channel_id=1, source_target_pairs={{0,2},{1,3},{2,0},{3,1},{4,6},{5,7},{6,4},{7,5},{8,10},{9,11},{10,... | collective-permute-start | bytes 786440 | tf_op jit(solution)/shard_map/ppermute | solution.py:313
  6.2 12.1 %all-to-all-start = ((bf16[64,16,128]{2,1,0:T(8,128)(2,1)}), bf16[64,16,128]{2,1,0:T(8,128)(2,1)S(1)}, u32[]{:S(2)}, u32[]{:S(2)}) async-start(bf16[64,16,128]{2,1,0:T(8,128)(2,1)} %get-tuple-element.16), calls=%async_computation | async-start | bytes 524288 | tf_op jit(solution)/shard_map/all_to_all | solution.py:369
  18.5 0.5 collective-permute-start.2
  19.0 3.4 %collective-permute-start.3 = (bf16[16,2048]{1,0:T(8,128)(2,1)}, bf16[16,2048]{1,0:T(8,128)(2,1)S(1)}, u32[]{:S(2)}, u32[]{:S(2)}) collective-permute-start(bf16[16,2048]{1,0:T(8,128)(2,1)} %get-tuple-element.21), channel_id=1, source_target_pairs={{0,4},{4,8},{8,12},{12,16},{16,20},{20,24},{24,28},{28,32},{32,36}... | collective-permute-start | bytes 196616 | tf_op jit(solution)/shard_map/ppermute | solution.py:336
  22.4 2.8 %copy-done = bf16[2,16,6,128,128]{4,3,2,1,0:T(8,128)(2,1)S(1)} copy-done((bf16[2,16,6,128,128]{4,3,2,1,0:T(8,128)(2,1)S(1)}, bf16[2,16,6,128,128]{4,3,2,1,0:T(8,128)(2,1)}, u32[]{:S(2)}) %copy-start) | copy-done | bytes 6291480
  25.2 0.9 %copy-done.4 = bf16[64,2048]{1,0:T(8,128)(2,1)S(1)} copy-done((bf16[64,2048]{1,0:T(8,128)(2,1)S(1)}, bf16[64,2048]{1,0:T(8,128)(2,1)}, u32[]{:S(2)}) %copy-start.4) | copy-done | bytes 262168
  26.1 2.7 %shard_map.114.refs_1_ = f32[64,2048]{1,0:T(8,128)S(1)} custom-call(s32[6,16]{1,0:T(8,128)S(1)} %bitcast.19, bf16[64,2048]{1,0:T(8,128)(2,1)S(1)} %copy-done.4, bf16[64,2048]{1,0:T(8,128)(2,1)S(1)} %collective-permute-done.refs_1_, bf16[64,2048]{1,0:T(8,128)(2,1)S(1)} %collective-permute-done.1.refs_2_, bf16[64,2048]{1,0:T(8,128)(2,1)S(1)} %collective-permute-done.2.refs_3_, ...), custom_call_target="tpu_custom_call" | custom-call | flops 402653184 | bytes 6291456 | tf_op jit(solution)/shard_map/pallas_call | solution.py:321
  28.8 1.3 %all-to-all-done.arrived_ref = bf16[64,16,128]{2,1,0:T(8,128)(2,1)S(1)} async-done(((bf16[64,16,128]{2,1,0:T(8,128)(2,1)}), bf16[64,16,128]{2,1,0:T(8,128)(2,1)S(1)}, u32[]{:S(2)}, u32[]{:S(2)}) %all-to-all-start) | async-done | bytes 262176 | tf_op jit(solution)/shard_map/all_to_all | solution.py:369
  30.1 0.2 shard_map.115
  30.3 0.7 shard_map.116
  31.1 26.5 %all_to_all.15.swap_ref.arrived_ref = f32[64,16,128]{2,1,0:T(8,128)S(1)} all-to-all(f32[64,16,128]{2,1,0:T(8,128)S(1)} %get-tuple-element.23), channel_id=1, replica_groups=mesh['cell'=64,'lev'=4] {'cell'}, dimensions={0} | all-to-all | bytes 1048576 | tf_op jit(solution)/shard_map/all_to_all | solution.py:369
  57.6 0.3 shard_map.117
  57.9 1.9 %collective-permute-start.5 = (bf16[64,2048]{1,0:T(8,128)(2,1)S(1)}, bf16[64,2048]{1,0:T(8,128)(2,1)S(1)}, u32[]{:S(2)}, u32[]{:S(2)}) collective-permute-start(bf16[64,2048]{1,0:T(8,128)(2,1)S(1)} %get-tuple-element.25.refs_0_), channel_id=1, source_target_pairs={{0,2},{1,3},{2,0},{3,1},{4,6},{5,7},{6,4},{7,5},{8,10},{9,11},{10,... | collective-permute-start | bytes 786440 | tf_op jit(solution)/shard_map/ppermute | solution.py:313
  59.8 0.5 shard_map.119
  60.3 0.8 %shard_map.120 = f32[64,8,128]{2,1,0:T(8,128)} custom-call(f32[64,16,128]{2,1,0:T(8,128)S(1)} %all_to_all.15.swap_ref.arrived_ref, f32[64,8,128]{2,1,0:T(8,128)S(1)} %get-tuple-element.20.refs_2_.entered_ref, f32[64,8,128]{2,1,0:T(8,128)S(1)} %get-tuple-element.26.pass_ref, f32[64,8,128]{2,1,0:T(8,128)S(1)} %get-tuple-element.27.same_ref, ...), custom_call_target="tpu_custom_call" | custom-call | flops 524288 | bytes 524288 | tf_op jit(solution)/shard_map/pallas_call | solution.py:300
  61.1 6.4 %all-to-all-start.2 = ((f32[64,8,128]{2,1,0:T(8,128)}), f32[64,8,128]{2,1,0:T(8,128)S(1)}, u32[]{:S(2)}, u32[]{:S(2)}) async-start(f32[64,8,128]{2,1,0:T(8,128)} %shard_map.120), calls=%async_computation.2 | async-start | bytes 524288 | tf_op jit(solution)/shard_map/all_to_all | solution.py:369
  67.6 0.1 collective-permute-start.4
  67.7 0.5 collective-permute-start.6
  68.2 3.4 %collective-permute-start.7 = (bf16[16,2048]{1,0:T(8,128)(2,1)S(1)}, bf16[16,2048]{1,0:T(8,128)(2,1)S(1)}, u32[]{:S(2)}, u32[]{:S(2)}) collective-permute-start(bf16[16,2048]{1,0:T(8,128)(2,1)S(1)} %get-tuple-element.29), channel_id=1, source_target_pairs={{0,4},{4,8},{8,12},{12,16},{16,20},{20,24},{24,28},{28,32},{32,36}... | collective-permute-start | bytes 196616 | tf_op jit(solution)/shard_map/ppermute | solution.py:336
  71.6 2.8 %copy-done.1 = bf16[2,16,6,128,128]{4,3,2,1,0:T(8,128)(2,1)S(1)} copy-done((bf16[2,16,6,128,128]{4,3,2,1,0:T(8,128)(2,1)S(1)}, bf16[2,16,6,128,128]{4,3,2,1,0:T(8,128)(2,1)}, u32[]{:S(2)}) %copy-start.1) | copy-done | bytes 6291480
  74.4 2.7 %shard_map.118.refs_1_ = f32[64,2048]{1,0:T(8,128)S(1)} custom-call(s32[6,16]{1,0:T(8,128)S(1)} %bitcast.20, bf16[64,2048]{1,0:T(8,128)(2,1)S(1)} %get-tuple-element.25.refs_0_, bf16[64,2048]{1,0:T(8,128)(2,1)S(1)} %collective-permute-done.4.refs_1_, bf16[64,2048]{1,0:T(8,128)(2,1)S(1)} %collective-permute-done.5.refs_2_, ...), custom_call_target="tpu_custom_call" | custom-call | flops 402653184 | bytes 6291456 | tf_op jit(solution)/shard_map/pallas_call | solution.py:321
  77.0 2.4 %all-to-all-done.2.refs_2_ = f32[64,8,128]{2,1,0:T(8,128)S(1)} async-done(((f32[64,8,128]{2,1,0:T(8,128)}), f32[64,8,128]{2,1,0:T(8,128)S(1)}, u32[]{:S(2)}, u32[]{:S(2)}) %all-to-all-start.2) | async-done | bytes 262176 | tf_op jit(solution)/shard_map/all_to_all | solution.py:369
  79.4 1.7 %shard_map.121 = (f32[64,2048]{1,0:T(8,128)}, f32[64,2048]{1,0:T(8,128)}) custom-call(f32[64,2048]{1,0:T(8,128)S(1)} %get-tuple-element.24.refs_0_, f32[64,2048]{1,0:T(8,128)S(1)} %shard_map.118.refs_1_, f32[64,8,128]{2,1,0:T(8,128)S(1)} %all-to-all-done.2.refs_2_, bf16[16,2048]{1,0:T(8,128)(2,1)S(1)} %collective-permute-done.7.refs_3_, ...), custom_call_target="tpu_custom_call" | custom-call | flops 2621440 | bytes 2621440 | tf_op jit(solution)/shard_map/pallas_call | solution.py:300
  (30 shorter events, 0.2 us)
Async XLA Ops:
  0.6 21.7 %copy-start.7 = (s32[16,6]{0,1:T(8,128)S(1)}, s32[16,6]{0,1:T(8,128)}, u32[]{:S(2)}) copy-start(s32[16,6]{0,1:T(8,128)} %param.12) | copy-start | bytes 1156
  0.6 21.7 %copy-start.9 = (s32[64]{0:T(128)S(1)}, s32[64]{0:T(128)}, u32[]{:S(2)}) copy-start(s32[64]{0:T(128)} %param.13) | copy-start | bytes 772
  0.7 29.6 %copy-start.3 = (f32[16,2048]{1,0:T(8,128)S(1)}, f32[16,2048]{1,0:T(8,128)}, u32[]{:S(2)}) copy-start(f32[16,2048]{1,0:T(8,128)} %refs_4_.7) | copy-start | bytes 393220
  0.7 29.6 %copy-start.6 = (f32[2048]{0:T(1024)S(1)}, f32[2048]{0:T(1024)}, u32[]{:S(2)}) copy-start(f32[2048]{0:T(1024)} %param.15) | copy-start | bytes 24580
  0.7 29.6 %copy-start.11 = (f32[64]{0:T(128)S(1)}, f32[64]{0:T(128)}, u32[]{:S(2)}) copy-start(f32[64]{0:T(128)} %param.18) | copy-start | bytes 772
  2.9 27.1 %copy-start.5 = (f32[2048]{0:T(1024)S(1)}, f32[2048]{0:T(1024)}, u32[]{:S(2)}) copy-start(f32[2048]{0:T(1024)} %param.14) | copy-start | bytes 24580
  2.9 27.4 %copy-start.2 = (f32[64,2048]{1,0:T(8,128)S(1)}, f32[64,2048]{1,0:T(8,128)}, u32[]{:S(2)}) copy-start(f32[64,2048]{1,0:T(8,128)} %refs_10_.1) | copy-start | bytes 1572868
  2.9 27.4 %copy-start.8 = (f32[64]{0:T(128)S(1)}, f32[64]{0:T(128)}, u32[]{:S(2)}) copy-start(f32[64]{0:T(128)} %param.16) | copy-start | bytes 772
  2.9 27.4 %copy-start.10 = (f32[64]{0:T(128)S(1)}, f32[64]{0:T(128)}, u32[]{:S(2)}) copy-start(f32[64]{0:T(128)} %param.17) | copy-start | bytes 772
  3.0 15.5 %collective-permute-start.1 = (bf16[64,2048]{1,0:T(8,128)(2,1)}, bf16[64,2048]{1,0:T(8,128)(2,1)S(1)}, u32[]{:S(2)}, u32[]{:S(2)}) collective-permute-start(bf16[64,2048]{1,0:T(8,128)(2,1)} %get-tuple-element.17.refs_0_), channel_id=1, source_target_pairs={{0,2},{1,3},{2,0},{3,1},{4,6},{5,7},{6,4},{7,5},{8,10},{9,11},{10,... | collective-permute-start | bytes 786440 | tf_op jit(solution)/shard_map/ppermute | solution.py:313
  6.2 23.8 %all-to-all-start = ((bf16[64,16,128]{2,1,0:T(8,128)(2,1)}), bf16[64,16,128]{2,1,0:T(8,128)(2,1)S(1)}, u32[]{:S(2)}, u32[]{:S(2)}) async-start(bf16[64,16,128]{2,1,0:T(8,128)(2,1)} %get-tuple-element.16), calls=%async_computation | async-start | bytes 524288 | tf_op jit(solution)/shard_map/all_to_all | solution.py:369
  18.4 4.0 %collective-permute-start = (bf16[64,2048]{1,0:T(8,128)(2,1)}, bf16[64,2048]{1,0:T(8,128)(2,1)S(1)}, u32[]{:S(2)}, u32[]{:S(2)}) collective-permute-start(bf16[64,2048]{1,0:T(8,128)(2,1)} %get-tuple-element.17.refs_0_), channel_id=1, source_target_pairs={{0,1},{1,0},{2,3},{3,2},{4,5},{5,4},{6,7},{7,6},{8,9},{9,8},{10,11... | collective-permute-start | bytes 786440 | tf_op jit(solution)/shard_map/ppermute | solution.py:313
  18.5 3.9 %collective-permute-start.2 = (bf16[64,2048]{1,0:T(8,128)(2,1)S(1)}, bf16[64,2048]{1,0:T(8,128)(2,1)S(1)}, u32[]{:S(2)}, u32[]{:S(2)}) collective-permute-start(bf16[64,2048]{1,0:T(8,128)(2,1)S(1)} %collective-permute-done.1.refs_2_), channel_id=1, source_target_pairs={{0,1},{1,0},{2,3},{3,2},{4,5},{5,4},{6,7},{7,6},{8,9},{9,8},{10,11... | collective-permute-start | bytes 786440 | tf_op jit(solution)/shard_map/ppermute | solution.py:313
  19.0 11.3 %collective-permute-start.3 = (bf16[16,2048]{1,0:T(8,128)(2,1)}, bf16[16,2048]{1,0:T(8,128)(2,1)S(1)}, u32[]{:S(2)}, u32[]{:S(2)}) collective-permute-start(bf16[16,2048]{1,0:T(8,128)(2,1)} %get-tuple-element.21), channel_id=1, source_target_pairs={{0,4},{4,8},{8,12},{12,16},{16,20},{20,24},{24,28},{28,32},{32,36}... | collective-permute-start | bytes 196616 | tf_op jit(solution)/shard_map/ppermute | solution.py:336
  22.4 2.8 %copy-start = (bf16[2,16,6,128,128]{4,3,2,1,0:T(8,128)(2,1)S(1)}, bf16[2,16,6,128,128]{4,3,2,1,0:T(8,128)(2,1)}, u32[]{:S(2)}) copy-start(bf16[2,16,6,128,128]{4,3,2,1,0:T(8,128)(2,1)} %refs_4_.6) | copy-start | bytes 18874372
  25.2 0.9 %copy-start.4 = (bf16[64,2048]{1,0:T(8,128)(2,1)S(1)}, bf16[64,2048]{1,0:T(8,128)(2,1)}, u32[]{:S(2)}) copy-start(bf16[64,2048]{1,0:T(8,128)(2,1)} %get-tuple-element.17.refs_0_) | copy-start | bytes 786436
  57.9 9.8 %collective-permute-start.5 = (bf16[64,2048]{1,0:T(8,128)(2,1)S(1)}, bf16[64,2048]{1,0:T(8,128)(2,1)S(1)}, u32[]{:S(2)}, u32[]{:S(2)}) collective-permute-start(bf16[64,2048]{1,0:T(8,128)(2,1)S(1)} %get-tuple-element.25.refs_0_), channel_id=1, source_target_pairs={{0,2},{1,3},{2,0},{3,1},{4,6},{5,7},{6,4},{7,5},{8,10},{9,11},{10,... | collective-permute-start | bytes 786440 | tf_op jit(solution)/shard_map/ppermute | solution.py:313
  61.1 18.3 %all-to-all-start.2 = ((f32[64,8,128]{2,1,0:T(8,128)}), f32[64,8,128]{2,1,0:T(8,128)S(1)}, u32[]{:S(2)}, u32[]{:S(2)}) async-start(f32[64,8,128]{2,1,0:T(8,128)} %shard_map.120), calls=%async_computation.2 | async-start | bytes 524288 | tf_op jit(solution)/shard_map/all_to_all | solution.py:369
  67.6 4.0 %collective-permute-start.4 = (bf16[64,2048]{1,0:T(8,128)(2,1)S(1)}, bf16[64,2048]{1,0:T(8,128)(2,1)S(1)}, u32[]{:S(2)}, u32[]{:S(2)}) collective-permute-start(bf16[64,2048]{1,0:T(8,128)(2,1)S(1)} %get-tuple-element.25.refs_0_), channel_id=1, source_target_pairs={{0,1},{1,0},{2,3},{3,2},{4,5},{5,4},{6,7},{7,6},{8,9},{9,8},{10,11... | collective-permute-start | bytes 786440 | tf_op jit(solution)/shard_map/ppermute | solution.py:313
  67.7 3.9 %collective-permute-start.6 = (bf16[64,2048]{1,0:T(8,128)(2,1)S(1)}, bf16[64,2048]{1,0:T(8,128)(2,1)S(1)}, u32[]{:S(2)}, u32[]{:S(2)}) collective-permute-start(bf16[64,2048]{1,0:T(8,128)(2,1)S(1)} %collective-permute-done.5.refs_2_), channel_id=1, source_target_pairs={{0,1},{1,0},{2,3},{3,2},{4,5},{5,4},{6,7},{7,6},{8,9},{9,8},{10,11... | collective-permute-start | bytes 786440 | tf_op jit(solution)/shard_map/ppermute | solution.py:313
  68.2 8.8 %collective-permute-start.7 = (bf16[16,2048]{1,0:T(8,128)(2,1)S(1)}, bf16[16,2048]{1,0:T(8,128)(2,1)S(1)}, u32[]{:S(2)}, u32[]{:S(2)}) collective-permute-start(bf16[16,2048]{1,0:T(8,128)(2,1)S(1)} %get-tuple-element.29), channel_id=1, source_target_pairs={{0,4},{4,8},{8,12},{12,16},{16,20},{20,24},{24,28},{28,32},{32,36}... | collective-permute-start | bytes 196616 | tf_op jit(solution)/shard_map/ppermute | solution.py:336
  71.6 2.8 %copy-start.1 = (bf16[2,16,6,128,128]{4,3,2,1,0:T(8,128)(2,1)S(1)}, bf16[2,16,6,128,128]{4,3,2,1,0:T(8,128)(2,1)}, u32[]{:S(2)}) copy-start(bf16[2,16,6,128,128]{4,3,2,1,0:T(8,128)(2,1)} %refs_4_.6) | copy-start | bytes 18874372

commit v8 on v7

--- a/solution.py
+++ b/solution.py
@@ -193,14 +193,19 @@
     scan(lambda at: exit_ref[at], pass_ref, enter_ref)
 
 
+def first_bracket_kernel(bracket_ref, first_ref):
+    first = jnp.where(column(bracket_ref[...]) == 0, 1.0, 0.0)
+    first_ref[...] = jnp.broadcast_to(first, first_ref.shape)
+
+
 def rate_kernel(axis, pattern_ref, *refs):
-    pieces, (table_ref, bracket_ref, out_ref, q_ref) = refs[:-4], refs[-4:]
+    pieces, (table_ref, first_ref, out_ref, q_ref) = refs[:-4], refs[-4:]
     brackets, rows, count = table_ref.shape[:3]
     width = pieces[0].shape[1]
     for place, piece in enumerate(pieces):
         q_ref[:, place * width : (place + 1) * width] = piece[...]
     me = lax.axis_index(axis)
-    bracket = column(bracket_ref[...])
+    first = first_ref[...] > 0.5
 
     def block(r, k):
         source = pattern_ref[k, r]
@@ -220,7 +225,7 @@
             picked, both, (((1,), (1,)), ((), ())), preferred_element_type=jnp.float32
         )
         out_ref[:, r * LANES : (r + 1) * LANES] = jnp.where(
-            bracket == 0, product[:, :LANES], product[:, LANES:]
+            first, product[:, :LANES], product[:, LANES:]
         )
 
 
@@ -316,7 +321,7 @@
     return q, swap(q, 1), far, swap(far, 1)
 
 
-def rate_term(pieces, rate_blocks, pattern, bracket):
+def rate_term(pieces, rate_blocks, pattern, first):
     cells, levels = pieces[0].shape
     return pl.pallas_call(
         functools.partial(rate_kernel, "lev"),
@@ -328,7 +333,7 @@
         cost_estimate=pl.CostEstimate(
             flops=2 * cells * rate_blocks.size, bytes_accessed=2 * rate_blocks.size, transcendentals=0
         ),
-    )(pattern, *pieces, rate_blocks, bracket)
+    )(pattern, *pieces, rate_blocks, first)
 
 
 def shifted(value, axis):
@@ -380,9 +385,16 @@
         pltpu.CompilerParams(vmem_limit_bytes=FIRST * 2**20),
     )
     pieces = gathered(q, "lev")
+    (first,) = call(
+        first_bracket_kernel,
+        (bracket,),
+        (jax.ShapeDtypeStruct((cells, LANES), jnp.float32),),
+        LONG * size,
+    )
+    last, first = lax.optimization_barrier((last, first))
     arrived = shifted(last, "cell")
     sent, rates = lax.optimization_barrier(
-        (swap(leaving), rate_term(pieces, rate_blocks, pattern, bracket))
+        (swap(leaving), rate_term(pieces, rate_blocks, pattern, first))
     )
     entered, passes = call(
         functools.partial(first_scan_kernel, "cell", cells // NY),
@@ -417,7 +429,7 @@
         [pltpu.VMEM(tiles.shape, jnp.float32)],
     )
     entering = swap(entering)
-    rates = rate_term(pieces, rate_blocks, pattern, bracket)
+    rates = rate_term(pieces, rate_blocks, pattern, first)
     return call(
         functools.partial(step_kernel, True, "cell"),
         (middle, rates, entering, arrived, inflow, cross, emission, absorber, stream, crossways, populations),

time: 81.5 us -> 79.2 us (0.972)
  waiting for transfers between devices: 3.69 us -> 7.53 us
  local copies, waits for them, and re-layouts: 6.56 us -> 3.45 us
  blocking collectives: 26.5 us -> 23.7 us
    all_to_all x2, waiting for transfers between devices: 3.67 us -> 7.51 us  [swap(): return lax.all_to_all(value, 'cell', 0, 0, tiled=True)]
    unnamed x24 -> x26, local copies, waits for them, and re-layouts: 6.56 us -> 3.45 us
    all_to_all x1, blocking collectives: 26.5 us -> 23.7 us  [swap(): return lax.all_to_all(value, 'cell', 0, 0, tiled=True)]
    pallas_call x7 -> x8, Pallas kernels: 6.42 us -> 6.4 us  [call(): pl.pallas_call(body, out_shape=outs, in_specs=in_specs or vmem(len(args))...]
  transfers between devices with their start and end apart: 10 -> 10, of which waited for: 2 -> 2; matrix products, arithmetic and copies ran while one was open for 0% -> 0% of each run, Pallas kernels for 8% -> 9%
where the time goes in v8:
time: 79.2 us; the launch traced here: 78.8 us
  starting transfers between devices  31.4 us (40%)
  blocking collectives  23.7 us (30%)
  Pallas kernels  11.7 us (15%)
  waiting for transfers between devices  7.53 us (10%)
  local copies, waits for them, and re-layouts  3.45 us (4%)
  between operations  0.96 us (1%)
    all_to_all x1, blocking collectives, swap(): return lax.all_to_all(value, 'cell', 0, 0, tiled=True)  23.7 us
    all_to_all x2, starting transfers between devices, swap(): return lax.all_to_all(value, 'cell', 0, 0, tiled=True)  18.6 us
    all_to_all x2, waiting for transfers between devices, swap(): return lax.all_to_all(value, 'cell', 0, 0, tiled=True)  7.51 us
    ppermute x2, starting transfers between devices, shifted(): return lax.ppermute(value, axis, [(i, i + 1) for i in range(peers - 1)])  6.98 us
    pallas_call x8, Pallas kernels, call(): pl.pallas_call(body, out_shape=outs, in_specs=in_specs or vmem(len(args))...  6.4 us
    ppermute x6, starting transfers between devices, swap(): lax.ppermute(value, axis, [(i, i ^ apart) for i in range(lax.axis_size(ax...  5.89 us
    pallas_call x2, Pallas kernels, rate_term(): pl.pallas_call(functools.partial(rate_kernel, 'lev'), in_specs=[pl.BlockS...  5.31 us
    unnamed x26, local copies, waits for them, and re-layouts  3.45 us
  transfers between devices with their start and end apart: 10, of which 2 were waited for; matrix products, arithmetic and copies ran while one was open for 0% of the time, Pallas kernels for 9%

profile of v8, /device:TPU:2, one launch (start us, length us, event | category | flops | bytes accessed | tf_op | source)
XLA Modules:
  0.0 78.8 jit_solution(3567008918704839774)
XLA Ops:
  0.6 2.2 %shard_map.113 = (bf16[64,2048]{1,0:T(8,128)(2,1)}, bf16[16,2048]{1,0:T(8,128)(2,1)}, bf16[64,16,128]{2,1,0:T(8,128)(2,1)}) custom-call(f32[64,2048]{1,0:T(8,128)} %refs_10_.1, f32[1,2048]{1,0:T(1,128)} %bitcast.9, f32[1,2048]{1,0:T(1,128)} %bitcast.15, f32[1,64]{1,0:T(1,128)} %bitcast.21), custom_call_target="tpu_custom_call" | custom-call | flops 20971520000 | bytes 20971520000 | tf_op jit(solution)/shard_map/pallas_call | solution.py:305
  2.8 3.3 %collective-permute-start.1 = (bf16[64,2048]{1,0:T(8,128)(2,1)}, bf16[64,2048]{1,0:T(8,128)(2,1)S(1)}, u32[]{:S(2)}, u32[]{:S(2)}) collective-permute-start(bf16[64,2048]{1,0:T(8,128)(2,1)} %get-tuple-element.19.refs_0_), channel_id=1, source_target_pairs={{0,2},{1,3},{2,0},{3,1},{4,6},{5,7},{6,4},{7,5},{8,10},{9,11},{10,... | collective-permute-start | bytes 786440 | tf_op jit(solution)/shard_map/ppermute | solution.py:318
  6.1 12.1 %all-to-all-start = ((bf16[64,16,128]{2,1,0:T(8,128)(2,1)}), bf16[64,16,128]{2,1,0:T(8,128)(2,1)S(1)}, u32[]{:S(2)}, u32[]{:S(2)}) async-start(bf16[64,16,128]{2,1,0:T(8,128)(2,1)} %get-tuple-element.18), calls=%async_computation | async-start | bytes 524288 | tf_op jit(solution)/shard_map/all_to_all | solution.py:374
  18.2 0.1 collective-permute-start.2
  18.4 0.1 shard_map.114.refs_5_
  18.6 0.6 copy-done.12
  19.2 3.6 %collective-permute-start.3 = (bf16[16,2048]{1,0:T(8,128)(2,1)S(1)}, bf16[16,2048]{1,0:T(8,128)(2,1)S(1)}, u32[]{:S(2)}, u32[]{:S(2)}) collective-permute-start(bf16[16,2048]{1,0:T(8,128)(2,1)S(1)} %copy-done.12), channel_id=1, source_target_pairs={{0,4},{4,8},{8,12},{12,16},{16,20},{20,24},{24,28},{28,32},{32,36}... | collective-permute-start | bytes 196616 | tf_op jit(solution)/shard_map/ppermute | solution.py:341
  22.9 2.7 %shard_map.115.refs_1_ = f32[64,2048]{1,0:T(8,128)S(1)} custom-call(s32[6,16]{1,0:T(8,128)S(1)} %bitcast.19, bf16[64,2048]{1,0:T(8,128)(2,1)S(1)} %copy-done.4, bf16[64,2048]{1,0:T(8,128)(2,1)S(1)} %collective-permute-done.refs_1_, bf16[64,2048]{1,0:T(8,128)(2,1)S(1)} %collective-permute-done.1.refs_2_, bf16[64,2048]{1,0:T(8,128)(2,1)S(1)} %collective-permute-done.2.refs_3_, ...), custom_call_target="tpu_custom_call" | custom-call | flops 402653184 | bytes 6291456 | tf_op jit(solution)/shard_map/pallas_call | solution.py:326
  25.5 5.1 %all-to-all-done.arrived_ref = bf16[64,16,128]{2,1,0:T(8,128)(2,1)S(1)} async-done(((bf16[64,16,128]{2,1,0:T(8,128)(2,1)}), bf16[64,16,128]{2,1,0:T(8,128)(2,1)S(1)}, u32[]{:S(2)}, u32[]{:S(2)}) %all-to-all-start) | async-done | bytes 262176 | tf_op jit(solution)/shard_map/all_to_all | solution.py:374
  30.7 0.2 shard_map.116
  31.0 0.7 shard_map.117
  31.7 23.7 %all_to_all.15.swap_ref.arrived_ref = f32[64,16,128]{2,1,0:T(8,128)S(1)} all-to-all(f32[64,16,128]{2,1,0:T(8,128)S(1)} %get-tuple-element.27), channel_id=1, replica_groups=mesh['cell'=64,'lev'=4] {'cell'}, dimensions={0} | all-to-all | bytes 1048576 | tf_op jit(solution)/shard_map/all_to_all | solution.py:374
  55.4 0.3 shard_map.118
  55.7 1.9 %collective-permute-start.5 = (bf16[64,2048]{1,0:T(8,128)(2,1)S(1)}, bf16[64,2048]{1,0:T(8,128)(2,1)S(1)}, u32[]{:S(2)}, u32[]{:S(2)}) collective-permute-start(bf16[64,2048]{1,0:T(8,128)(2,1)S(1)} %get-tuple-element.29.refs_0_), channel_id=1, source_target_pairs={{0,2},{1,3},{2,0},{3,1},{4,6},{5,7},{6,4},{7,5},{8,10},{9,11},{10,... | collective-permute-start | bytes 786440 | tf_op jit(solution)/shard_map/ppermute | solution.py:318
  57.6 0.5 shard_map.120
  58.1 0.8 %shard_map.121 = f32[64,8,128]{2,1,0:T(8,128)} custom-call(f32[64,16,128]{2,1,0:T(8,128)S(1)} %all_to_all.15.swap_ref.arrived_ref, f32[64,8,128]{2,1,0:T(8,128)S(1)} %get-tuple-element.24.refs_2_.entered_ref, f32[64,8,128]{2,1,0:T(8,128)S(1)} %get-tuple-element.30.pass_ref, f32[64,8,128]{2,1,0:T(8,128)S(1)} %get-tuple-element.31.same_ref, ...), custom_call_target="tpu_custom_call" | custom-call | flops 524288 | bytes 524288 | tf_op jit(solution)/shard_map/pallas_call | solution.py:305
  58.9 6.4 %all-to-all-start.2 = ((f32[64,8,128]{2,1,0:T(8,128)}), f32[64,8,128]{2,1,0:T(8,128)S(1)}, u32[]{:S(2)}, u32[]{:S(2)}) async-start(f32[64,8,128]{2,1,0:T(8,128)} %shard_map.121), calls=%async_computation.2 | async-start | bytes 524288 | tf_op jit(solution)/shard_map/all_to_all | solution.py:374
  65.4 0.1 collective-permute-start.4
  65.5 0.5 collective-permute-start.6
  66.0 3.4 %collective-permute-start.7 = (bf16[16,2048]{1,0:T(8,128)(2,1)S(1)}, bf16[16,2048]{1,0:T(8,128)(2,1)S(1)}, u32[]{:S(2)}, u32[]{:S(2)}) collective-permute-start(bf16[16,2048]{1,0:T(8,128)(2,1)S(1)} %get-tuple-element.33), channel_id=1, source_target_pairs={{0,4},{4,8},{8,12},{12,16},{16,20},{20,24},{24,28},{28,32},{32,36}... | collective-permute-start | bytes 196616 | tf_op jit(solution)/shard_map/ppermute | solution.py:341
  69.4 2.8 %copy-done.1 = bf16[2,16,6,128,128]{4,3,2,1,0:T(8,128)(2,1)S(1)} copy-done((bf16[2,16,6,128,128]{4,3,2,1,0:T(8,128)(2,1)S(1)}, bf16[2,16,6,128,128]{4,3,2,1,0:T(8,128)(2,1)}, u32[]{:S(2)}) %copy-start.1) | copy-done | bytes 6291480
  72.2 2.7 %shard_map.119.refs_1_ = f32[64,2048]{1,0:T(8,128)S(1)} custom-call(s32[6,16]{1,0:T(8,128)S(1)} %bitcast.20, bf16[64,2048]{1,0:T(8,128)(2,1)S(1)} %get-tuple-element.29.refs_0_, bf16[64,2048]{1,0:T(8,128)(2,1)S(1)} %collective-permute-done.4.refs_1_, bf16[64,2048]{1,0:T(8,128)(2,1)S(1)} %collective-permute-done.5.refs_2_, ...), custom_call_target="tpu_custom_call" | custom-call | flops 402653184 | bytes 6291456 | tf_op jit(solution)/shard_map/pallas_call | solution.py:326
  74.8 2.4 %all-to-all-done.2.refs_2_ = f32[64,8,128]{2,1,0:T(8,128)S(1)} async-done(((f32[64,8,128]{2,1,0:T(8,128)}), f32[64,8,128]{2,1,0:T(8,128)S(1)}, u32[]{:S(2)}, u32[]{:S(2)}) %all-to-all-start.2) | async-done | bytes 262176 | tf_op jit(solution)/shard_map/all_to_all | solution.py:374
  77.2 1.6 %shard_map.122 = (f32[64,2048]{1,0:T(8,128)}, f32[64,2048]{1,0:T(8,128)}) custom-call(f32[64,2048]{1,0:T(8,128)S(1)} %get-tuple-element.28.refs_0_, f32[64,2048]{1,0:T(8,128)S(1)} %shard_map.119.refs_1_, f32[64,8,128]{2,1,0:T(8,128)S(1)} %all-to-all-done.2.refs_2_, bf16[16,2048]{1,0:T(8,128)(2,1)S(1)} %collective-permute-done.7.refs_3_, ...), custom_call_target="tpu_custom_call" | custom-call | flops 2621440 | bytes 2621440 | tf_op jit(solution)/shard_map/pallas_call | solution.py:305
  (33 shorter events, 0.1 us)
Async XLA Ops:
  0.6 17.7 %copy-start.11 = (s32[64]{0:T(128)S(1)}, s32[64]{0:T(128)}, u32[]{:S(2)}) copy-start(s32[64]{0:T(128)} %param.13) | copy-start | bytes 772
  2.8 15.4 %collective-permute-start.1 = (bf16[64,2048]{1,0:T(8,128)(2,1)}, bf16[64,2048]{1,0:T(8,128)(2,1)S(1)}, u32[]{:S(2)}, u32[]{:S(2)}) collective-permute-start(bf16[64,2048]{1,0:T(8,128)(2,1)} %get-tuple-element.19.refs_0_), channel_id=1, source_target_pairs={{0,2},{1,3},{2,0},{3,1},{4,6},{5,7},{6,4},{7,5},{8,10},{9,11},{10,... | collective-permute-start | bytes 786440 | tf_op jit(solution)/shard_map/ppermute | solution.py:318
  6.1 16.7 %collective-permute-start = (bf16[64,2048]{1,0:T(8,128)(2,1)}, bf16[64,2048]{1,0:T(8,128)(2,1)S(1)}, u32[]{:S(2)}, u32[]{:S(2)}) collective-permute-start(bf16[64,2048]{1,0:T(8,128)(2,1)} %get-tuple-element.19.refs_0_), channel_id=1, source_target_pairs={{0,1},{1,0},{2,3},{3,2},{4,5},{5,4},{6,7},{7,6},{8,9},{9,8},{10,11... | collective-permute-start | bytes 786440 | tf_op jit(solution)/shard_map/ppermute | solution.py:318
  6.1 24.6 %all-to-all-start = ((bf16[64,16,128]{2,1,0:T(8,128)(2,1)}), bf16[64,16,128]{2,1,0:T(8,128)(2,1)S(1)}, u32[]{:S(2)}, u32[]{:S(2)}) async-start(bf16[64,16,128]{2,1,0:T(8,128)(2,1)} %get-tuple-element.18), calls=%async_computation | async-start | bytes 524288 | tf_op jit(solution)/shard_map/all_to_all | solution.py:374
  18.2 4.6 %collective-permute-start.2 = (bf16[64,2048]{1,0:T(8,128)(2,1)S(1)}, bf16[64,2048]{1,0:T(8,128)(2,1)S(1)}, u32[]{:S(2)}, u32[]{:S(2)}) collective-permute-start(bf16[64,2048]{1,0:T(8,128)(2,1)S(1)} %collective-permute-done.1.refs_2_), channel_id=1, source_target_pairs={{0,1},{1,0},{2,3},{3,2},{4,5},{5,4},{6,7},{7,6},{8,9},{9,8},{10,11... | collective-permute-start | bytes 786440 | tf_op jit(solution)/shard_map/ppermute | solution.py:318
  18.3 0.8 %copy-start.12 = (bf16[16,2048]{1,0:T(8,128)(2,1)S(1)}, bf16[16,2048]{1,0:T(8,128)(2,1)}, u32[]{:S(2)}) copy-start(bf16[16,2048]{1,0:T(8,128)(2,1)} %get-tuple-element.25) | copy-start | bytes 196612
  18.4 4.5 %copy-start = (bf16[2,16,6,128,128]{4,3,2,1,0:T(8,128)(2,1)S(1)}, bf16[2,16,6,128,128]{4,3,2,1,0:T(8,128)(2,1)}, u32[]{:S(2)}) copy-start(bf16[2,16,6,128,128]{4,3,2,1,0:T(8,128)(2,1)} %refs_4_.6) | copy-start | bytes 18874372
  18.4 4.5 %copy-start.4 = (bf16[64,2048]{1,0:T(8,128)(2,1)S(1)}, bf16[64,2048]{1,0:T(8,128)(2,1)}, u32[]{:S(2)}) copy-start(bf16[64,2048]{1,0:T(8,128)(2,1)} %get-tuple-element.19.refs_0_) | copy-start | bytes 786436
  18.4 4.5 %copy-start.7 = (s32[16,6]{0,1:T(8,128)S(1)}, s32[16,6]{0,1:T(8,128)}, u32[]{:S(2)}) copy-start(s32[16,6]{0,1:T(8,128)} %param.12) | copy-start | bytes 1156
  18.5 12.2 %copy-start.5 = (f32[2048]{0:T(1024)S(1)}, f32[2048]{0:T(1024)}, u32[]{:S(2)}) copy-start(f32[2048]{0:T(1024)} %param.14) | copy-start | bytes 24580
  18.5 12.4 %copy-start.2 = (f32[64,2048]{1,0:T(8,128)S(1)}, f32[64,2048]{1,0:T(8,128)}, u32[]{:S(2)}) copy-start(f32[64,2048]{1,0:T(8,128)} %refs_10_.1) | copy-start | bytes 1572868
  18.5 12.4 %copy-start.3 = (f32[16,2048]{1,0:T(8,128)S(1)}, f32[16,2048]{1,0:T(8,128)}, u32[]{:S(2)}) copy-start(f32[16,2048]{1,0:T(8,128)} %refs_4_.7) | copy-start | bytes 393220
  18.5 12.4 %copy-start.6 = (f32[2048]{0:T(1024)S(1)}, f32[2048]{0:T(1024)}, u32[]{:S(2)}) copy-start(f32[2048]{0:T(1024)} %param.15) | copy-start | bytes 24580
  18.5 12.4 %copy-start.8 = (f32[64]{0:T(128)S(1)}, f32[64]{0:T(128)}, u32[]{:S(2)}) copy-start(f32[64]{0:T(128)} %param.16) | copy-start | bytes 772
  18.6 12.4 %copy-start.9 = (f32[64]{0:T(128)S(1)}, f32[64]{0:T(128)}, u32[]{:S(2)}) copy-start(f32[64]{0:T(128)} %param.17) | copy-start | bytes 772
  18.6 12.4 %copy-start.10 = (f32[64]{0:T(128)S(1)}, f32[64]{0:T(128)}, u32[]{:S(2)}) copy-start(f32[64]{0:T(128)} %param.18) | copy-start | bytes 772
  19.2 11.7 %collective-permute-start.3 = (bf16[16,2048]{1,0:T(8,128)(2,1)S(1)}, bf16[16,2048]{1,0:T(8,128)(2,1)S(1)}, u32[]{:S(2)}, u32[]{:S(2)}) collective-permute-start(bf16[16,2048]{1,0:T(8,128)(2,1)S(1)} %copy-done.12), channel_id=1, source_target_pairs={{0,4},{4,8},{8,12},{12,16},{16,20},{20,24},{24,28},{28,32},{32,36}... | collective-permute-start | bytes 196616 | tf_op jit(solution)/shard_map/ppermute | solution.py:341
  55.7 9.8 %collective-permute-start.5 = (bf16[64,2048]{1,0:T(8,128)(2,1)S(1)}, bf16[64,2048]{1,0:T(8,128)(2,1)S(1)}, u32[]{:S(2)}, u32[]{:S(2)}) collective-permute-start(bf16[64,2048]{1,0:T(8,128)(2,1)S(1)} %get-tuple-element.29.refs_0_), channel_id=1, source_target_pairs={{0,2},{1,3},{2,0},{3,1},{4,6},{5,7},{6,4},{7,5},{8,10},{9,11},{10,... | collective-permute-start | bytes 786440 | tf_op jit(solution)/shard_map/ppermute | solution.py:318
  58.9 18.3 %all-to-all-start.2 = ((f32[64,8,128]{2,1,0:T(8,128)}), f32[64,8,128]{2,1,0:T(8,128)S(1)}, u32[]{:S(2)}, u32[]{:S(2)}) async-start(f32[64,8,128]{2,1,0:T(8,128)} %shard_map.121), calls=%async_computation.2 | async-start | bytes 524288 | tf_op jit(solution)/shard_map/all_to_all | solution.py:374
  65.4 4.0 %collective-permute-start.4 = (bf16[64,2048]{1,0:T(8,128)(2,1)S(1)}, bf16[64,2048]{1,0:T(8,128)(2,1)S(1)}, u32[]{:S(2)}, u32[]{:S(2)}) collective-permute-start(bf16[64,2048]{1,0:T(8,128)(2,1)S(1)} %get-tuple-element.29.refs_0_), channel_id=1, source_target_pairs={{0,1},{1,0},{2,3},{3,2},{4,5},{5,4},{6,7},{7,6},{8,9},{9,8},{10,11... | collective-permute-start | bytes 786440 | tf_op jit(solution)/shard_map/ppermute | solution.py:318
  65.5 3.9 %collective-permute-start.6 = (bf16[64,2048]{1,0:T(8,128)(2,1)S(1)}, bf16[64,2048]{1,0:T(8,128)(2,1)S(1)}, u32[]{:S(2)}, u32[]{:S(2)}) collective-permute-start(bf16[64,2048]{1,0:T(8,128)(2,1)S(1)} %collective-permute-done.5.refs_2_), channel_id=1, source_target_pairs={{0,1},{1,0},{2,3},{3,2},{4,5},{5,4},{6,7},{7,6},{8,9},{9,8},{10,11... | collective-permute-start | bytes 786440 | tf_op jit(solution)/shard_map/ppermute | solution.py:318
  66.0 8.8 %collective-permute-start.7 = (bf16[16,2048]{1,0:T(8,128)(2,1)S(1)}, bf16[16,2048]{1,0:T(8,128)(2,1)S(1)}, u32[]{:S(2)}, u32[]{:S(2)}) collective-permute-start(bf16[16,2048]{1,0:T(8,128)(2,1)S(1)} %get-tuple-element.33), channel_id=1, source_target_pairs={{0,4},{4,8},{8,12},{12,16},{16,20},{20,24},{24,28},{28,32},{32,36}... | collective-permute-start | bytes 196616 | tf_op jit(solution)/shard_map/ppermute | solution.py:341
  69.4 2.8 %copy-start.1 = (bf16[2,16,6,128,128]{4,3,2,1,0:T(8,128)(2,1)S(1)}, bf16[2,16,6,128,128]{4,3,2,1,0:T(8,128)(2,1)}, u32[]{:S(2)}) copy-start(bf16[2,16,6,128,128]{4,3,2,1,0:T(8,128)(2,1)} %refs_4_.6) | copy-start | bytes 18874372

commit v9 on v8

--- a/solution.py
+++ b/solution.py
@@ -14,6 +14,7 @@
 PARTS = 2
 FIRST = 57
 LONG = 40000
+CHUNKS = 4
 time_step = 0.25
 
 
@@ -109,22 +110,31 @@
 
 def first_kernel(p_hbm, cross_hbm, emission_hbm, absorber_hbm, q_ref, last_ref, exit_ref, *scratch):
     sems = scratch[-1]
-    copies = [
-        pltpu.make_async_copy(source, target, sems.at[i])
+    p_ref, cross_ref, emission_ref, absorber_ref = scratch[:-1]
+    small = [
+        pltpu.make_async_copy(source, target, sems.at[CHUNKS + i])
         for i, (source, target) in enumerate(
-            zip((p_hbm, cross_hbm, emission_hbm, absorber_hbm), scratch[:-1])
+            ((absorber_hbm, absorber_ref), (cross_hbm, cross_ref), (emission_hbm, emission_ref))
         )
     ]
-    for copy in copies:
+    width = p_ref.shape[1] // CHUNKS
+    large = [
+        pltpu.make_async_copy(
+            p_hbm.at[:, c * width : (c + 1) * width], p_ref.at[:, c * width : (c + 1) * width], sems.at[c]
+        )
+        for c in range(CHUNKS)
+    ]
+    for copy in (*small, *large):
         copy.start()
-    for copy in copies:
+    for copy in small:
         copy.wait()
-    p_ref, cross_ref, emission_ref, absorber_ref = scratch[:-1]
     absorber = column(absorber_ref[...])
     depths = depth_tiles(absorber)
     groups = p_ref.shape[1] // LANES
     for g in range(groups):
         at = slice(g * LANES, (g + 1) * LANES)
+        if g * LANES % width == 0:
+            large[g * LANES // width].wait()
         p = p_ref[:, at]
         q = p.astype(jnp.bfloat16)
         q_ref[:, at] = q
@@ -239,6 +249,7 @@
     backward_y = layers(jnp.minimum(along_y, 0.0))
     inlet = lax.axis_index(axis) == 0
     groups = p_ref.shape[1] // LANES
+    copies = []
     for g in range(groups):
         at = slice(g * LANES, (g + 1) * LANES)
         p = layers(p_ref[:, at])
@@ -252,12 +263,22 @@
         rates = layers(rate_ref[:, at])
         tendency = [q - e + a + v for q, e, a, v in zip(rates, emitted, absorbed, carried)]
         if final:
-            start_ref, updated_ref, absorption_ref = refs[10:]
+            start_ref, updated_hbm, absorption_hbm, updated_ref, absorption_ref, sems = refs[10:]
             start = layers(start_ref[:, at])
             for k, rate in enumerate(tendency):
                 here = slice(k * NY, (k + 1) * NY)
                 updated_ref[here, at] = 0.5 * (start[k] + p[k] + time_step * rate)
                 absorption_ref[here, at] = absorbed[k]
+            width = p_ref.shape[1] // CHUNKS
+            if (g + 1) * LANES % width == 0:
+                c = (g + 1) * LANES // width - 1
+                part = slice(c * width, (c + 1) * width)
+                for i, (source, target) in enumerate(
+                    ((updated_ref, updated_hbm), (absorption_ref, absorption_hbm))
+                ):
+                    copy = pltpu.make_async_copy(source.at[:, part], target.at[:, part], sems.at[i, c])
+                    copy.start()
+                    copies.append(copy)
         else:
             middle_ref, swap_ref = refs[10:]
             middle = [value + time_step * rate for value, rate in zip(p, tendency)]
@@ -267,6 +288,8 @@
             for k, tile in enumerate(leaving):
                 swap_ref[k * groups + g, :ROWS] = enter_ref[k * groups + g]
                 swap_ref[k * groups + g, ROWS:] = tile
+    for copy in copies:
+        copy.wait()
 
 
 def middle_kernel(part_ref, swap_ref, cross_ref, absorber_ref, middle_ref, q_ref, last_ref):
@@ -301,12 +324,12 @@
 LIMIT = pltpu.CompilerParams(vmem_limit_bytes=24 * 2**20)
 
 
-def call(body, args, outs, cost, scratch=(), in_specs=None, params=LIMIT):
+def call(body, args, outs, cost, scratch=(), in_specs=None, params=LIMIT, out_specs=None):
     return pl.pallas_call(
         body,
         out_shape=outs,
         in_specs=in_specs or vmem(len(args)),
-        out_specs=vmem(len(outs)),
+        out_specs=out_specs or vmem(len(outs)),
         scratch_shapes=scratch,
         compiler_params=params,
         cost_estimate=pl.CostEstimate(flops=cost, bytes_accessed=cost, transcendentals=0),
@@ -380,7 +403,7 @@
         (rounded, layer, jax.ShapeDtypeStruct((strips, 2 * ROWS, LANES), jnp.bfloat16)),
         LONG * size,
         [pltpu.VMEM(value.shape, value.dtype) for value in sources]
-        + [pltpu.SemaphoreType.DMA((len(sources),))],
+        + [pltpu.SemaphoreType.DMA((len(sources) - 1 + CHUNKS,))],
         [pl.BlockSpec(memory_space=pl.ANY)] * len(sources),
         pltpu.CompilerParams(vmem_limit_bytes=FIRST * 2**20),
     )
@@ -435,6 +458,8 @@
         (middle, rates, entering, arrived, inflow, cross, emission, absorber, stream, crossways, populations),
         (field, field),
         5 * size,
+        [pltpu.VMEM(field.shape, field.dtype)] * 2 + [pltpu.SemaphoreType.DMA((2, CHUNKS))],
+        out_specs=[pl.BlockSpec(memory_space=pl.ANY)] * 2,
     )
 
 

time: 79.2 us -> 78.9 us (level)
  no operation moved by 1% of the time
where the time goes in v9:
time: 78.9 us; the launch traced here: 78.5 us
  starting transfers between devices  31.4 us (40%)
  blocking collectives  23.7 us (30%)
  Pallas kernels  11.4 us (14%)
  waiting for transfers between devices  7.52 us (10%)
  local copies, waits for them, and re-layouts  3.45 us (4%)
  between operations  0.96 us (1%)
    all_to_all x1, blocking collectives, swap(): return lax.all_to_all(value, 'cell', 0, 0, tiled=True)  23.7 us
    all_to_all x2, starting transfers between devices, swap(): return lax.all_to_all(value, 'cell', 0, 0, tiled=True)  18.6 us
    all_to_all x2, waiting for transfers between devices, swap(): return lax.all_to_all(value, 'cell', 0, 0, tiled=True)  7.5 us
    ppermute x2, starting transfers between devices, shifted(): return lax.ppermute(value, axis, [(i, i + 1) for i in range(peers - 1)])  6.98 us
    pallas_call x8, Pallas kernels, call(): pl.pallas_call(body, out_shape=outs, in_specs=in_specs or vmem(len(args))...  6.11 us
    ppermute x6, starting transfers between devices, swap(): lax.ppermute(value, axis, [(i, i ^ apart) for i in range(lax.axis_size(ax...  5.89 us
    pallas_call x2, Pallas kernels, rate_term(): pl.pallas_call(functools.partial(rate_kernel, 'lev'), in_specs=[pl.BlockS...  5.32 us
    unnamed x26, local copies, waits for them, and re-layouts  3.45 us
  transfers between devices with their start and end apart: 10, of which 2 were waited for; matrix products, arithmetic and copies ran while one was open for 0% of the time, Pallas kernels for 9%

profile of v9, /device:TPU:2, one launch (start us, length us, event | category | flops | bytes accessed | tf_op | source)
XLA Modules:
  0.0 78.5 jit_solution(16297775162533234757)
XLA Ops:
  0.6 2.0 %shard_map.113 = (bf16[64,2048]{1,0:T(8,128)(2,1)}, bf16[16,2048]{1,0:T(8,128)(2,1)}, bf16[64,16,128]{2,1,0:T(8,128)(2,1)}) custom-call(f32[64,2048]{1,0:T(8,128)} %refs_10_.1, f32[1,2048]{1,0:T(1,128)} %bitcast.9, f32[1,2048]{1,0:T(1,128)} %bitcast.15, f32[1,64]{1,0:T(1,128)} %bitcast.21), custom_call_target="tpu_custom_call" | custom-call | flops 20971520000 | bytes 20971520000 | tf_op jit(solution)/shard_map/pallas_call | solution.py:328
  2.7 3.3 %collective-permute-start.1 = (bf16[64,2048]{1,0:T(8,128)(2,1)}, bf16[64,2048]{1,0:T(8,128)(2,1)S(1)}, u32[]{:S(2)}, u32[]{:S(2)}) collective-permute-start(bf16[64,2048]{1,0:T(8,128)(2,1)} %get-tuple-element.19.refs_0_), channel_id=1, source_target_pairs={{0,2},{1,3},{2,0},{3,1},{4,6},{5,7},{6,4},{7,5},{8,10},{9,11},{10,... | collective-permute-start | bytes 786440 | tf_op jit(solution)/shard_map/ppermute | solution.py:341
  6.0 12.1 %all-to-all-start = ((bf16[64,16,128]{2,1,0:T(8,128)(2,1)}), bf16[64,16,128]{2,1,0:T(8,128)(2,1)S(1)}, u32[]{:S(2)}, u32[]{:S(2)}) async-start(bf16[64,16,128]{2,1,0:T(8,128)(2,1)} %get-tuple-element.18), calls=%async_computation | async-start | bytes 524288 | tf_op jit(solution)/shard_map/all_to_all | solution.py:397
  18.1 0.1 collective-permute-start.2
  18.3 0.1 shard_map.114.refs_5_
  18.5 0.6 copy-done.12
  19.1 3.6 %collective-permute-start.3 = (bf16[16,2048]{1,0:T(8,128)(2,1)S(1)}, bf16[16,2048]{1,0:T(8,128)(2,1)S(1)}, u32[]{:S(2)}, u32[]{:S(2)}) collective-permute-start(bf16[16,2048]{1,0:T(8,128)(2,1)S(1)} %copy-done.12), channel_id=1, source_target_pairs={{0,4},{4,8},{8,12},{12,16},{16,20},{20,24},{24,28},{28,32},{32,36}... | collective-permute-start | bytes 196616 | tf_op jit(solution)/shard_map/ppermute | solution.py:364
  22.8 2.7 %shard_map.115.refs_1_ = f32[64,2048]{1,0:T(8,128)S(1)} custom-call(s32[6,16]{1,0:T(8,128)S(1)} %bitcast.19, bf16[64,2048]{1,0:T(8,128)(2,1)S(1)} %copy-done.4, bf16[64,2048]{1,0:T(8,128)(2,1)S(1)} %collective-permute-done.refs_1_, bf16[64,2048]{1,0:T(8,128)(2,1)S(1)} %collective-permute-done.1.refs_2_, bf16[64,2048]{1,0:T(8,128)(2,1)S(1)} %collective-permute-done.2.refs_3_, ...), custom_call_target="tpu_custom_call" | custom-call | flops 402653184 | bytes 6291456 | tf_op jit(solution)/shard_map/pallas_call | solution.py:349
  25.4 5.1 %all-to-all-done.arrived_ref = bf16[64,16,128]{2,1,0:T(8,128)(2,1)S(1)} async-done(((bf16[64,16,128]{2,1,0:T(8,128)(2,1)}), bf16[64,16,128]{2,1,0:T(8,128)(2,1)S(1)}, u32[]{:S(2)}, u32[]{:S(2)}) %all-to-all-start) | async-done | bytes 262176 | tf_op jit(solution)/shard_map/all_to_all | solution.py:397
  30.6 0.2 shard_map.116
  30.9 0.7 shard_map.117
  31.6 23.7 %all_to_all.15.swap_ref.arrived_ref = f32[64,16,128]{2,1,0:T(8,128)S(1)} all-to-all(f32[64,16,128]{2,1,0:T(8,128)S(1)} %get-tuple-element.27), channel_id=1, replica_groups=mesh['cell'=64,'lev'=4] {'cell'}, dimensions={0} | all-to-all | bytes 1048576 | tf_op jit(solution)/shard_map/all_to_all | solution.py:397
  55.3 0.3 shard_map.118
  55.6 1.9 %collective-permute-start.5 = (bf16[64,2048]{1,0:T(8,128)(2,1)S(1)}, bf16[64,2048]{1,0:T(8,128)(2,1)S(1)}, u32[]{:S(2)}, u32[]{:S(2)}) collective-permute-start(bf16[64,2048]{1,0:T(8,128)(2,1)S(1)} %get-tuple-element.29.refs_0_), channel_id=1, source_target_pairs={{0,2},{1,3},{2,0},{3,1},{4,6},{5,7},{6,4},{7,5},{8,10},{9,11},{10,... | collective-permute-start | bytes 786440 | tf_op jit(solution)/shard_map/ppermute | solution.py:341
  57.5 0.5 shard_map.120
  58.0 0.8 %shard_map.121 = f32[64,8,128]{2,1,0:T(8,128)} custom-call(f32[64,16,128]{2,1,0:T(8,128)S(1)} %all_to_all.15.swap_ref.arrived_ref, f32[64,8,128]{2,1,0:T(8,128)S(1)} %get-tuple-element.24.refs_2_.entered_ref, f32[64,8,128]{2,1,0:T(8,128)S(1)} %get-tuple-element.30.pass_ref, f32[64,8,128]{2,1,0:T(8,128)S(1)} %get-tuple-element.31.same_ref, ...), custom_call_target="tpu_custom_call" | custom-call | flops 524288 | bytes 524288 | tf_op jit(solution)/shard_map/pallas_call | solution.py:328
  58.8 6.4 %all-to-all-start.2 = ((f32[64,8,128]{2,1,0:T(8,128)}), f32[64,8,128]{2,1,0:T(8,128)S(1)}, u32[]{:S(2)}, u32[]{:S(2)}) async-start(f32[64,8,128]{2,1,0:T(8,128)} %shard_map.121), calls=%async_computation.2 | async-start | bytes 524288 | tf_op jit(solution)/shard_map/all_to_all | solution.py:397
  65.3 0.1 collective-permute-start.4
  65.4 0.5 collective-permute-start.6
  65.9 3.4 %collective-permute-start.7 = (bf16[16,2048]{1,0:T(8,128)(2,1)S(1)}, bf16[16,2048]{1,0:T(8,128)(2,1)S(1)}, u32[]{:S(2)}, u32[]{:S(2)}) collective-permute-start(bf16[16,2048]{1,0:T(8,128)(2,1)S(1)} %get-tuple-element.33), channel_id=1, source_target_pairs={{0,4},{4,8},{8,12},{12,16},{16,20},{20,24},{24,28},{28,32},{32,36}... | collective-permute-start | bytes 196616 | tf_op jit(solution)/shard_map/ppermute | solution.py:364
  69.3 2.8 %copy-done.1 = bf16[2,16,6,128,128]{4,3,2,1,0:T(8,128)(2,1)S(1)} copy-done((bf16[2,16,6,128,128]{4,3,2,1,0:T(8,128)(2,1)S(1)}, bf16[2,16,6,128,128]{4,3,2,1,0:T(8,128)(2,1)}, u32[]{:S(2)}) %copy-start.1) | copy-done | bytes 6291480
  72.1 2.7 %shard_map.119.refs_1_ = f32[64,2048]{1,0:T(8,128)S(1)} custom-call(s32[6,16]{1,0:T(8,128)S(1)} %bitcast.20, bf16[64,2048]{1,0:T(8,128)(2,1)S(1)} %get-tuple-element.29.refs_0_, bf16[64,2048]{1,0:T(8,128)(2,1)S(1)} %collective-permute-done.4.refs_1_, bf16[64,2048]{1,0:T(8,128)(2,1)S(1)} %collective-permute-done.5.refs_2_, ...), custom_call_target="tpu_custom_call" | custom-call | flops 402653184 | bytes 6291456 | tf_op jit(solution)/shard_map/pallas_call | solution.py:349
  74.7 2.4 %all-to-all-done.2.refs_2_ = f32[64,8,128]{2,1,0:T(8,128)S(1)} async-done(((f32[64,8,128]{2,1,0:T(8,128)}), f32[64,8,128]{2,1,0:T(8,128)S(1)}, u32[]{:S(2)}, u32[]{:S(2)}) %all-to-all-start.2) | async-done | bytes 262176 | tf_op jit(solution)/shard_map/all_to_all | solution.py:397
  77.1 1.4 %shard_map.122 = (f32[64,2048]{1,0:T(8,128)}, f32[64,2048]{1,0:T(8,128)}) custom-call(f32[64,2048]{1,0:T(8,128)S(1)} %get-tuple-element.28.refs_0_, f32[64,2048]{1,0:T(8,128)S(1)} %shard_map.119.refs_1_, f32[64,8,128]{2,1,0:T(8,128)S(1)} %all-to-all-done.2.refs_2_, bf16[16,2048]{1,0:T(8,128)(2,1)S(1)} %collective-permute-done.7.refs_3_, ...), custom_call_target="tpu_custom_call" | custom-call | flops 2621440 | bytes 2621440 | tf_op jit(solution)/shard_map/pallas_call | solution.py:328
  (33 shorter events, 0.1 us)
Async XLA Ops:
  0.6 17.6 %copy-start.11 = (s32[64]{0:T(128)S(1)}, s32[64]{0:T(128)}, u32[]{:S(2)}) copy-start(s32[64]{0:T(128)} %param.13) | copy-start | bytes 772
  2.7 15.4 %collective-permute-start.1 = (bf16[64,2048]{1,0:T(8,128)(2,1)}, bf16[64,2048]{1,0:T(8,128)(2,1)S(1)}, u32[]{:S(2)}, u32[]{:S(2)}) collective-permute-start(bf16[64,2048]{1,0:T(8,128)(2,1)} %get-tuple-element.19.refs_0_), channel_id=1, source_target_pairs={{0,2},{1,3},{2,0},{3,1},{4,6},{5,7},{6,4},{7,5},{8,10},{9,11},{10,... | collective-permute-start | bytes 786440 | tf_op jit(solution)/shard_map/ppermute | solution.py:341
  6.0 16.7 %collective-permute-start = (bf16[64,2048]{1,0:T(8,128)(2,1)}, bf16[64,2048]{1,0:T(8,128)(2,1)S(1)}, u32[]{:S(2)}, u32[]{:S(2)}) collective-permute-start(bf16[64,2048]{1,0:T(8,128)(2,1)} %get-tuple-element.19.refs_0_), channel_id=1, source_target_pairs={{0,1},{1,0},{2,3},{3,2},{4,5},{5,4},{6,7},{7,6},{8,9},{9,8},{10,11... | collective-permute-start | bytes 786440 | tf_op jit(solution)/shard_map/ppermute | solution.py:341
  6.0 24.6 %all-to-all-start = ((bf16[64,16,128]{2,1,0:T(8,128)(2,1)}), bf16[64,16,128]{2,1,0:T(8,128)(2,1)S(1)}, u32[]{:S(2)}, u32[]{:S(2)}) async-start(bf16[64,16,128]{2,1,0:T(8,128)(2,1)} %get-tuple-element.18), calls=%async_computation | async-start | bytes 524288 | tf_op jit(solution)/shard_map/all_to_all | solution.py:397
  18.1 4.6 %collective-permute-start.2 = (bf16[64,2048]{1,0:T(8,128)(2,1)S(1)}, bf16[64,2048]{1,0:T(8,128)(2,1)S(1)}, u32[]{:S(2)}, u32[]{:S(2)}) collective-permute-start(bf16[64,2048]{1,0:T(8,128)(2,1)S(1)} %collective-permute-done.1.refs_2_), channel_id=1, source_target_pairs={{0,1},{1,0},{2,3},{3,2},{4,5},{5,4},{6,7},{7,6},{8,9},{9,8},{10,11... | collective-permute-start | bytes 786440 | tf_op jit(solution)/shard_map/ppermute | solution.py:341
  18.2 0.8 %copy-start.12 = (bf16[16,2048]{1,0:T(8,128)(2,1)S(1)}, bf16[16,2048]{1,0:T(8,128)(2,1)}, u32[]{:S(2)}) copy-start(bf16[16,2048]{1,0:T(8,128)(2,1)} %get-tuple-element.25) | copy-start | bytes 196612
  18.2 4.5 %copy-start = (bf16[2,16,6,128,128]{4,3,2,1,0:T(8,128)(2,1)S(1)}, bf16[2,16,6,128,128]{4,3,2,1,0:T(8,128)(2,1)}, u32[]{:S(2)}) copy-start(bf16[2,16,6,128,128]{4,3,2,1,0:T(8,128)(2,1)} %refs_4_.6) | copy-start | bytes 18874372
  18.3 4.5 %copy-start.4 = (bf16[64,2048]{1,0:T(8,128)(2,1)S(1)}, bf16[64,2048]{1,0:T(8,128)(2,1)}, u32[]{:S(2)}) copy-start(bf16[64,2048]{1,0:T(8,128)(2,1)} %get-tuple-element.19.refs_0_) | copy-start | bytes 786436
  18.3 4.5 %copy-start.7 = (s32[16,6]{0,1:T(8,128)S(1)}, s32[16,6]{0,1:T(8,128)}, u32[]{:S(2)}) copy-start(s32[16,6]{0,1:T(8,128)} %param.12) | copy-start | bytes 1156
  18.4 12.2 %copy-start.5 = (f32[2048]{0:T(1024)S(1)}, f32[2048]{0:T(1024)}, u32[]{:S(2)}) copy-start(f32[2048]{0:T(1024)} %param.14) | copy-start | bytes 24580
  18.4 12.4 %copy-start.2 = (f32[64,2048]{1,0:T(8,128)S(1)}, f32[64,2048]{1,0:T(8,128)}, u32[]{:S(2)}) copy-start(f32[64,2048]{1,0:T(8,128)} %refs_10_.1) | copy-start | bytes 1572868
  18.4 12.4 %copy-start.3 = (f32[16,2048]{1,0:T(8,128)S(1)}, f32[16,2048]{1,0:T(8,128)}, u32[]{:S(2)}) copy-start(f32[16,2048]{1,0:T(8,128)} %refs_4_.7) | copy-start | bytes 393220
  18.4 12.4 %copy-start.6 = (f32[2048]{0:T(1024)S(1)}, f32[2048]{0:T(1024)}, u32[]{:S(2)}) copy-start(f32[2048]{0:T(1024)} %param.15) | copy-start | bytes 24580
  18.4 12.4 %copy-start.8 = (f32[64]{0:T(128)S(1)}, f32[64]{0:T(128)}, u32[]{:S(2)}) copy-start(f32[64]{0:T(128)} %param.16) | copy-start | bytes 772
  18.4 12.4 %copy-start.9 = (f32[64]{0:T(128)S(1)}, f32[64]{0:T(128)}, u32[]{:S(2)}) copy-start(f32[64]{0:T(128)} %param.17) | copy-start | bytes 772
  18.5 12.4 %copy-start.10 = (f32[64]{0:T(128)S(1)}, f32[64]{0:T(128)}, u32[]{:S(2)}) copy-start(f32[64]{0:T(128)} %param.18) | copy-start | bytes 772
  19.1 11.7 %collective-permute-start.3 = (bf16[16,2048]{1,0:T(8,128)(2,1)S(1)}, bf16[16,2048]{1,0:T(8,128)(2,1)S(1)}, u32[]{:S(2)}, u32[]{:S(2)}) collective-permute-start(bf16[16,2048]{1,0:T(8,128)(2,1)S(1)} %copy-done.12), channel_id=1, source_target_pairs={{0,4},{4,8},{8,12},{12,16},{16,20},{20,24},{24,28},{28,32},{32,36}... | collective-permute-start | bytes 196616 | tf_op jit(solution)/shard_map/ppermute | solution.py:364
  55.6 9.8 %collective-permute-start.5 = (bf16[64,2048]{1,0:T(8,128)(2,1)S(1)}, bf16[64,2048]{1,0:T(8,128)(2,1)S(1)}, u32[]{:S(2)}, u32[]{:S(2)}) collective-permute-start(bf16[64,2048]{1,0:T(8,128)(2,1)S(1)} %get-tuple-element.29.refs_0_), channel_id=1, source_target_pairs={{0,2},{1,3},{2,0},{3,1},{4,6},{5,7},{6,4},{7,5},{8,10},{9,11},{10,... | collective-permute-start | bytes 786440 | tf_op jit(solution)/shard_map/ppermute | solution.py:341
  58.8 18.3 %all-to-all-start.2 = ((f32[64,8,128]{2,1,0:T(8,128)}), f32[64,8,128]{2,1,0:T(8,128)S(1)}, u32[]{:S(2)}, u32[]{:S(2)}) async-start(f32[64,8,128]{2,1,0:T(8,128)} %shard_map.121), calls=%async_computation.2 | async-start | bytes 524288 | tf_op jit(solution)/shard_map/all_to_all | solution.py:397
  65.3 4.0 %collective-permute-start.4 = (bf16[64,2048]{1,0:T(8,128)(2,1)S(1)}, bf16[64,2048]{1,0:T(8,128)(2,1)S(1)}, u32[]{:S(2)}, u32[]{:S(2)}) collective-permute-start(bf16[64,2048]{1,0:T(8,128)(2,1)S(1)} %get-tuple-element.29.refs_0_), channel_id=1, source_target_pairs={{0,1},{1,0},{2,3},{3,2},{4,5},{5,4},{6,7},{7,6},{8,9},{9,8},{10,11... | collective-permute-start | bytes 786440 | tf_op jit(solution)/shard_map/ppermute | solution.py:341
  65.4 3.9 %collective-permute-start.6 = (bf16[64,2048]{1,0:T(8,128)(2,1)S(1)}, bf16[64,2048]{1,0:T(8,128)(2,1)S(1)}, u32[]{:S(2)}, u32[]{:S(2)}) collective-permute-start(bf16[64,2048]{1,0:T(8,128)(2,1)S(1)} %collective-permute-done.5.refs_2_), channel_id=1, source_target_pairs={{0,1},{1,0},{2,3},{3,2},{4,5},{5,4},{6,7},{7,6},{8,9},{9,8},{10,11... | collective-permute-start | bytes 786440 | tf_op jit(solution)/shard_map/ppermute | solution.py:341
  65.9 8.8 %collective-permute-start.7 = (bf16[16,2048]{1,0:T(8,128)(2,1)S(1)}, bf16[16,2048]{1,0:T(8,128)(2,1)S(1)}, u32[]{:S(2)}, u32[]{:S(2)}) collective-permute-start(bf16[16,2048]{1,0:T(8,128)(2,1)S(1)} %get-tuple-element.33), channel_id=1, source_target_pairs={{0,4},{4,8},{8,12},{12,16},{16,20},{20,24},{24,28},{28,32},{32,36}... | collective-permute-start | bytes 196616 | tf_op jit(solution)/shard_map/ppermute | solution.py:364
  69.3 2.8 %copy-start.1 = (bf16[2,16,6,128,128]{4,3,2,1,0:T(8,128)(2,1)S(1)}, bf16[2,16,6,128,128]{4,3,2,1,0:T(8,128)(2,1)}, u32[]{:S(2)}) copy-start(bf16[2,16,6,128,128]{4,3,2,1,0:T(8,128)(2,1)} %refs_4_.6) | copy-start | bytes 18874372
